TPU v7x, 32 devices: a whole 2x2x4 slice. The times are simulated.
32 devices in a mesh: dp: 2 (over x), ctx: 4 (over z), space: 4 (over y, core).
Axes of the slice: x: 2, y: 2, z: 4, core: 2. Of those that a mesh axis runs over, the one named last changes fastest.
Arguments:
- inputs: bfloat16 [8, 4, 256, 3072], P('dp', 'ctx', 'space'), may hold values from -64 to 64
- upstream: bfloat16 [8, 4, 256, 3072], P('dp', 'ctx', 'space'), may hold values from -6 to 6
- qkv_weight: bfloat16 [3, 3072, 1536], P(None, None, 'space'), may hold values from -0.109375 to 0.109375
- out_weight: bfloat16 [3072, 1536], P(None, 'space'), may hold values from -0.15625 to 0.15625
Outputs:
- input_grad: bfloat16 [8, 4, 256, 3072], P('dp', 'ctx', 'space')
- qkv_grad: float32 [3, 3072, 1536], P(None, ('dp', 'ctx'), 'space')
- proj_grad: float32 [3072, 1536], P(('dp', 'ctx'), 'space')
All inputs are finite; a program needn't handle non-finite values.
Results may differ from a plain program's by a relative error of at most 0.01.
The roundings to bfloat16 on the way count: a program that leaves them out, or rounds other values in their place, can miss the bound.
Values may be sent and summed in bfloat16 or wider, within the bound.
No kernel may reach another device: no remote copies, remote signals or barrier semaphores. Data moves between devices by JAX's collectives and lax.ppermute only.
A program may use at most 192 MiB of HBM per device.

v0:
```python
import math

import jax
import jax.numpy as jnp
from jax import lax
from jax.sharding import PartitionSpec as P

HS = 128


def attend_block(queries, key_rows, value_rows, out_front):
    clips, frames, patches, width = queries.shape
    heads_local = width // HS
    scale = 1.0 / math.sqrt(HS)
    f32 = jnp.float32

    def heads_view(array):
        return array.reshape(clips, frames, patches, heads_local, HS)

    query_h = heads_view(queries)
    key_h = heads_view(key_rows)
    value_h = heads_view(value_rows)
    front_h = heads_view(out_front)
    scores = jnp.einsum("cfphd,cgphd->cphfg", query_h, key_h, preferred_element_type=f32) * scale
    causal = jnp.arange(frames)[:, None] >= jnp.arange(frames)[None, :]
    masked = jnp.where(causal, scores, f32(-1e30))
    top = jnp.max(masked, axis=-1, keepdims=True)
    expo = jnp.where(causal, jnp.exp(masked - top), f32(0.0))
    probs = expo / jnp.sum(expo, axis=-1, keepdims=True)
    probs_b = probs.astype(jnp.bfloat16)
    attended = jnp.einsum(
        "cphfg,cgphd->cfphd", probs_b, value_h, preferred_element_type=f32
    ).astype(jnp.bfloat16)
    dprobs = jnp.einsum("cfphd,cgphd->cphfg", front_h, value_h, preferred_element_type=f32)
    dvalue = jnp.einsum("cphfg,cfphd->cgphd", probs_b, front_h, preferred_element_type=f32).astype(
        jnp.bfloat16
    )
    dscore = probs * (dprobs - jnp.sum(probs * dprobs, axis=-1, keepdims=True))
    dscore_b = dscore.astype(jnp.bfloat16)
    dquery = (
        jnp.einsum("cphfg,cgphd->cfphd", dscore_b, key_h, preferred_element_type=f32) * scale
    ).astype(jnp.bfloat16)
    dkey = (
        jnp.einsum("cphfg,cfphd->cgphd", dscore_b, query_h, preferred_element_type=f32) * scale
    ).astype(jnp.bfloat16)
    shape = (clips, frames, patches, width)
    return (
        attended.reshape(shape),
        dquery.reshape(shape),
        dkey.reshape(shape),
        dvalue.reshape(shape),
    )


def body(inputs, upstream, qkv_weight, out_weight):
    gathered, cotangent = (
        lax.all_gather(inputs, "space", axis=2, tiled=True),
        lax.all_gather(upstream, "space", axis=2, tiled=True),
    )
    clips, single, patches, model = gathered.shape
    width = qkv_weight.shape[2]
    rows = gathered.reshape(clips * patches, model)
    up_rows = cotangent.reshape(clips * patches, model)

    def project(source, matrix):
        product = jnp.dot(source, matrix, preferred_element_type=jnp.float32)
        return product.astype(jnp.bfloat16).reshape(clips, 1, patches, width)

    queries = project(rows, qkv_weight[0])
    key_rows = project(rows, qkv_weight[1])
    value_rows = project(rows, qkv_weight[2])
    out_front = project(up_rows, out_weight)
    queries, key_rows, value_rows, out_front = (
        lax.all_to_all(queries, "ctx", split_axis=2, concat_axis=1, tiled=True),
        lax.all_to_all(key_rows, "ctx", split_axis=2, concat_axis=1, tiled=True),
        lax.all_to_all(value_rows, "ctx", split_axis=2, concat_axis=1, tiled=True),
        lax.all_to_all(out_front, "ctx", split_axis=2, concat_axis=1, tiled=True),
    )
    results = attend_block(queries, key_rows, value_rows, out_front)
    attended, dquery, dkey, dvalue = (
        lax.all_to_all(results[0], "ctx", split_axis=1, concat_axis=2, tiled=True),
        lax.all_to_all(results[1], "ctx", split_axis=1, concat_axis=2, tiled=True),
        lax.all_to_all(results[2], "ctx", split_axis=1, concat_axis=2, tiled=True),
        lax.all_to_all(results[3], "ctx", split_axis=1, concat_axis=2, tiled=True),
    )

    def flatten(array):
        return array.reshape(clips * patches, width)

    grads = [flatten(dquery), flatten(dkey), flatten(dvalue)]
    partial_value = jnp.dot(grads[0], qkv_weight[0].T, preferred_element_type=jnp.float32)
    partial_value = partial_value + jnp.dot(
        grads[1], qkv_weight[1].T, preferred_element_type=jnp.float32
    )
    partial_value = partial_value + jnp.dot(
        grads[2], qkv_weight[2].T, preferred_element_type=jnp.float32
    )
    summed = lax.psum_scatter(
        partial_value.reshape(clips, 1, patches, model).astype(jnp.bfloat16),
        "space",
        scatter_dimension=2,
        tiled=True,
    )
    qkv_part = jnp.stack(
        [jnp.dot(rows.T, grads[s], preferred_element_type=jnp.float32) for s in range(3)]
    )
    proj_part = jnp.dot(up_rows.T, flatten(attended), preferred_element_type=jnp.float32)
    qkv_grad, proj_grad = (
        lax.psum_scatter(qkv_part, ("dp", "ctx"), scatter_dimension=1, tiled=True),
        lax.psum_scatter(proj_part, ("dp", "ctx"), scatter_dimension=0, tiled=True),
    )
    return (summed, qkv_grad, proj_grad)


def solution(mesh):
    placed = (
        P("dp", "ctx", "space", None),
        P("dp", "ctx", "space", None),
        P(None, None, "space"),
        P(None, "space"),
    )
    return jax.shard_map(
        body,
        mesh=mesh,
        in_specs=placed,
        out_specs=(
            P("dp", "ctx", "space", None),
            P(None, ("dp", "ctx"), "space"),
            P(("dp", "ctx"), "space"),
        ),
        check_vma=False,
    )
```

profile of v0, /device:TPU:0, one launch (start us, length us, event | category | flops | bytes accessed | tf_op | source)
XLA Modules:
  0.0 654.9 jit_solution(17708837716123347475)
XLA Ops:
  8.7 50.0 %all-gather.3.cloned.1.call-done = bf16[4,1,256,3072]{3,2,1,0:T(8,128)(2,1)} async-done(((bf16[4,1,64,3072]{3,2,1,0:T(8,128)(2,1)}), bf16[4,1,256,3072]{3,2,1,0:T(8,128)(2,1)}) %all-gather.3.cloned.1.call-update) | async-done | bytes 6291472 | tf_op jit(solution)/shard_map/all_gather | solution.py:57
  58.7 6.9 %fusion.25 = bf16[1024,384]{1,0:T(8,128)(2,1)S(1)} fusion(bf16[1024,3072]{1,0:T(8,128)(2,1)} %bitcast.90, bf16[3,3072,384]{2,1,0:T(8,128)(2,1)} %param.6), kind=kOutput, calls=%fused_computation.33 | convolution fusion | flops 2416312320 | bytes 9437184 | tf_op jit(solution)/shard_map/dot_general | solution.py:66
  67.1 4.6 all-to-all-start.3
  71.7 6.9 %fusion.22 = bf16[1024,384]{1,0:T(8,128)(2,1)S(1)} fusion(bf16[1024,3072]{1,0:T(8,128)(2,1)} %bitcast.91, bf16[3,3072,384]{2,1,0:T(8,128)(2,1)} %param.6), kind=kOutput, calls=%fused_computation.32 | convolution fusion | flops 2416312320 | bytes 9437184 | tf_op jit(solution)/shard_map/dot_general | solution.py:66
  80.1 12.1 %all-to-all-done.3 = bf16[4,1,256,384]{3,0,1,2:T(4,128)(2,1)S(1)} async-done(((bf16[4,1,256,384]{3,0,1,2:T(4,128)(2,1)}), bf16[4,1,256,384]{3,0,1,2:T(4,128)(2,1)S(1)}, u32[]{:S(2)}, u32[]{:S(2)}) %all-to-all-start.3) | async-done | bytes 786464 | tf_op jit(solution)/shard_map/all_to_all | solution.py:76
  96.4 7.0 %fusion.19 = bf16[1024,384]{1,0:T(8,128)(2,1)S(1)} fusion(bf16[1024,3072]{1,0:T(8,128)(2,1)} %bitcast.92, bf16[3,3072,384]{2,1,0:T(8,128)(2,1)} %param.6), kind=kOutput, calls=%fused_computation.31 | convolution fusion | flops 2416312320 | bytes 9437184 | tf_op jit(solution)/shard_map/dot_general | solution.py:66
  104.9 11.3 %all-to-all-done.1 = bf16[4,1,256,384]{3,0,1,2:T(4,128)(2,1)} async-done(((bf16[4,1,256,384]{3,0,1,2:T(4,128)(2,1)}), bf16[4,1,256,384]{3,0,1,2:T(4,128)(2,1)}, u32[]{:S(2)}, u32[]{:S(2)}) %all-to-all-start.1) | async-done | bytes 786464 | tf_op jit(solution)/shard_map/all_to_all | solution.py:74
  124.3 15.8 %all-to-all-done = bf16[4,1,256,384]{3,0,1,2:T(4,128)(2,1)} async-done(((bf16[4,1,256,384]{3,0,1,2:T(4,128)(2,1)}), bf16[4,1,256,384]{3,0,1,2:T(4,128)(2,1)}, u32[]{:S(2)}, u32[]{:S(2)}) %all-to-all-start) | async-done | bytes 786464 | tf_op jit(solution)/shard_map/all_to_all | solution.py:75
  143.3 6.4 fusion.43
  154.8 23.1 %all_to_all.32 = bf16[4,4,64,384]{3,2,0,1:T(8,128)(2,1)S(1)} all-to-all(bf16[4,4,64,384]{3,2,0,1:T(8,128)(2,1)} %reshape.130), channel_id=1, replica_groups=mesh['dp'=2,'ctx'=4,'space'=4] {'ctx'}, dimensions={1} | all-to-all | bytes 1572864 | tf_op jit(solution)/shard_map/all_to_all | solution.py:81
  178.0 7.5 %convolution_bitcast_fusion = f32[3072,384]{0,1:T(8,128)} fusion(bf16[1024,384]{1,0:T(8,128)(2,1)S(1)} %bitcast.107, bf16[1024,3072]{1,0:T(8,128)(2,1)} %bitcast.99), kind=kOutput, calls=%fused_computation.3 | convolution fusion | flops 2415919104 | bytes 11796480 | tf_op jit(solution)/shard_map/dot_general | solution.py:107
  185.6 5.6 convolution_convert_fusion.2
  191.8 42.4 %all_to_all.33 = bf16[4,1,256,384]{3,0,1,2:T(4,128)(2,1)S(1)} all-to-all(bf16[4,1,256,384]{3,0,1,2:T(4,128)(2,1)S(1)} %copy.64), channel_id=1, replica_groups=mesh['dp'=2,'ctx'=4,'space'=4] {'ctx'}, dimensions={2} | all-to-all | bytes 1572864 | tf_op jit(solution)/shard_map/all_to_all | solution.py:77
  252.6 13.0 %all-to-all-done.6 = bf16[4,4,64,384]{3,2,0,1:T(8,128)(2,1)S(1)} async-done(((bf16[4,4,64,384]{3,2,0,1:T(8,128)(2,1)}), bf16[4,4,64,384]{3,2,0,1:T(8,128)(2,1)S(1)}, u32[]{:S(2)}, u32[]{:S(2)}) %all-to-all-start.6) | async-done | bytes 786464 | tf_op jit(solution)/shard_map/all_to_all | solution.py:84
  273.7 27.6 %all-to-all-done.4 = bf16[4,4,64,384]{3,2,0,1:T(8,128)(2,1)S(1)} async-done(((bf16[4,4,64,384]{3,2,0,1:T(8,128)(2,1)}), bf16[4,4,64,384]{3,2,0,1:T(8,128)(2,1)S(1)}, u32[]{:S(2)}, u32[]{:S(2)}) %all-to-all-start.4) | async-done | bytes 786464 | tf_op jit(solution)/shard_map/all_to_all | solution.py:82
  306.0 19.4 %all-to-all-done.5 = bf16[4,4,64,384]{3,2,0,1:T(8,128)(2,1)} async-done(((bf16[4,4,64,384]{3,2,0,1:T(8,128)(2,1)}), bf16[4,4,64,384]{3,2,0,1:T(8,128)(2,1)}, u32[]{:S(2)}, u32[]{:S(2)}) %all-to-all-start.5) | async-done | bytes 786464 | tf_op jit(solution)/shard_map/all_to_all | solution.py:83
  326.6 7.7 %convolution_bitcast_fusion.2 = f32[1,3072,384]{1,2,0:T(8,128)} fusion(bf16[1024,384]{1,0:T(8,128)(2,1)S(1)} %bitcast.105, bf16[1024,3072]{1,0:T(8,128)(2,1)} %bitcast.93), kind=kOutput, calls=%fused_computation.5 | convolution fusion | flops 2415919104 | bytes 11796480 | tf_op jit(solution)/shard_map/dot_general | solution.py:105
  334.3 7.8 %convolution_bitcast_fusion.3 = f32[1,3072,384]{1,2,0:T(8,128)} fusion(bf16[1024,384]{1,0:T(8,128)(2,1)S(1)} %bitcast.103, bf16[1024,3072]{1,0:T(8,128)(2,1)} %bitcast.94), kind=kOutput, calls=%fused_computation.6 | convolution fusion | flops 2415919104 | bytes 11796480 | tf_op jit(solution)/shard_map/dot_general | solution.py:105
  346.5 12.2 %pad_maximum_fusion = f32[3,3072,384]{1,2,0:T(8,128)} fusion(f32[1,3072,384]{1,2,0:T(8,128)} %convolution_bitcast_fusion.1, f32[1,3072,384]{1,2,0:T(8,128)} %convolution_bitcast_fusion.2, f32[1,3072,384]{1,2,0:T(8,128)} %convolution_bitcast_fusion.3), kind=kLoop, calls=%fused_computation.1 | loop fusion | flops 7077888 | bytes 28311552 | tf_op jit(solution)/shard_map/stack | solution.py:104
  358.8 8.7 %fusion.4 = f32[1024,3072]{1,0:T(8,128)} fusion(bf16[1024,384]{1,0:T(8,128)(2,1)S(1)} %bitcast.104, bf16[3,3072,384]{2,1,0:T(8,128)(2,1)} %param.6), kind=kOutput, calls=%fused_computation.10 | convolution fusion | flops 2415919104 | bytes 15728640 | tf_op jit(solution)/shard_map/dot_general | solution.py:91
  367.6 8.1 %fusion.8 = f32[1024,3072]{1,0:T(8,128)} fusion(bf16[1024,384]{1,0:T(8,128)(2,1)S(1)} %bitcast.106, bf16[3,3072,384]{2,1,0:T(8,128)(2,1)} %param.6), kind=kOutput, calls=%fused_computation.14 | convolution fusion | flops 2415919104 | bytes 15728640 | tf_op jit(solution)/shard_map/dot_general | solution.py:92
  375.7 13.5 %add_convert_fusion = bf16[1024,3072]{1,0:T(8,128)(2,1)} fusion(f32[1024,3072]{1,0:T(8,128)} %fusion.4, f32[1024,3072]{1,0:T(8,128)} %fusion.8, bf16[1024,384]{1,0:T(8,128)(2,1)S(1)} %bitcast.102, bf16[3,3072,384]{2,1,0:T(8,128)(2,1)} %param.6), kind=kOutput, calls=%fused_computation.2 | convolution fusion | flops 2425356288 | bytes 34603008 | tf_op jit(solution)/shard_map/dot_general | solution.py:95
  391.6 195.9 %reduce-scatter.6.cloned.1.call-done = f32[3,384,384]{1,2,0:T(8,128)} async-done(((f32[3,3072,384]{1,2,0:T(8,128)}), f32[3,384,384]{1,2,0:T(8,128)}) %reduce-scatter.6.cloned.1.call-update) | async-done | bytes 1769488 | tf_op jit(solution)/shard_map/reduce_scatter | solution.py:109
  590.3 57.6 %reduce-scatter.4.cloned.1.call-done = bf16[4,1,64,3072]{3,2,1,0:T(8,128)(2,1)} async-done(((bf16[4,1,256,3072]{3,2,1,0:T(8,128)(2,1)}), bf16[4,1,64,3072]{3,2,1,0:T(8,128)(2,1)}) %reduce-scatter.4.cloned.1.call-update) | async-done | bytes 1572880 | tf_op jit(solution)/shard_map/reduce_scatter | solution.py:98
  (70 shorter events, 69.2 us)
Async XLA Ops:
  7.2 178.4 %copy-start = (bf16[3072,384]{1,0:T(8,128)(2,1)S(1)}, bf16[3072,384]{1,0:T(8,128)(2,1)}, u32[]{:S(2)}) copy-start(bf16[3072,384]{1,0:T(8,128)(2,1)} %param.7) | copy-start | bytes 7077892
  7.2 51.5 %all-gather.3.cloned.1.call-start = ((), (), s32[]{:S(2)}) async-start(), calls=%async_computation.11 | async-start | bytes 7864320 | tf_op jit(solution)/shard_map/all_gather | solution.py:57
  7.9 170.1 %all-gather.5.cloned.1.call-start = ((), (), s32[]{:S(2)}) async-start(), calls=%async_computation.12 | async-start | bytes 7864320 | tf_op jit(solution)/shard_map/all_gather | solution.py:58
  67.1 25.1 %all-to-all-start.3 = ((bf16[4,1,256,384]{3,0,1,2:T(4,128)(2,1)}), bf16[4,1,256,384]{3,0,1,2:T(4,128)(2,1)S(1)}, u32[]{:S(2)}, u32[]{:S(2)}) async-start(bf16[4,1,256,384]{3,0,1,2:T(4,128)(2,1)} %copy.66), calls=%async_computation.3 | async-start | bytes 1572864 | tf_op jit(solution)/shard_map/all_to_all | solution.py:76
  92.2 24.0 %all-to-all-start.1 = ((bf16[4,1,256,384]{3,0,1,2:T(4,128)(2,1)}), bf16[4,1,256,384]{3,0,1,2:T(4,128)(2,1)}, u32[]{:S(2)}, u32[]{:S(2)}) async-start(bf16[4,1,256,384]{3,0,1,2:T(4,128)(2,1)} %copy.60), calls=%async_computation.1 | async-start | bytes 1572864 | tf_op jit(solution)/shard_map/all_to_all | solution.py:74
  116.2 23.9 %all-to-all-start = ((bf16[4,1,256,384]{3,0,1,2:T(4,128)(2,1)}), bf16[4,1,256,384]{3,0,1,2:T(4,128)(2,1)}, u32[]{:S(2)}, u32[]{:S(2)}) async-start(bf16[4,1,256,384]{3,0,1,2:T(4,128)(2,1)} %copy.58), calls=%async_computation | async-start | bytes 1572864 | tf_op jit(solution)/shard_map/all_to_all | solution.py:75
  120.4 268.9 %reduce-scatter.8.cloned.1.call-start = ((), (), s32[]{:S(2)}) async-start(), calls=%async_computation.15 | async-start | bytes 5308416 | tf_op jit(solution)/shard_map/reduce_scatter | solution.py:110
  124.3 25.5 %copy-start.3 = (bf16[4,4,64,3,128]{4,3,0,2,1:T(4,128)(2,1)}, bf16[4,4,64,3,128]{4,3,0,2,1:T(4,128)(2,1)S(1)}, u32[]{:S(2)}) copy-start(bf16[4,4,64,3,128]{4,3,0,2,1:T(4,128)(2,1)S(1)} %reshape.132) | copy-start | bytes 2359300
  191.2 44.4 %copy-start.8 = (f32[4,64,3,4]{3,2,1,0:T(4,128)S(1)}, f32[4,64,3,4]{3,2,1,0:T(4,128)}, u32[]{:S(2)}) copy-start(f32[4,64,3,4]{3,2,1,0:T(4,128)} %get-tuple-element.15) | copy-start | bytes 36868
  234.6 1.0 copy-start.6
  238.2 5.5 copy-start.4
  240.2 25.4 %all-to-all-start.6 = ((bf16[4,4,64,384]{3,2,0,1:T(8,128)(2,1)}), bf16[4,4,64,384]{3,2,0,1:T(8,128)(2,1)S(1)}, u32[]{:S(2)}, u32[]{:S(2)}) async-start(bf16[4,4,64,384]{3,2,0,1:T(8,128)(2,1)} %reshape.129), calls=%async_computation.6 | async-start | bytes 1572864 | tf_op jit(solution)/shard_map/all_to_all | solution.py:84
  243.8 4.3 copy-start.2
  248.1 1.2 copy-start.5
  249.3 1.3 copy-start.7
  265.6 35.7 %all-to-all-start.4 = ((bf16[4,4,64,384]{3,2,0,1:T(8,128)(2,1)}), bf16[4,4,64,384]{3,2,0,1:T(8,128)(2,1)S(1)}, u32[]{:S(2)}, u32[]{:S(2)}) async-start(bf16[4,4,64,384]{3,2,0,1:T(8,128)(2,1)} %reshape.127), calls=%async_computation.4 | async-start | bytes 1572864 | tf_op jit(solution)/shard_map/all_to_all | solution.py:82
  301.3 24.1 %all-to-all-start.5 = ((bf16[4,4,64,384]{3,2,0,1:T(8,128)(2,1)}), bf16[4,4,64,384]{3,2,0,1:T(8,128)(2,1)}, u32[]{:S(2)}, u32[]{:S(2)}) async-start(bf16[4,4,64,384]{3,2,0,1:T(8,128)(2,1)} %reshape.128), calls=%async_computation.5 | async-start | bytes 1572864 | tf_op jit(solution)/shard_map/all_to_all | solution.py:83
  305.5 281.9 %reduce-scatter.6.cloned.1.call-start = ((), (), s32[]{:S(2)}) async-start(), calls=%async_computation.14 | async-start | bytes 15925248 | tf_op jit(solution)/shard_map/reduce_scatter | solution.py:109
  326.6 15.5 %slice-start = ((s8[6291456]{0:T(1024)(128)(4,1)}), s8[4194304]{0:T(1024)(128)(4,1)S(1)}, s32[]{:S(2)}) async-start(s8[6291456]{0:T(1024)(128)(4,1)} %bitcast.95), calls=%async_computation.16 | async-start | bytes 8388608
  334.3 7.8 %slice-start.1 = ((s8[6291456]{0:T(1024)(128)(4,1)}), s8[2097152]{0:T(1024)(128)(4,1)S(1)}, s32[]{:S(2)}) async-start(s8[6291456]{0:T(1024)(128)(4,1)} %bitcast.95), calls=%async_computation.17 | async-start | bytes 4194304
  358.8 289.2 %reduce-scatter.4.cloned.1.call-start = ((), (), s32[]{:S(2)}) async-start(), calls=%async_computation.13 | async-start | bytes 7864320 | tf_op jit(solution)/shard_map/reduce_scatter | solution.py:98
  389.2 258.7 %copy-start.1 = (bf16[3072,384]{1,0:T(8,128)(2,1)S(1)}, bf16[3072,384]{1,0:T(8,128)(2,1)}, u32[]{:S(2)}) copy-start(bf16[3072,384]{1,0:T(8,128)(2,1)} %param.7) | copy-start | bytes 7077892
Sparse Core Ops, SparseCore 0:
  9.6 49.0 all-gather.2
  60.3 46.3 all-gather.4
  185.7 132.1 reduce-scatter.7
  358.9 228.5 reduce-scatter.5
  590.4 57.4 reduce-scatter.3
where the time goes:
time: 662 us; the launch traced here: 655 us
  waiting for transfers between devices  404 us (61%)
  matrix products  105 us (16%)
  blocking collectives  65.5 us (10%)
  local copies, waits for them, and re-layouts  28.3 us (4%)
  starting transfers between devices  24.8 us (4%)
  between operations  14.5 us (2%)
  other arithmetic  12.9 us (2%)
    reduce_scatter x1, waiting for transfers between devices, body(): lax.psum_scatter(qkv_part, ('dp', 'ctx'), scatter_dimension=1, tiled=True)  196 us
    reduce_scatter x1, waiting for transfers between devices, body(): lax.psum_scatter(partial_value.reshape(clips, 1, patches, model).astype(j...  57.6 us
    all_gather x1, waiting for transfers between devices, body(): lax.all_gather(inputs, 'space', axis=2, tiled=True)  50 us
    all_to_all x1, blocking collectives, body(): lax.all_to_all(out_front, 'ctx', split_axis=2, concat_axis=1, tiled=True)  42.4 us
    all_to_all x1, waiting for transfers between devices, body(): lax.all_to_all(results[1], 'ctx', split_axis=1, concat_axis=2, tiled=True)  27.6 us
    dot_general x4, matrix products, project(): product = jnp.dot(source, matrix, preferred_element_type=jnp.float32)  26.3 us
    all_to_all x1, blocking collectives, body(): lax.all_to_all(results[0], 'ctx', split_axis=1, concat_axis=2, tiled=True)  23.1 us
    dot_general x3, matrix products, body(): jnp.dot(rows.T, grads[s], preferred_element_type=jnp.float32)  19.9 us
  transfers between devices with their start and end apart: 11, of which 9 were waited for; matrix products, arithmetic and copies ran while one was open for 21% of the time, Pallas kernels for 0%

commit v1 on v0

v1 whole, which is shorter than its diff:
```python
import functools
import math

import jax
import jax.numpy as jnp
from jax import lax
from jax.experimental import pallas as pl
from jax.experimental.pallas import tpu as pltpu
from jax.sharding import PartitionSpec as P

HS = 128
F32 = jnp.float32
BF16 = jnp.bfloat16


def attention_kernel(frames, heads, me_ref, q_ref, k_ref, v_ref, o_ref, att_ref, dq_ref, dk_ref, dv_ref):
    me = me_ref[0]
    scale = 1.0 / math.sqrt(HS)
    slots = [lax.rem(me - f + frames, frames) for f in range(frames)]

    for h in range(heads):
        cols = pl.ds(h * HS, HS)

        def load(ref):
            return [ref[0, slots[f], :, cols].astype(F32) for f in range(frames)]

        q, k, v, o = load(q_ref), load(k_ref), load(v_ref), load(o_ref)
        dk = [None] * frames
        dv = [None] * frames
        for f in range(frames):
            scores = [jnp.sum(q[f] * k[g], axis=-1, keepdims=True) * scale for g in range(f + 1)]
            top = functools.reduce(jnp.maximum, scores)
            expo = [jnp.exp(s - top) for s in scores]
            total = functools.reduce(jnp.add, expo)
            probs = [e / total for e in expo]
            probs_b = [p.astype(BF16).astype(F32) for p in probs]
            dprobs = [jnp.sum(o[f] * v[g], axis=-1, keepdims=True) for g in range(f + 1)]
            inner = functools.reduce(jnp.add, [p * d for p, d in zip(probs, dprobs)])
            dscores = [
                (p * (d - inner)).astype(BF16).astype(F32) for p, d in zip(probs, dprobs)
            ]
            att = functools.reduce(jnp.add, [probs_b[g] * v[g] for g in range(f + 1)])
            dq = functools.reduce(jnp.add, [dscores[g] * k[g] for g in range(f + 1)])
            att_ref[0, slots[f], :, cols] = att.astype(BF16)
            dq_ref[0, slots[f], :, cols] = (dq * scale).astype(BF16)
            for g in range(f + 1):
                add_k, add_v = dscores[g] * q[f], probs_b[g] * o[f]
                dk[g] = add_k if dk[g] is None else dk[g] + add_k
                dv[g] = add_v if dv[g] is None else dv[g] + add_v
        for g in range(frames):
            dk_ref[0, slots[g], :, cols] = (dk[g] * scale).astype(BF16)
            dv_ref[0, slots[g], :, cols] = dv[g].astype(BF16)


def attend(me, q, k, v, o):
    groups, frames, patches, width = q.shape
    block = pl.BlockSpec((1, frames, patches, width), lambda i, me_ref: (i, 0, 0, 0))
    return pl.pallas_call(
        functools.partial(attention_kernel, frames, width // HS),
        grid_spec=pltpu.PrefetchScalarGridSpec(
            num_scalar_prefetch=1,
            grid=(groups,),
            in_specs=[block] * 4,
            out_specs=[block] * 4,
        ),
        out_shape=[jax.ShapeDtypeStruct(q.shape, BF16)] * 4,
        compiler_params=pltpu.CompilerParams(vmem_limit_bytes=32 * 1024 * 1024),
        cost_estimate=pl.CostEstimate(
            flops=q.size * 80, bytes_accessed=q.size * 16, transcendentals=q.size * 4
        ),
    )(me.reshape(1), q, k, v, o)


def dot(a, b, contract):
    return lax.dot_general(a, b, ((contract[:1], contract[1:]), ((), ())), preferred_element_type=F32)


def body(sizes, inputs, upstream, qkv_weight, out_weight):
    n_dp, n, n_space = sizes
    me = lax.axis_index("ctx")
    me_dp = lax.axis_index("dp")
    clips, single, patches, model = inputs.shape
    width = qkv_weight.shape[2]
    rows = clips * single * patches // n
    parts = 2
    half = rows // parts
    bits = []
    bit = n_space // 2
    while bit:
        bits.append(bit)
        bit //= 2

    def shift(x, d):
        return lax.ppermute(x, "ctx", [(i, (i + d) % n) for i in range(n)])

    def flip(x, bit):
        return lax.ppermute(x, "space", [(i, i ^ bit) for i in range(n_space)])

    def spread(x, c):
        x = x.reshape(n, rows, model)[:, c * half : (c + 1) * half]

        def to(d):
            return lax.dynamic_index_in_dim(x, lax.rem(me + d, n), 0, keepdims=False)

        own = jnp.stack([to(0)] + [shift(to(d), d) for d in range(1, n)])
        held = [own]
        for bit in bits:
            held = held + [flip(h, bit) for h in held]
        return jnp.stack(held).reshape(-1, model)

    def project(tokens, weight):
        return dot(tokens, weight, (1, 0)).astype(BF16).reshape(n_space, n, half, width)

    tokens = [spread(inputs, c) for c in range(parts)]
    ups = [spread(upstream, c) for c in range(parts)]
    results = []
    for c in range(parts):
        q, k, v = (project(tokens[c], qkv_weight[s]) for s in range(3))
        o = project(ups[c], out_weight)
        results.append(attend(me, q, k, v, o))

    pieces = []
    for c in range(parts):
        _, dq, dk, dv = (r.reshape(-1, width) for r in results[c])
        part = dot(dq, qkv_weight[0], (1, 1)) + dot(dk, qkv_weight[1], (1, 1))
        part = (part + dot(dv, qkv_weight[2], (1, 1))).astype(BF16)
        part = part.reshape(n_space, n, half, model)
        for bit in reversed(bits):
            size = part.shape[0] // 2
            got = flip(part[size:], bit)
            part = (part[:size].astype(F32) + got.astype(F32)).astype(BF16)
        part = part[0]
        back = [part[0]] + [shift(part[d], n - d) for d in range(1, n)]
        back = jnp.stack([back[d] for d in range(n)])
        order = lax.rem(jnp.arange(n) - me + n, n)
        pieces.append(jnp.take(back, order, axis=0))
    input_grad = jnp.stack(pieces, axis=1).reshape(inputs.shape)

    token_all = jnp.concatenate(tokens, 0)
    up_all = jnp.concatenate(ups, 0)

    def reduce_rows(left, right):
        share = model // n_dp
        other = lax.dynamic_slice_in_dim(left, (1 - me_dp) * share, share, 1)
        mine = lax.dynamic_slice_in_dim(left, me_dp * share, share, 1)
        sent = lax.ppermute(dot(other, right, (0, 0)).astype(BF16), "dp", [(0, 1), (1, 0)])
        acc = dot(mine, right, (0, 0)) + sent.astype(F32)
        acc = acc.reshape(n, share // n, width)
        for step in range(n - 1):
            count = n - 1 - step
            start = jnp.where(me == step, step + 1, 0)
            give = lax.dynamic_slice_in_dim(acc, start, count, 0).astype(BF16)
            got = lax.ppermute(give, "ctx", [(step, step + 1), (n - 1 - step, n - 2 - step)])
            at = jnp.where(me == step + 1, step + 1, 0)
            old = lax.dynamic_slice_in_dim(acc, at, count, 0)
            acc = lax.dynamic_update_slice_in_dim(acc, old + got.astype(F32), at, 0)
        return lax.dynamic_index_in_dim(acc, me, 0, keepdims=False)

    cat = [jnp.concatenate([results[c][i].reshape(-1, width) for c in range(parts)], 0) for i in range(4)]
    proj_grad = reduce_rows(up_all, cat[0])
    qkv_grad = jnp.stack([reduce_rows(token_all, cat[1 + s]) for s in range(3)])
    return (input_grad, qkv_grad, proj_grad)


def solution(mesh):
    placed = (
        P("dp", "ctx", "space", None),
        P("dp", "ctx", "space", None),
        P(None, None, "space"),
        P(None, "space"),
    )
    sizes = tuple(mesh.shape[a] for a in ("dp", "ctx", "space"))
    return jax.shard_map(
        functools.partial(body, sizes),
        mesh=mesh,
        in_specs=placed,
        out_specs=(
            P("dp", "ctx", "space", None),
            P(None, ("dp", "ctx"), "space"),
            P(("dp", "ctx"), "space"),
        ),
        check_vma=False,
    )
```

time: 662 us -> 374 us (0.56)
  waiting for transfers between devices: 404 us -> 170 us
  starting transfers between devices: 24.8 us -> 101 us
  blocking collectives: 65.5 us -> 0 us
  matrix products: 105 us -> 59.6 us
  between operations: 14.5 us -> 1.84 us
  local copies, waits for them, and re-layouts: 28.3 us -> 17.3 us
    reduce_scatter x3 -> x0, waiting for transfers between devices: 254 us -> none  [the longest x1 196 us: body(): lax.psum_scatter(qkv_part, ('dp', 'ctx'), scatter_dimension=1, tiled=True)]
    ppermute x0 -> x50, waiting for transfers between devices: none -> 170 us  [the longest x4 65.7 us: reduce_rows(): lax.ppermute(dot(other, right, (0, 0)).astype(BF16), 'dp', [(0, 1), (1, 0)])]
    ppermute x0 -> x50, starting transfers between devices: none -> 101 us  [the longest x18 59.5 us: shift(): return lax.ppermute(x, 'ctx', [(i, (i + d) % n) for i in range(n)])]
    all_to_all x6 -> x0, waiting for transfers between devices: 99.2 us -> none  [the longest x1 27.6 us: body(): lax.all_to_all(results[1], 'ctx', split_axis=1, concat_axis=2, tiled=True)]
    all_to_all x2 -> x0, blocking collectives: 65.5 us -> none  [the longest x1 42.4 us: body(): lax.all_to_all(out_front, 'ctx', split_axis=2, concat_axis=1, tiled=True)]
    all_gather x2 -> x0, waiting for transfers between devices: 50.1 us -> none  [the longest x1 50 us: body(): lax.all_gather(inputs, 'space', axis=2, tiled=True)]
    dot_general x16 -> x22, matrix products: 98.2 us -> 59.6 us  [dot(): lax.dot_general(a, b, ((contract[:1], contract[1:]), ((), ())), preferred...]
    all_to_all x6 -> x0, starting transfers between devices: 24.2 us -> none  [the longest x1 4.6 us: body(): lax.all_to_all(value_rows, 'ctx', split_axis=2, concat_axis=1, tiled=True)]
  transfers between devices with their start and end apart: 11 -> 50, of which waited for: 9 -> 20; matrix products, arithmetic and copies ran while one was open for 21% -> 17% of each run, Pallas kernels for 0% -> 0%
where the time goes in v1:
time: 374 us; the launch traced here: 371 us
  waiting for transfers between devices  170 us (45%)
  starting transfers between devices  101 us (27%)
  matrix products  59.6 us (16%)
  other arithmetic  17.7 us (5%)
  local copies, waits for them, and re-layouts  17.3 us (5%)
  Pallas kernels  4.66 us (1%)
    ppermute x4, waiting for transfers between devices, reduce_rows(): lax.ppermute(dot(other, right, (0, 0)).astype(BF16), 'dp', [(0, 1), (1, 0)])  65.7 us
    dot_general x22, matrix products, dot(): lax.dot_general(a, b, ((contract[:1], contract[1:]), ((), ())), preferred...  59.6 us
    ppermute x18, starting transfers between devices, shift(): return lax.ppermute(x, 'ctx', [(i, (i + d) % n) for i in range(n)])  59.5 us
    ppermute x18, waiting for transfers between devices, shift(): return lax.ppermute(x, 'ctx', [(i, (i + d) % n) for i in range(n)])  39.9 us
    ppermute x12, waiting for transfers between devices, reduce_rows(): lax.ppermute(give, 'ctx', [(step, step + 1), (n - 1 - step, n - 2 - step)])  36.1 us
    ppermute x12, starting transfers between devices, reduce_rows(): lax.ppermute(give, 'ctx', [(step, step + 1), (n - 1 - step, n - 2 - step)])  28.6 us
    ppermute x16, waiting for transfers between devices, flip(): return lax.ppermute(x, 'space', [(i, i ^ bit) for i in range(n_space)])  27.9 us
    ppermute x16, starting transfers between devices, flip(): return lax.ppermute(x, 'space', [(i, i ^ bit) for i in range(n_space)])  8.53 us
  transfers between devices with their start and end apart: 50, of which 20 were waited for; matrix products, arithmetic and copies ran while one was open for 17% of the time, Pallas kernels for 0%

profile of v1, /device:TPU:0, one launch (start us, length us, event | category | flops | bytes accessed | tf_op | source)
XLA Modules:
  0.0 371.3 jit_solution(8249492309943586891)
XLA Ops:
  15.4 9.4 %collective-permute-start.1 = (bf16[32,3072]{1,0:T(8,128)(2,1)}, bf16[32,3072]{1,0:T(8,128)(2,1)S(1)}, u32[]{:S(2)}, u32[]{:S(2)}) collective-permute-start(bf16[32,3072]{1,0:T(8,128)(2,1)} %get-tuple-element.44), channel_id=1, source_target_pairs={{0,8},{4,12},{8,0},{12,4},{1,9},{5,13},{9,1},{13,5},{2,10},{6,14},... | collective-permute-start | bytes 589832 | tf_op jit(solution)/shard_map/ppermute | solution.py:94
  24.8 5.1 %collective-permute-start.2 = (bf16[32,3072]{1,0:T(8,128)(2,1)}, bf16[32,3072]{1,0:T(8,128)(2,1)S(1)}, u32[]{:S(2)}, u32[]{:S(2)}) collective-permute-start(bf16[32,3072]{1,0:T(8,128)(2,1)} %get-tuple-element.43), channel_id=1, source_target_pairs={{0,12},{4,0},{8,4},{12,8},{1,13},{5,1},{9,5},{13,9},{2,14},{6,2},{... | collective-permute-start | bytes 589832 | tf_op jit(solution)/shard_map/ppermute | solution.py:94
  32.9 12.9 %collective-permute-start.24 = (bf16[32,3072]{1,0:T(8,128)(2,1)S(1)}, bf16[32,3072]{1,0:T(8,128)(2,1)S(1)}, u32[]{:S(2)}, u32[]{:S(2)}) collective-permute-start(bf16[32,3072]{1,0:T(8,128)(2,1)S(1)} %copy-done.22), channel_id=1, source_target_pairs={{0,8},{4,12},{8,0},{12,4},{1,9},{5,13},{9,1},{13,5},{2,10},{6,14},... | collective-permute-start | bytes 589832 | tf_op jit(solution)/shard_map/ppermute | solution.py:94
  45.8 9.3 %collective-permute-start.25 = (bf16[32,3072]{1,0:T(8,128)(2,1)S(1)}, bf16[32,3072]{1,0:T(8,128)(2,1)S(1)}, u32[]{:S(2)}, u32[]{:S(2)}) collective-permute-start(bf16[32,3072]{1,0:T(8,128)(2,1)S(1)} %copy-done.21), channel_id=1, source_target_pairs={{0,12},{4,0},{8,4},{12,8},{1,13},{5,1},{9,5},{13,9},{2,14},{6,2},{... | collective-permute-start | bytes 589832 | tf_op jit(solution)/shard_map/ppermute | solution.py:94
  69.1 6.2 %collective-permute-done.7 = bf16[32,3072]{1,0:T(8,128)(2,1)S(1)} collective-permute-done((bf16[32,3072]{1,0:T(8,128)(2,1)S(1)}, bf16[32,3072]{1,0:T(8,128)(2,1)S(1)}, u32[]{:S(2)}, u32[]{:S(2)}) %collective-permute-start.7) | collective-permute-done | bytes 196640 | tf_op jit(solution)/shard_map/ppermute | solution.py:94
  86.5 9.5 %collective-permute-done.26 = bf16[4,32,3072]{2,1,0:T(8,128)(2,1)S(1)} collective-permute-done((bf16[4,32,3072]{2,1,0:T(8,128)(2,1)S(1)}, bf16[4,32,3072]{2,1,0:T(8,128)(2,1)S(1)}, u32[]{:S(2)}, u32[]{:S(2)}) %collective-permute-start.26) | collective-permute-done | bytes 786464 | tf_op jit(solution)/shard_map/ppermute | solution.py:97
  96.0 15.8 %collective-permute-done.9 = bf16[4,32,3072]{2,1,0:T(8,128)(2,1)S(1)} collective-permute-done((bf16[4,32,3072]{2,1,0:T(8,128)(2,1)S(1)}, bf16[4,32,3072]{2,1,0:T(8,128)(2,1)S(1)}, u32[]{:S(2)}, u32[]{:S(2)}) %collective-permute-start.9) | collective-permute-done | bytes 786464 | tf_op jit(solution)/shard_map/ppermute | solution.py:97
  135.1 4.4 %fusion.30 = f32[512,3072]{1,0:T(8,128)} fusion(bf16[512,384]{1,0:T(8,128)(2,1)S(1)} %bitcast.185, bf16[3,3072,384]{2,1,0:T(8,128)(2,1)S(1)} %bitcast.210), kind=kOutput, calls=%fused_computation.45 | convolution fusion | flops 1207959552 | bytes 9043968 | tf_op jit(solution)/shard_map/dot_general | solution.py:75
  142.4 4.5 %fusion.34 = f32[512,3072]{1,0:T(8,128)} fusion(bf16[512,384]{1,0:T(8,128)(2,1)S(1)} %bitcast.189, bf16[3,3072,384]{2,1,0:T(8,128)(2,1)S(1)} %bitcast.210), kind=kOutput, calls=%fused_computation.49 | convolution fusion | flops 1207959552 | bytes 9043968 | tf_op jit(solution)/shard_map/dot_general | solution.py:75
  156.8 4.6 %add_convert_fusion = bf16[512,3072]{1,0:T(8,128)(2,1)S(1)} fusion(f32[512,3072]{1,0:T(8,128)} %fusion.30, f32[512,3072]{1,0:T(8,128)S(1)} %fusion.22, bf16[512,384]{1,0:T(8,128)(2,1)S(1)} %bitcast.200, bf16[3,3072,384]{2,1,0:T(8,128)(2,1)S(1)} %bitcast.210), kind=kOutput, calls=%fused_computation.10 | convolution fusion | flops 1212678144 | bytes 18481152 | tf_op jit(solution)/shard_map/dot_general | solution.py:75
  162.8 4.8 %add_convert_fusion.1 = bf16[512,3072]{1,0:T(8,128)(2,1)S(1)} fusion(f32[512,3072]{1,0:T(8,128)} %fusion.34, f32[512,3072]{1,0:T(8,128)S(1)} %fusion.26, bf16[512,384]{1,0:T(8,128)(2,1)S(1)} %bitcast.203, bf16[3,3072,384]{2,1,0:T(8,128)(2,1)S(1)} %bitcast.210), kind=kOutput, calls=%fused_computation.11 | convolution fusion | flops 1212678144 | bytes 18481152 | tf_op jit(solution)/shard_map/dot_general | solution.py:75
  167.8 11.3 %collective-permute-done.46 = bf16[1536,384]{1,0:T(8,128)(2,1)} collective-permute-done((bf16[1536,384]{1,0:T(8,128)(2,1)}, bf16[1536,384]{1,0:T(8,128)(2,1)}, u32[]{:S(2)}, u32[]{:S(2)}) %collective-permute-start.46) | collective-permute-done | bytes 1179680 | tf_op jit(solution)/shard_map/ppermute | solution.py:146
  182.5 21.8 %collective-permute-done.34 = bf16[1536,384]{1,0:T(8,128)(2,1)} collective-permute-done((bf16[1536,384]{1,0:T(8,128)(2,1)}, bf16[1536,384]{1,0:T(8,128)(2,1)}, u32[]{:S(2)}, u32[]{:S(2)}) %collective-permute-start.34) | collective-permute-done | bytes 1179680 | tf_op jit(solution)/shard_map/ppermute | solution.py:146
  204.3 5.2 %collective-permute-start.47 = (bf16[3,384,384]{2,1,0:T(8,128)(2,1)S(1)}, bf16[3,384,384]{2,1,0:T(8,128)(2,1)S(1)}, u32[]{:S(2)}, u32[]{:S(2)}) collective-permute-start(bf16[3,384,384]{2,1,0:T(8,128)(2,1)S(1)} %dynamic-slice_convert_fusion), channel_id=1, source_target_pairs={{0,4},{12,8},{1,5},{13,9},{2,6},{14,10},{3,7},{15,11},{16,20},{28,... | collective-permute-start | bytes 2654216 | tf_op jit(solution)/shard_map/ppermute | solution.py:153
  212.9 16.8 %collective-permute-done.38 = bf16[1536,384]{1,0:T(8,128)(2,1)} collective-permute-done((bf16[1536,384]{1,0:T(8,128)(2,1)S(1)}, bf16[1536,384]{1,0:T(8,128)(2,1)}, u32[]{:S(2)}, u32[]{:S(2)}) %collective-permute-start.38) | collective-permute-done | bytes 1179680 | tf_op jit(solution)/shard_map/ppermute | solution.py:146
  229.6 5.2 %collective-permute-start.35 = (bf16[3,384,384]{2,1,0:T(8,128)(2,1)S(1)}, bf16[3,384,384]{2,1,0:T(8,128)(2,1)S(1)}, u32[]{:S(2)}, u32[]{:S(2)}) collective-permute-start(bf16[3,384,384]{2,1,0:T(8,128)(2,1)S(1)} %dynamic-slice_convert_fusion.3), channel_id=1, source_target_pairs={{0,4},{12,8},{1,5},{13,9},{2,6},{14,10},{3,7},{15,11},{16,20},{28,... | collective-permute-start | bytes 2654216 | tf_op jit(solution)/shard_map/ppermute | solution.py:153
  238.1 15.8 %collective-permute-done.42 = bf16[1536,384]{1,0:T(8,128)(2,1)} collective-permute-done((bf16[1536,384]{1,0:T(8,128)(2,1)}, bf16[1536,384]{1,0:T(8,128)(2,1)}, u32[]{:S(2)}, u32[]{:S(2)}) %collective-permute-start.42) | collective-permute-done | bytes 1179680 | tf_op jit(solution)/shard_map/ppermute | solution.py:146
  254.0 5.2 %collective-permute-start.39 = (bf16[3,384,384]{2,1,0:T(8,128)(2,1)S(1)}, bf16[3,384,384]{2,1,0:T(8,128)(2,1)S(1)}, u32[]{:S(2)}, u32[]{:S(2)}) collective-permute-start(bf16[3,384,384]{2,1,0:T(8,128)(2,1)S(1)} %dynamic-slice_convert_fusion.2), channel_id=1, source_target_pairs={{0,4},{12,8},{1,5},{13,9},{2,6},{14,10},{3,7},{15,11},{16,20},{28,... | collective-permute-start | bytes 2654216 | tf_op jit(solution)/shard_map/ppermute | solution.py:153
  271.4 7.8 %collective-permute-done.39 = bf16[3,384,384]{2,1,0:T(8,128)(2,1)S(1)} collective-permute-done((bf16[3,384,384]{2,1,0:T(8,128)(2,1)S(1)}, bf16[3,384,384]{2,1,0:T(8,128)(2,1)S(1)}, u32[]{:S(2)}, u32[]{:S(2)}) %collective-permute-start.39) | collective-permute-done | bytes 884768 | tf_op jit(solution)/shard_map/ppermute | solution.py:153
  282.2 14.1 %collective-permute-done.43 = bf16[3,384,384]{2,1,0:T(8,128)(2,1)S(1)} collective-permute-done((bf16[3,384,384]{2,1,0:T(8,128)(2,1)S(1)}, bf16[3,384,384]{2,1,0:T(8,128)(2,1)S(1)}, u32[]{:S(2)}, u32[]{:S(2)}) %collective-permute-start.43) | collective-permute-done | bytes 884768 | tf_op jit(solution)/shard_map/ppermute | solution.py:153
  306.4 4.1 %collective-permute-start.14 = (bf16[32,3072]{1,0:T(8,128)(2,1)S(1)}, bf16[32,3072]{1,0:T(8,128)(2,1)S(1)}, u32[]{:S(2)}, u32[]{:S(2)}) collective-permute-start(bf16[32,3072]{1,0:T(8,128)(2,1)S(1)} %get-tuple-element.33), channel_id=1, source_target_pairs={{0,12},{4,0},{8,4},{12,8},{1,13},{5,1},{9,5},{13,9},{2,14},{6,2},{... | collective-permute-start | bytes 589832 | tf_op jit(solution)/shard_map/ppermute | solution.py:94
  310.5 16.5 %collective-permute-done.32 = bf16[32,3072]{1,0:T(8,128)(2,1)S(1)} collective-permute-done((bf16[32,3072]{1,0:T(8,128)(2,1)S(1)}, bf16[32,3072]{1,0:T(8,128)(2,1)S(1)}, u32[]{:S(2)}, u32[]{:S(2)}) %collective-permute-start.32) | collective-permute-done | bytes 196640 | tf_op jit(solution)/shard_map/ppermute | solution.py:94
  329.2 8.5 %collective-permute-done.15 = bf16[32,3072]{1,0:T(8,128)(2,1)S(1)} collective-permute-done((bf16[32,3072]{1,0:T(8,128)(2,1)S(1)}, bf16[32,3072]{1,0:T(8,128)(2,1)S(1)}, u32[]{:S(2)}, u32[]{:S(2)}) %collective-permute-start.15) | collective-permute-done | bytes 196640 | tf_op jit(solution)/shard_map/ppermute | solution.py:94
  363.1 5.6 %collective-permute-done.45 = bf16[1,384,384]{2,1,0:T(8,128)(2,1)S(1)} collective-permute-done((bf16[1,384,384]{2,1,0:T(8,128)(2,1)S(1)}, bf16[1,384,384]{2,1,0:T(8,128)(2,1)S(1)}, u32[]{:S(2)}, u32[]{:S(2)}) %collective-permute-start.45) | collective-permute-done | bytes 294944 | tf_op jit(solution)/shard_map/ppermute | solution.py:153
  (215 shorter events, 144.8 us)
Async XLA Ops:
  12.1 44.3 %collective-permute-start.23 = (bf16[32,3072]{1,0:T(8,128)(2,1)}, bf16[32,3072]{1,0:T(8,128)(2,1)}, u32[]{:S(2)}, u32[]{:S(2)}) collective-permute-start(bf16[32,3072]{1,0:T(8,128)(2,1)} %get-tuple-element.55), channel_id=1, source_target_pairs={{0,4},{4,8},{8,12},{12,0},{1,5},{5,9},{9,13},{13,1},{2,6},{6,10},{... | collective-permute-start | bytes 589832 | tf_op jit(solution)/shard_map/ppermute | solution.py:94
  15.4 30.5 %collective-permute-start.1 = (bf16[32,3072]{1,0:T(8,128)(2,1)}, bf16[32,3072]{1,0:T(8,128)(2,1)S(1)}, u32[]{:S(2)}, u32[]{:S(2)}) collective-permute-start(bf16[32,3072]{1,0:T(8,128)(2,1)} %get-tuple-element.44), channel_id=1, source_target_pairs={{0,8},{4,12},{8,0},{12,4},{1,9},{5,13},{9,1},{13,5},{2,10},{6,14},... | collective-permute-start | bytes 589832 | tf_op jit(solution)/shard_map/ppermute | solution.py:94
  24.8 30.4 %collective-permute-start.2 = (bf16[32,3072]{1,0:T(8,128)(2,1)}, bf16[32,3072]{1,0:T(8,128)(2,1)S(1)}, u32[]{:S(2)}, u32[]{:S(2)}) collective-permute-start(bf16[32,3072]{1,0:T(8,128)(2,1)} %get-tuple-element.43), channel_id=1, source_target_pairs={{0,12},{4,0},{8,4},{12,8},{1,13},{5,1},{9,5},{13,9},{2,14},{6,2},{... | collective-permute-start | bytes 589832 | tf_op jit(solution)/shard_map/ppermute | solution.py:94
  31.2 29.0 %collective-permute-start.20 = (bf16[4,32,3072]{2,1,0:T(8,128)(2,1)S(1)}, bf16[4,32,3072]{2,1,0:T(8,128)(2,1)S(1)}, u32[]{:S(2)}, u32[]{:S(2)}) collective-permute-start(bf16[4,32,3072]{2,1,0:T(8,128)(2,1)S(1)} %get-tuple-element.57), channel_id=1, source_target_pairs={{0,2},{1,3},{2,0},{3,1},{4,6},{5,7},{6,4},{7,5},{8,10},{9,11},{10,... | collective-permute-start | bytes 2359304 | tf_op jit(solution)/shard_map/ppermute | solution.py:97
  32.9 25.8 %collective-permute-start.24 = (bf16[32,3072]{1,0:T(8,128)(2,1)S(1)}, bf16[32,3072]{1,0:T(8,128)(2,1)S(1)}, u32[]{:S(2)}, u32[]{:S(2)}) collective-permute-start(bf16[32,3072]{1,0:T(8,128)(2,1)S(1)} %copy-done.22), channel_id=1, source_target_pairs={{0,8},{4,12},{8,0},{12,4},{1,9},{5,13},{9,1},{13,5},{2,10},{6,14},... | collective-permute-start | bytes 589832 | tf_op jit(solution)/shard_map/ppermute | solution.py:94
  75.9 40.5 %collective-permute-start.27 = (bf16[4,32,3072]{2,1,0:T(8,128)(2,1)S(1)}, bf16[4,32,3072]{2,1,0:T(8,128)(2,1)S(1)}, u32[]{:S(2)}, u32[]{:S(2)}) collective-permute-start(bf16[4,32,3072]{2,1,0:T(8,128)(2,1)S(1)} %get-tuple-element.51), channel_id=1, source_target_pairs={{0,1},{1,0},{2,3},{3,2},{4,5},{5,4},{6,7},{7,6},{8,9},{9,8},{10,11... | collective-permute-start | bytes 2359304 | tf_op jit(solution)/shard_map/ppermute | solution.py:97
  76.0 35.7 %collective-permute-start.4 = (bf16[4,32,3072]{2,1,0:T(8,128)(2,1)S(1)}, bf16[4,32,3072]{2,1,0:T(8,128)(2,1)S(1)}, u32[]{:S(2)}, u32[]{:S(2)}) collective-permute-start(bf16[4,32,3072]{2,1,0:T(8,128)(2,1)S(1)} %get-tuple-element.41), channel_id=1, source_target_pairs={{0,1},{1,0},{2,3},{3,2},{4,5},{5,4},{6,7},{7,6},{8,9},{9,8},{10,11... | collective-permute-start | bytes 2359304 | tf_op jit(solution)/shard_map/ppermute | solution.py:97
  79.1 32.7 %collective-permute-start.9 = (bf16[4,32,3072]{2,1,0:T(8,128)(2,1)S(1)}, bf16[4,32,3072]{2,1,0:T(8,128)(2,1)S(1)}, u32[]{:S(2)}, u32[]{:S(2)}) collective-permute-start(bf16[4,32,3072]{2,1,0:T(8,128)(2,1)S(1)} %get-tuple-element.35), channel_id=1, source_target_pairs={{0,2},{1,3},{2,0},{3,1},{4,6},{5,7},{6,4},{7,5},{8,10},{9,11},{10,... | collective-permute-start | bytes 2359304 | tf_op jit(solution)/shard_map/ppermute | solution.py:97
  80.6 31.7 %collective-permute-start.5 = (bf16[4,32,3072]{2,1,0:T(8,128)(2,1)S(1)}, bf16[4,32,3072]{2,1,0:T(8,128)(2,1)S(1)}, u32[]{:S(2)}, u32[]{:S(2)}) collective-permute-start(bf16[4,32,3072]{2,1,0:T(8,128)(2,1)S(1)} %collective-permute-done.3), channel_id=1, source_target_pairs={{0,1},{1,0},{2,3},{3,2},{4,5},{5,4},{6,7},{7,6},{8,9},{9,8},{10,11... | collective-permute-start | bytes 2359304 | tf_op jit(solution)/shard_map/ppermute | solution.py:97
  149.9 29.1 %collective-permute-start.46 = (bf16[1536,384]{1,0:T(8,128)(2,1)}, bf16[1536,384]{1,0:T(8,128)(2,1)}, u32[]{:S(2)}, u32[]{:S(2)}) collective-permute-start(bf16[1536,384]{1,0:T(8,128)(2,1)} %fusion.13), channel_id=1, source_target_pairs={{0,16},{16,0},{1,17},{17,1},{2,18},{18,2},{3,19},{19,3},{4,20},{20... | collective-permute-start | bytes 3538952 | tf_op jit(solution)/shard_map/ppermute | solution.py:146
  151.4 53.0 %collective-permute-start.34 = (bf16[1536,384]{1,0:T(8,128)(2,1)}, bf16[1536,384]{1,0:T(8,128)(2,1)}, u32[]{:S(2)}, u32[]{:S(2)}) collective-permute-start(bf16[1536,384]{1,0:T(8,128)(2,1)} %convolution_convert_fusion.2), channel_id=1, source_target_pairs={{0,16},{16,0},{1,17},{17,1},{2,18},{18,2},{3,19},{19,3},{4,20},{20... | collective-permute-start | bytes 3538952 | tf_op jit(solution)/shard_map/ppermute | solution.py:146
  151.9 77.7 %collective-permute-start.38 = (bf16[1536,384]{1,0:T(8,128)(2,1)S(1)}, bf16[1536,384]{1,0:T(8,128)(2,1)}, u32[]{:S(2)}, u32[]{:S(2)}) collective-permute-start(bf16[1536,384]{1,0:T(8,128)(2,1)S(1)} %convolution_convert_fusion.1), channel_id=1, source_target_pairs={{0,16},{16,0},{1,17},{17,1},{2,18},{18,2},{3,19},{19,3},{4,20},{20... | collective-permute-start | bytes 3538952 | tf_op jit(solution)/shard_map/ppermute | solution.py:146
  156.2 97.7 %collective-permute-start.42 = (bf16[1536,384]{1,0:T(8,128)(2,1)}, bf16[1536,384]{1,0:T(8,128)(2,1)}, u32[]{:S(2)}, u32[]{:S(2)}) collective-permute-start(bf16[1536,384]{1,0:T(8,128)(2,1)} %convolution_convert_fusion), channel_id=1, source_target_pairs={{0,16},{16,0},{1,17},{17,1},{2,18},{18,2},{3,19},{19,3},{4,20},{20... | collective-permute-start | bytes 3538952 | tf_op jit(solution)/shard_map/ppermute | solution.py:146
  162.8 99.7 %collective-permute-start.29 = (bf16[2,4,32,3072]{3,2,1,0:T(8,128)(2,1)}, bf16[2,4,32,3072]{3,2,1,0:T(8,128)(2,1)S(1)}, u32[]{:S(2)}, u32[]{:S(2)}) collective-permute-start(bf16[2,4,32,3072]{3,2,1,0:T(8,128)(2,1)} %bitcast.75), channel_id=1, source_target_pairs={{0,1},{1,0},{2,3},{3,2},{4,5},{5,4},{6,7},{7,6},{8,9},{9,8},{10,11... | collective-permute-start | bytes 4718600 | tf_op jit(solution)/shard_map/ppermute | solution.py:97
  179.1 85.5 %collective-permute-start.12 = (bf16[2,4,32,3072]{3,2,1,0:T(8,128)(2,1)S(1)}, bf16[2,4,32,3072]{3,2,1,0:T(8,128)(2,1)S(1)}, u32[]{:S(2)}, u32[]{:S(2)}) collective-permute-start(bf16[2,4,32,3072]{3,2,1,0:T(8,128)(2,1)S(1)} %bitcast.238), channel_id=1, source_target_pairs={{0,1},{1,0},{2,3},{3,2},{4,5},{5,4},{6,7},{7,6},{8,9},{9,8},{10,11... | collective-permute-start | bytes 4718600 | tf_op jit(solution)/shard_map/ppermute | solution.py:97
  204.3 62.0 %collective-permute-start.47 = (bf16[3,384,384]{2,1,0:T(8,128)(2,1)S(1)}, bf16[3,384,384]{2,1,0:T(8,128)(2,1)S(1)}, u32[]{:S(2)}, u32[]{:S(2)}) collective-permute-start(bf16[3,384,384]{2,1,0:T(8,128)(2,1)S(1)} %dynamic-slice_convert_fusion), channel_id=1, source_target_pairs={{0,4},{12,8},{1,5},{13,9},{2,6},{14,10},{3,7},{15,11},{16,20},{28,... | collective-permute-start | bytes 2654216 | tf_op jit(solution)/shard_map/ppermute | solution.py:153
  229.6 39.0 %collective-permute-start.35 = (bf16[3,384,384]{2,1,0:T(8,128)(2,1)S(1)}, bf16[3,384,384]{2,1,0:T(8,128)(2,1)S(1)}, u32[]{:S(2)}, u32[]{:S(2)}) collective-permute-start(bf16[3,384,384]{2,1,0:T(8,128)(2,1)S(1)} %dynamic-slice_convert_fusion.3), channel_id=1, source_target_pairs={{0,4},{12,8},{1,5},{13,9},{2,6},{14,10},{3,7},{15,11},{16,20},{28,... | collective-permute-start | bytes 2654216 | tf_op jit(solution)/shard_map/ppermute | solution.py:153
  254.0 25.3 %collective-permute-start.39 = (bf16[3,384,384]{2,1,0:T(8,128)(2,1)S(1)}, bf16[3,384,384]{2,1,0:T(8,128)(2,1)S(1)}, u32[]{:S(2)}, u32[]{:S(2)}) collective-permute-start(bf16[3,384,384]{2,1,0:T(8,128)(2,1)S(1)} %dynamic-slice_convert_fusion.2), channel_id=1, source_target_pairs={{0,4},{12,8},{1,5},{13,9},{2,6},{14,10},{3,7},{15,11},{16,20},{28,... | collective-permute-start | bytes 2654216 | tf_op jit(solution)/shard_map/ppermute | solution.py:153
  262.5 33.9 %collective-permute-start.43 = (bf16[3,384,384]{2,1,0:T(8,128)(2,1)S(1)}, bf16[3,384,384]{2,1,0:T(8,128)(2,1)S(1)}, u32[]{:S(2)}, u32[]{:S(2)}) collective-permute-start(bf16[3,384,384]{2,1,0:T(8,128)(2,1)S(1)} %dynamic-slice_convert_fusion.1), channel_id=1, source_target_pairs={{0,4},{12,8},{1,5},{13,9},{2,6},{14,10},{3,7},{15,11},{16,20},{28,... | collective-permute-start | bytes 2654216 | tf_op jit(solution)/shard_map/ppermute | solution.py:153
  264.5 33.1 %collective-permute-start.30 = (bf16[1,4,32,3072]{3,2,1,0:T(8,128)(2,1)S(1)}, bf16[1,4,32,3072]{3,2,1,0:T(8,128)(2,1)S(1)}, u32[]{:S(2)}, u32[]{:S(2)}) collective-permute-start(bf16[1,4,32,3072]{3,2,1,0:T(8,128)(2,1)S(1)} %slice.144), channel_id=1, source_target_pairs={{0,2},{1,3},{2,0},{3,1},{4,6},{5,7},{6,4},{7,5},{8,10},{9,11},{10,... | collective-permute-start | bytes 2359304 | tf_op jit(solution)/shard_map/ppermute | solution.py:97
  266.4 35.8 %collective-permute-start.13 = (bf16[1,4,32,3072]{3,2,1,0:T(8,128)(2,1)S(1)}, bf16[1,4,32,3072]{3,2,1,0:T(8,128)(2,1)S(1)}, u32[]{:S(2)}, u32[]{:S(2)}) collective-permute-start(bf16[1,4,32,3072]{3,2,1,0:T(8,128)(2,1)S(1)} %slice.134), channel_id=1, source_target_pairs={{0,2},{1,3},{2,0},{3,1},{4,6},{5,7},{6,4},{7,5},{8,10},{9,11},{10,... | collective-permute-start | bytes 2359304 | tf_op jit(solution)/shard_map/ppermute | solution.py:97
  268.7 73.0 %collective-permute-start.48 = (bf16[2,384,384]{2,1,0:T(8,128)(2,1)}, bf16[2,384,384]{2,1,0:T(8,128)(2,1)}, u32[]{:S(2)}, u32[]{:S(2)}) collective-permute-start(bf16[2,384,384]{2,1,0:T(8,128)(2,1)} %dynamic-slice_convert_fusion.4), channel_id=1, source_target_pairs={{4,8},{8,4},{5,9},{9,5},{6,10},{10,6},{7,11},{11,7},{20,24},{24,20... | collective-permute-start | bytes 1769480 | tf_op jit(solution)/shard_map/ppermute | solution.py:153
  279.3 66.0 %collective-permute-start.36 = (bf16[2,384,384]{2,1,0:T(8,128)(2,1)}, bf16[2,384,384]{2,1,0:T(8,128)(2,1)}, u32[]{:S(2)}, u32[]{:S(2)}) collective-permute-start(bf16[2,384,384]{2,1,0:T(8,128)(2,1)} %dynamic-slice_convert_fusion.7), channel_id=1, source_target_pairs={{4,8},{8,4},{5,9},{9,5},{6,10},{10,6},{7,11},{11,7},{20,24},{24,20... | collective-permute-start | bytes 1769480 | tf_op jit(solution)/shard_map/ppermute | solution.py:153
  300.7 26.2 %collective-permute-start.32 = (bf16[32,3072]{1,0:T(8,128)(2,1)S(1)}, bf16[32,3072]{1,0:T(8,128)(2,1)S(1)}, u32[]{:S(2)}, u32[]{:S(2)}) collective-permute-start(bf16[32,3072]{1,0:T(8,128)(2,1)S(1)} %get-tuple-element.48), channel_id=1, source_target_pairs={{0,8},{4,12},{8,0},{12,4},{1,9},{5,13},{9,1},{13,5},{2,10},{6,14},... | collective-permute-start | bytes 589832 | tf_op jit(solution)/shard_map/ppermute | solution.py:94
  (51 other events, 730.6 us)

commit v2 on v1

v2 whole, which is shorter than its diff:
```python
import functools
import math

import jax
import jax.numpy as jnp
from jax import lax
from jax.experimental import pallas as pl
from jax.experimental.pallas import tpu as pltpu
from jax.sharding import PartitionSpec as P

HS = 128
F32 = jnp.float32
BF16 = jnp.bfloat16
SCALE = 1.0 / math.sqrt(HS)


FREE = pl.CostEstimate(flops=1, bytes_accessed=1, transcendentals=0)
PARAMS = pltpu.CompilerParams(vmem_limit_bytes=60 * 1024 * 1024)
SMALL = pltpu.CompilerParams(vmem_limit_bytes=40 * 1024 * 1024)


def softmax_row(q, keys):
    scores = [jnp.sum(q * k, axis=-1, keepdims=True) * SCALE for k in keys]
    top = functools.reduce(jnp.maximum, scores)
    expo = [jnp.exp(s - top) for s in scores]
    total = functools.reduce(jnp.add, expo)
    return [e / total for e in expo]


def weighted(weights, values):
    return functools.reduce(jnp.add, [w * v for w, v in zip(weights, values)])


def rounded(values):
    return [v.astype(BF16).astype(F32) for v in values]


def forward_kernel(frames, heads, slot_ref, q_ref, k_ref, v_ref, att_ref):
    slots = [slot_ref[f] for f in range(frames)]
    for h in range(heads):
        cols = pl.ds(h * HS, HS)
        q, k, v = (
            [ref[0, slots[f], :, cols].astype(F32) for f in range(frames)]
            for ref in (q_ref, k_ref, v_ref)
        )
        for f in range(frames):
            probs_b = rounded(softmax_row(q[f], k[: f + 1]))
            att_ref[0, slots[f], :, cols] = weighted(probs_b, v).astype(BF16)


def backward_kernel(frames, heads, slot_ref, q_ref, k_ref, v_ref, near_ref, far_ref, dq_ref, dk_ref, dv_ref):
    slots = [slot_ref[f] for f in range(frames)]
    for h in range(heads):
        cols = pl.ds(h * HS, HS)
        q, k, v = (
            [ref[0, slots[f], :, cols].astype(F32) for f in range(frames)]
            for ref in (q_ref, k_ref, v_ref)
        )
        far = far_ref[0, 0, :, cols].astype(F32)
        o = [
            jnp.where(
                slots[f] == frames - 1,
                far,
                near_ref[0, jnp.minimum(slots[f], frames - 2), :, cols].astype(F32),
            )
            for f in range(frames)
        ]
        dk = [None] * frames
        dv = [None] * frames
        for f in range(frames):
            probs = softmax_row(q[f], k[: f + 1])
            probs_b = rounded(probs)
            dprobs = [jnp.sum(o[f] * v[g], axis=-1, keepdims=True) for g in range(f + 1)]
            inner = weighted(probs, dprobs)
            dscores = rounded([p * (d - inner) for p, d in zip(probs, dprobs)])
            dq = weighted(dscores, k)
            dq_ref[0, slots[f], :, cols] = (dq * SCALE).astype(BF16)
            for g in range(f + 1):
                add_k, add_v = dscores[g] * q[f], probs_b[g] * o[f]
                dk[g] = add_k if dk[g] is None else dk[g] + add_k
                dv[g] = add_v if dv[g] is None else dv[g] + add_v
        for g in range(frames):
            dk_ref[0, slots[g], :, cols] = (dk[g] * SCALE).astype(BF16)
            dv_ref[0, slots[g], :, cols] = dv[g].astype(BF16)


def per_group(kernel, slots, args, count):
    groups, frames, patches, width = args[0].shape

    def block(shape):
        return pl.BlockSpec((1,) + shape[1:], lambda i, slot_ref: (i, 0, 0, 0))

    out = jax.ShapeDtypeStruct(args[0].shape, BF16)
    return pl.pallas_call(
        functools.partial(kernel, frames, width // HS),
        grid_spec=pltpu.PrefetchScalarGridSpec(
            num_scalar_prefetch=1,
            grid=(groups,),
            in_specs=[block(a.shape) for a in args],
            out_specs=[block(out.shape)] * count,
        ),
        out_shape=[out] * count,
        compiler_params=SMALL,
        cost_estimate=FREE,
    )(slots, *args)


def mxu(a, b, contract):
    return lax.dot_general(a, b, ((contract[:1], contract[1:]), ((), ())), preferred_element_type=F32)


def block_of(extent, most):
    size = most - most % 128
    while extent % size:
        size -= 128
    return size


def in_order(sets):
    pieces = []
    for e in range(2 * len(sets[0])):
        for held in sets:
            array = held[e // 2]
            size = array.shape[1] * array.shape[2]
            pieces.append((array.reshape(-1, array.shape[-1]), size, e % 2))
    return pieces


def project(sets, weights):
    pieces = in_order(sets)
    count, model, width = weights.shape
    total = sum(size for _, size, _ in pieces)

    def kernel(*refs):
        x_refs, w_ref, x_ref = refs[: len(pieces)], refs[len(pieces)], refs[-1]
        step = pl.program_id(0)

        @pl.when(step == 0)
        def _():
            row = 0
            for ref, (_, size, _) in zip(x_refs, pieces):
                x_ref[row : row + size] = ref[...]
                row += size

        product = mxu(x_ref[...], w_ref[0], (1, 0)).astype(BF16)
        for s, out_ref in enumerate(refs[len(pieces) + 1 : -1]):

            @pl.when(step == s)
            def _():
                out_ref[...] = product

    out = jax.ShapeDtypeStruct((total, width), BF16)
    outs = pl.pallas_call(
        kernel,
        grid=(count,),
        in_specs=[pl.BlockSpec((size, model), lambda i, at=at: (at, 0)) for _, size, at in pieces]
        + [pl.BlockSpec((1, model, width), lambda i: (i, 0, 0))],
        out_specs=[pl.BlockSpec(out.shape, lambda i: (0, 0))] * count,
        out_shape=[out] * count,
        scratch_shapes=[pltpu.VMEM((total, model), BF16)],
        compiler_params=SMALL,
        cost_estimate=FREE,
    )(*[array for array, _, _ in pieces], weights)
    rows = sets[0][0].shape[2]
    return [o.reshape(2 * len(sets[0]), -1, rows, width) for o in outs]


def outer(sets, grads, column, share, dtype, plus=None):
    pieces = in_order(sets)
    width = grads[0].shape[-1]
    count = len(grads)
    wide = block_of(share, 768)
    steps = share // wide
    extra = [] if plus is None else [plus]

    def kernel(column_ref, *refs):
        x = jnp.concatenate([ref[...] for ref in refs[: len(pieces)]], 0)
        grad_refs = refs[len(pieces) : len(pieces) + count]
        for grad_ref, out_ref in zip(grad_refs, refs[-count:]):
            total = mxu(x, grad_ref[...], (0, 0))
            if extra:
                total = total + refs[len(pieces) + count][...]
            out_ref[...] = total.astype(dtype)

    grads = [g.reshape(-1, width) for g in grads]
    out = jax.ShapeDtypeStruct((share, width), dtype)
    tile = pl.BlockSpec((wide, width), lambda i, c: (i, 0))
    return pl.pallas_call(
        kernel,
        grid_spec=pltpu.PrefetchScalarGridSpec(
            num_scalar_prefetch=1,
            grid=(steps,),
            in_specs=[
                pl.BlockSpec((size, wide), lambda i, c, at=at: (at, c[0] * steps + i))
                for _, size, at in pieces
            ]
            + [pl.BlockSpec(g.shape, lambda i, c: (0, 0)) for g in grads]
            + [tile] * len(extra),
            out_specs=[tile] * count,
        ),
        out_shape=[out] * count,
        compiler_params=PARAMS,
        cost_estimate=FREE,
    )(jnp.asarray(column, jnp.int32).reshape(1), *[array for array, _, _ in pieces], *grads, *extra)


def backproject(grads, block, rows, weights, splits=None):
    _, model, width = weights[0].shape
    wide = block_of(model, 512)
    splits = splits or [rows]
    count = len(grads)

    def kernel(*refs):
        w_refs, out_refs = refs[count : count + len(weights)], refs[-len(splits) :]
        matrices = [w_ref[s] for w_ref in w_refs for s in range(w_ref.shape[0])]
        total = sum(mxu(ref[...], w, (1, 1)) for ref, w in zip(refs[:count], matrices))
        row = 0
        for size, out_ref in zip(splits, out_refs):
            out_ref[...] = total[row : row + size].astype(BF16)
            row += size

    return pl.pallas_call(
        kernel,
        grid=(model // wide,),
        in_specs=[pl.BlockSpec((rows, width), lambda i: (block, 0))] * count
        + [pl.BlockSpec((w.shape[0], wide, width), lambda i: (0, i, 0)) for w in weights],
        out_specs=[pl.BlockSpec((size, wide), lambda i: (0, i)) for size in splits],
        out_shape=[jax.ShapeDtypeStruct((size, model), BF16) for size in splits],
        compiler_params=PARAMS,
        cost_estimate=FREE,
    )(*[g.reshape(-1, width) for g in grads], *weights)


def placed_at(pieces, where):
    shape = pieces[0].shape
    count = len(pieces)

    def kernel(where_ref, *refs):
        for i in range(count):

            @pl.when(pl.program_id(0) == i)
            def _():
                refs[-1][0] = refs[i][...]

    return pl.pallas_call(
        kernel,
        grid_spec=pltpu.PrefetchScalarGridSpec(
            num_scalar_prefetch=1,
            grid=(count,),
            in_specs=[pl.BlockSpec(shape, lambda i, w: (0, 0))] * count,
            out_specs=pl.BlockSpec((1,) + shape, lambda i, w: (w[i], 0, 0)),
        ),
        out_shape=jax.ShapeDtypeStruct((count,) + shape, pieces[0].dtype),
        compiler_params=PARAMS,
        cost_estimate=FREE,
    )(where, *pieces)


def tie(x, *first):
    return lax.optimization_barrier((x, *first))[0]


def tie_all(*x):
    return lax.optimization_barrier(x)


def body(sizes, inputs, upstream, qkv_weight, out_weight):
    n_dp, n, n_space = sizes
    me = lax.axis_index("ctx")
    me_dp = lax.axis_index("dp")
    clips, single, patches, model = inputs.shape
    width = qkv_weight.shape[2]
    rows = clips * single * patches // n
    bits = [1 << i for i in range(n_space.bit_length() - 1)][::-1]
    order = [0] + [d for d in range(1, n) if d != n // 2] + [n // 2]
    place = {d: i for i, d in enumerate(order)}
    slots = jnp.array([place[d] for d in range(n)], jnp.int32)[
        lax.rem(me - jnp.arange(n) + n, n)
    ]
    home, others, across = order[:1], order[1:-1], order[-1:]

    def shift(x, d):
        return lax.ppermute(x, "ctx", [(i, (i + d) % n) for i in range(n)])

    def flip(x, bit):
        return lax.ppermute(x, "space", [(i, i ^ bit) for i in range(n_space)])

    def swap(x):
        return lax.ppermute(x, "dp", [(0, 1), (1, 0)])

    def to(x, d):
        x = x.reshape(n, rows, model)
        return lax.dynamic_index_in_dim(x, lax.rem(me + d, n), 0, keepdims=False)

    def spread(held):
        held = [held]
        for bit in bits[1:]:
            held = held + [flip(h, bit) for h in held]
        return held

    share = model // n_dp

    def lend(held):
        return swap(lax.dynamic_slice_in_dim(held, (1 - me_dp) * share, share, 3))

    def cut(x, ds):
        return [to(x, d) for d in ds]

    def moved(pieces, ds):
        return [shift(p, d) for p, d in zip(pieces, ds)]

    here_hi, here_hu = to(inputs, 0)[None], to(upstream, 0)[None]
    send_ci, send_cu, send_bu = cut(inputs, others), cut(upstream, others), cut(upstream, across)

    near_bi = moved(cut(inputs, across), across)
    there_hi, there_hu = flip(here_hi, bits[0]), flip(here_hu, bits[0])
    weights = [qkv_weight, flip(qkv_weight, bits[-1])]
    near_bi, there_hi, there_hu, weights, send_ci, send_cu, send_bu = tie_all(
        near_bi, there_hi, there_hu, weights, send_ci, send_cu, send_bu
    )

    pair_hi, pair_hu = jnp.stack([here_hi, there_hi]), jnp.stack([here_hu, there_hu])
    here_bi = jnp.stack(near_bi)
    near_ci = moved(send_ci, others)
    there_bi = flip(here_bi, bits[0])
    lent_hi = lend(pair_hi)
    all_hi = spread(pair_hi)
    near_ci, there_bi, lent_hi, all_hi, pair_hu, send_cu, send_bu = tie_all(
        near_ci, there_bi, lent_hi, all_hi, pair_hu, send_cu, send_bu
    )

    pair_bi = jnp.stack([here_bi, there_bi])
    here_ci = jnp.stack(near_ci)
    near_cu = moved(send_cu, others)
    there_ci = flip(here_ci, bits[0])
    lent_bi = lend(pair_bi)
    all_bi = spread(pair_bi)
    near_cu, there_ci, lent_bi, all_bi, pair_hu, lent_hi, send_bu = tie_all(
        near_cu, there_ci, lent_bi, all_bi, pair_hu, lent_hi, send_bu
    )

    pair_ci = jnp.stack([here_ci, there_ci])
    here_cu = jnp.stack(near_cu)
    near_bu = moved(send_bu, across)
    there_cu = flip(here_cu, bits[0])
    lent_ci = lend(pair_ci)
    all_ci = spread(pair_ci)
    tokens = [all_hi, all_ci, all_bi]
    q, k, v = project(tokens, qkv_weight)
    near_bu, there_cu, lent_ci, q, k, v, lent_hi, lent_bi, pair_hu = tie_all(
        near_bu, there_cu, lent_ci, q, k, v, lent_hi, lent_bi, pair_hu
    )

    pair_cu = jnp.stack([here_cu, there_cu])
    here_bu = jnp.stack(near_bu)
    there_bu = flip(here_bu, bits[0])
    all_hu, all_cu = spread(pair_hu), spread(pair_cu)
    from_hi, from_bi = spread(lent_hi), spread(lent_bi)
    (o_near,) = project([all_hu, all_cu], out_weight[None])
    there_bu, from_hi, from_bi, o_near, all_hu, all_cu, lent_ci = tie_all(
        there_bu, from_hi, from_bi, o_near, all_hu, all_cu, lent_ci
    )

    all_bu = spread(jnp.stack([here_bu, there_bu]))
    (o_far,) = project([all_bu], out_weight[None])
    ups = [all_hu, all_cu, all_bu]
    grads = list(per_group(backward_kernel, slots, (q, k, v, o_near, o_far), 3))
    grads = list(tie_all(*grads))

    def along_ctx(term):
        return lax.psum_scatter(term, "ctx", scatter_dimension=0, tiled=True)

    def summed(a, b):
        return (a.astype(F32) + b.astype(F32)).astype(BF16)

    for _ in bits[2:]:
        raise NotImplementedError
    crossed = swap(grads[0])
    got = flip(jnp.stack([g[n_space // 2 :] for g in grads]), bits[-1])
    lent = [from_hi, spread(lent_ci), from_bi]
    mine = outer(tokens, grads, me_dp, share, F32)
    (att,) = per_group(forward_kernel, slots, (q, k, tie(v, mine[0])), 1)
    (proj_send,) = outer(ups, [att], 1 - me_dp, share, BF16)
    crossed, got, lent, mine, att, proj_send, grads = tie_all(
        crossed, got, lent, mine, att, proj_send, grads
    )

    moving = swap(grads[1])
    (term,) = outer(lent, [crossed], 0, share, BF16, mine[0])
    sums = [along_ctx(term)]
    parts = [tie(g, term) for g in grads] + [got[s] for s in range(3)]
    home, mid, far = backproject(parts, 1, n * rows, weights, [rows, (n - 2) * rows, rows])
    crossed, home, mid, far, mine, grads, parts = tie_all(
        moving, home, mid, far, mine, grads, parts
    )

    moving = swap(grads[2])
    far_there, mid_there = flip(far, bits[0]), flip(mid, bits[0])
    (term,) = outer(lent, [crossed], 0, share, BF16, mine[1])
    kept = backproject([tie(p, term) for p in parts], 0, n * rows, weights, [rows] * n)
    sums.append(along_ctx(tie(term, sums[-1])))
    crossed, far_there, mid_there, mine, kept, proj_send, sums[0] = tie_all(
        moving, far_there, mid_there, mine, kept, proj_send, sums[0]
    )

    moving = swap(proj_send)
    home_there = flip(home, bits[0])
    back = {across[0]: shift(summed(kept[n - 1], far_there), n - across[0])}
    mid_sums = [
        summed(kept[1 + i], mid_there[i * rows : (i + 1) * rows]) for i in range(n - 2)
    ]
    (term,) = outer(lent, [crossed], 0, share, BF16, mine[2])
    (proj_mine,) = outer(ups, [tie(att, term)], me_dp, share, F32)
    sums.append(along_ctx(tie(term, sums[-1])))
    crossed, home_there, back, mid_sums, proj_mine, sums[1] = tie_all(
        moving, home_there, back, mid_sums, proj_mine, sums[1]
    )

    for i, d in enumerate(others):
        back[d] = shift(mid_sums[i], n - d)
    back[0] = summed(kept[0], home_there)
    term = summed(proj_mine, crossed)
    where = lax.rem(jnp.arange(n, dtype=jnp.int32) + me, n)
    input_grad = placed_at([back[d] for d in range(n)], where)
    sums.append(along_ctx(tie(term, sums[-1], input_grad)))
    qkv_grad = jnp.stack([x.astype(F32) for x in sums[:3]])
    return (input_grad.reshape(inputs.shape), qkv_grad, sums[3].astype(F32))


def solution(mesh):
    placed = (
        P("dp", "ctx", "space", None),
        P("dp", "ctx", "space", None),
        P(None, None, "space"),
        P(None, "space"),
    )
    sizes = tuple(mesh.shape[a] for a in ("dp", "ctx", "space"))
    return jax.shard_map(
        functools.partial(body, sizes),
        mesh=mesh,
        in_specs=placed,
        out_specs=(
            P("dp", "ctx", "space", None),
            P(None, ("dp", "ctx"), "space"),
            P(("dp", "ctx"), "space"),
        ),
        check_vma=False,
    )
```

time: 374 us -> 319 us (0.85)
  Pallas kernels: 4.66 us -> 83.1 us
  starting transfers between devices: 101 us -> 33.8 us
  matrix products: 59.6 us -> 0 us
  waiting for transfers between devices: 170 us -> 157 us
  between operations: 1.84 us -> 14.4 us
  other arithmetic: 17.7 us -> 12.2 us
    ppermute x16 -> x7, waiting for transfers between devices: 102 us -> 19.9 us  [swap(): return lax.ppermute(x, 'dp', [(0, 1), (1, 0)])]
    pallas_call x2 -> x14, Pallas kernels: 4.66 us -> 83.1 us  [the longest x6 34.7 us: outer(): pl.pallas_call(kernel, grid_spec=pltpu.PrefetchScalarGridSpec(num_scalar_...]
    dot_general x22 -> x0, matrix products: 59.6 us -> none  [dot(): lax.dot_general(a, b, ((contract[:1], contract[1:]), ((), ())), preferred...]
    ppermute x18 -> x9, starting transfers between devices: 59.5 us -> 14.9 us  [shift(): return lax.ppermute(x, 'ctx', [(i, (i + d) % n) for i in range(n)])]
    ppermute x18 -> x9, waiting for transfers between devices: 39.9 us -> 81.5 us  [shift(): return lax.ppermute(x, 'ctx', [(i, (i + d) % n) for i in range(n)])]
    reduce_scatter x0 -> x4, waiting for transfers between devices: none -> 27.2 us  [along_ctx(): return lax.psum_scatter(term, 'ctx', scatter_dimension=0, tiled=True)]
    ppermute x16 -> x7, starting transfers between devices: 32.7 us -> 6.7 us  [swap(): return lax.ppermute(x, 'dp', [(0, 1), (1, 0)])]
    unnamed x50 -> x112, local copies, waits for them, and re-layouts: 2.15 us -> 11.2 us
  transfers between devices with their start and end apart: 50 -> 40, of which waited for: 20 -> 19; matrix products, arithmetic and copies ran while one was open for 17% -> 5% of each run, Pallas kernels for 0% -> 23%
where the time goes in v2:
time: 319 us
  waiting for transfers between devices  157 us (49%)
  Pallas kernels  83.1 us (26%)
  starting transfers between devices  33.8 us (11%)
  local copies, waits for them, and re-layouts  18.2 us (6%)
  between operations  14.4 us (5%)
  other arithmetic  12.2 us (4%)
    ppermute x9, waiting for transfers between devices, shift(): return lax.ppermute(x, 'ctx', [(i, (i + d) % n) for i in range(n)])  81.5 us
    pallas_call x6, Pallas kernels, outer(): pl.pallas_call(kernel, grid_spec=pltpu.PrefetchScalarGridSpec(num_scalar_...  34.7 us
    ppermute x20, waiting for transfers between devices, flip(): return lax.ppermute(x, 'space', [(i, i ^ bit) for i in range(n_space)])  28.1 us
    reduce_scatter x4, waiting for transfers between devices, along_ctx(): return lax.psum_scatter(term, 'ctx', scatter_dimension=0, tiled=True)  27.2 us
    pallas_call x2, Pallas kernels, backproject(): pl.pallas_call(kernel, grid=(model // wide,), in_specs=[pl.BlockSpec((row...  21.2 us
    ppermute x7, waiting for transfers between devices, swap(): return lax.ppermute(x, 'dp', [(0, 1), (1, 0)])  19.9 us
    pallas_call x3, Pallas kernels, project(): pl.pallas_call(kernel, grid=(count,), in_specs=[pl.BlockSpec((size, model...  16.7 us
    ppermute x9, starting transfers between devices, shift(): return lax.ppermute(x, 'ctx', [(i, (i + d) % n) for i in range(n)])  14.9 us
  transfers between devices with their start and end apart: 40, of which 19 were waited for; matrix products, arithmetic and copies ran while one was open for 5% of the time, Pallas kernels for 23%

profile of v2, /device:TPU:0, one launch (start us, length us, event | category | flops | bytes accessed | tf_op | source)
XLA Modules:
  0.0 318.6 jit_solution(11592651613261285383)
XLA Ops:
  16.9 5.9 %collective-permute-done.2 = bf16[1,64,3072]{2,1,0:T(8,128)(2,1)S(1)} collective-permute-done((bf16[1,64,3072]{2,1,0:T(8,128)(2,1)S(1)}, bf16[1,64,3072]{2,1,0:T(8,128)(2,1)S(1)}, u32[]{:S(2)}, u32[]{:S(2)}) %collective-permute-start.2) | collective-permute-done | bytes 393248 | tf_op jit(solution)/shard_map/ppermute | solution.py:286
  22.8 11.6 %collective-permute-done = bf16[64,3072]{1,0:T(8,128)(2,1)S(1)} collective-permute-done((bf16[64,3072]{1,0:T(8,128)(2,1)S(1)}, bf16[64,3072]{1,0:T(8,128)(2,1)S(1)}, u32[]{:S(2)}, u32[]{:S(2)}) %collective-permute-start) | collective-permute-done | bytes 393248 | tf_op jit(solution)/shard_map/ppermute | solution.py:283
  40.5 5.6 %collective-permute-done.7 = bf16[2,1,64,1536]{3,2,1,0:T(8,128)(2,1)S(1)} collective-permute-done((bf16[2,1,64,1536]{3,2,1,0:T(8,128)(2,1)S(1)}, bf16[2,1,64,1536]{3,2,1,0:T(8,128)(2,1)S(1)}, u32[]{:S(2)}, u32[]{:S(2)}) %collective-permute-start.7) | collective-permute-done | bytes 393248 | tf_op jit(solution)/shard_map/ppermute | solution.py:289
  46.1 4.0 %collective-permute-done.4 = bf16[64,3072]{1,0:T(8,128)(2,1)S(1)} collective-permute-done((bf16[64,3072]{1,0:T(8,128)(2,1)}, bf16[64,3072]{1,0:T(8,128)(2,1)S(1)}, u32[]{:S(2)}, u32[]{:S(2)}) %collective-permute-start.4) | collective-permute-done | bytes 393248 | tf_op jit(solution)/shard_map/ppermute | solution.py:283
  50.1 6.3 %collective-permute-done.5 = bf16[64,3072]{1,0:T(8,128)(2,1)S(1)} collective-permute-done((bf16[64,3072]{1,0:T(8,128)(2,1)}, bf16[64,3072]{1,0:T(8,128)(2,1)S(1)}, u32[]{:S(2)}, u32[]{:S(2)}) %collective-permute-start.5) | collective-permute-done | bytes 393248 | tf_op jit(solution)/shard_map/ppermute | solution.py:283
  61.0 7.6 %collective-permute-done.12 = bf16[2,1,64,1536]{3,2,0,1:T(8,128)(2,1)S(1)} collective-permute-done((bf16[2,1,64,1536]{3,2,0,1:T(8,128)(2,1)S(1)}, bf16[2,1,64,1536]{3,2,0,1:T(8,128)(2,1)S(1)}, u32[]{:S(2)}, u32[]{:S(2)}) %collective-permute-start.12) | collective-permute-done | bytes 393248 | tf_op jit(solution)/shard_map/ppermute | solution.py:289
  70.5 8.4 %collective-permute-done.9 = bf16[64,3072]{1,0:T(8,128)(2,1)S(1)} collective-permute-done((bf16[64,3072]{1,0:T(8,128)(2,1)S(1)}, bf16[64,3072]{1,0:T(8,128)(2,1)S(1)}, u32[]{:S(2)}, u32[]{:S(2)}) %collective-permute-start.9) | collective-permute-done | bytes 393248 | tf_op jit(solution)/shard_map/ppermute | solution.py:283
  84.0 13.1 %shard_map.76 = (bf16[1024,384]{1,0:T(8,128)(2,1)S(1)}, bf16[1024,384]{1,0:T(8,128)(2,1)S(1)}, bf16[1024,384]{1,0:T(8,128)(2,1)S(1)}) custom-call(bf16[128,3072]{1,0:T(8,128)(2,1)S(1)} %bitcast.150, bf16[256,3072]{1,0:T(8,128)(2,1)S(1)} %bitcast.118, bf16[128,3072]{1,0:T(8,128)(2,1)S(1)} %bitcast.154, bf16[128,3072]{1,0:T(8,128)(2,1)S(1)} %bitcast.151, ...), custom_call_target="tpu_custom_call" | custom-call | flops 1 | bytes 1 | tf_op jit(solution)/shard_map/pallas_call | solution.py:153
  110.8 3.6 %collective-permute-done.18 = bf16[1,64,3072]{2,1,0:T(8,128)(2,1)S(1)} collective-permute-done((bf16[1,64,3072]{2,1,0:T(8,128)(2,1)S(1)}, bf16[1,64,3072]{2,1,0:T(8,128)(2,1)S(1)}, u32[]{:S(2)}, u32[]{:S(2)}) %collective-permute-start.18) | collective-permute-done | bytes 393248 | tf_op jit(solution)/shard_map/ppermute | solution.py:286
  120.6 4.2 %shard_map.79 = (bf16[4,4,64,384]{3,2,1,0:T(8,128)(2,1)S(1)}, bf16[4,4,64,384]{3,2,1,0:T(8,128)(2,1)S(1)}, bf16[4,4,64,384]{3,2,1,0:T(8,128)(2,1)S(1)}) custom-call(s32[4]{0:T(128)S(1)} %gather_fusion, bf16[4,4,64,384]{3,2,1,0:T(8,128)(2,1)S(1)} %bitcast.179, bf16[4,4,64,384]{3,2,1,0:T(8,128)(2,1)S(1)} %bitcast.181, bf16[4,4,64,384]{3,2,1,0:T(8,128)(2,1)S(1)} %bitcast.183, ...), custom_call_target="tpu_custom_call" | custom-call | flops 1 | bytes 1 | tf_op jit(solution)/shard_map/pallas_call | solution.py:94
  127.5 8.9 %shard_map.80 = (f32[1536,384]{1,0:T(8,128)}, f32[1536,384]{1,0:T(8,128)}, f32[1536,384]{1,0:T(8,128)}) custom-call(s32[1]{0:T(128)} %bitcast.48.column_ref, bf16[128,3072]{1,0:T(8,128)(2,1)} %bitcast.152, bf16[256,3072]{1,0:T(8,128)(2,1)} %bitcast.120, bf16[128,3072]{1,0:T(8,128)(2,1)} %bitcast.156, bf16[128,3072]{1,0:T(8,128)(2,1)} %bitcast.153, ...), custom_call_target="tpu_custom_call" | custom-call | flops 1 | bytes 1 | tf_op jit(solution)/shard_map/pallas_call | solution.py:188
  139.8 4.9 %shard_map.82 = bf16[1536,384]{1,0:T(8,128)(2,1)} custom-call(s32[1]{0:T(128)} %bitcast.52.column_ref, bf16[128,3072]{1,0:T(8,128)(2,1)} %bitcast.124, bf16[256,3072]{1,0:T(8,128)(2,1)} %bitcast.108, bf16[128,3072]{1,0:T(8,128)(2,1)} %bitcast.130, bf16[128,3072]{1,0:T(8,128)(2,1)} %bitcast.125, bf16[256,3072]{1,0:T(8,128)(2,1)} %bitcast.109, ...), custom_call_target="tpu_custom_call" | custom-call | flops 1 | bytes 1 | tf_op jit(solution)/shard_map/pallas_call | solution.py:188
  146.6 5.3 %shard_map.83 = bf16[1536,384]{1,0:T(8,128)(2,1)} custom-call(s32[1]{0:T(128)} %constant.68.clone.1.column_ref, bf16[128,1536]{1,0:T(8,128)(2,1)} %bitcast.193, bf16[256,1536]{1,0:T(8,128)(2,1)} %bitcast.187, bf16[128,1536]{1,0:T(8,128)(2,1)} %bitcast.199, bf16[128,1536]{1,0:T(8,128)(2,1)} %bitcast.194, bf16[256,1536]{1,0:T(8,128)(2,1)} %bitcast.188, ...), custom_call_target="tpu_custom_call" | custom-call | flops 1 | bytes 1 | tf_op jit(solution)/shard_map/pallas_call | solution.py:188
  155.3 10.6 %shard_map.84 = (bf16[64,3072]{1,0:T(8,128)(2,1)}, bf16[128,3072]{1,0:T(8,128)(2,1)}, bf16[64,3072]{1,0:T(8,128)(2,1)}) custom-call(bf16[1024,384]{1,0:T(8,128)(2,1)} %bitcast.170, bf16[1024,384]{1,0:T(8,128)(2,1)} %bitcast.173, bf16[1024,384]{1,0:T(8,128)(2,1)} %bitcast.167, bf16[512,384]{1,0:T(8,128)(2,1)} %bitcast.234, bf16[512,384]{1,0:T(8,128)(2,1)} %bitcast.233, ...), custom_call_target="tpu_custom_call" | custom-call | flops 1 | bytes 1 | tf_op jit(solution)/shard_map/pallas_call | solution.py:222
  166.0 4.8 %collective-permute-done.27 = bf16[4,4,64,384]{3,2,1,0:T(8,128)(2,1)S(1)} collective-permute-done((bf16[4,4,64,384]{3,2,1,0:T(8,128)(2,1)S(1)}, bf16[4,4,64,384]{3,2,1,0:T(8,128)(2,1)S(1)}, u32[]{:S(2)}, u32[]{:S(2)}) %collective-permute-start.27) | collective-permute-done | bytes 786464 | tf_op jit(solution)/shard_map/ppermute | solution.py:289
  171.7 5.3 %shard_map.85 = bf16[1536,384]{1,0:T(8,128)(2,1)} custom-call(s32[1]{0:T(128)} %constant.68.clone.1.column_ref, bf16[128,1536]{1,0:T(8,128)(2,1)} %bitcast.195, bf16[256,1536]{1,0:T(8,128)(2,1)} %bitcast.189, bf16[128,1536]{1,0:T(8,128)(2,1)} %bitcast.201, bf16[128,1536]{1,0:T(8,128)(2,1)} %bitcast.196, bf16[256,1536]{1,0:T(8,128)(2,1)} %bitcast.190, ...), custom_call_target="tpu_custom_call" | custom-call | flops 1 | bytes 1 | tf_op jit(solution)/shard_map/pallas_call | solution.py:188
  184.6 10.6 %shard_map.86 = (bf16[64,3072]{1,0:T(8,128)(2,1)}, bf16[64,3072]{1,0:T(8,128)(2,1)}, bf16[64,3072]{1,0:T(8,128)(2,1)}, bf16[64,3072]{1,0:T(8,128)(2,1)}) custom-call(bf16[1024,384]{1,0:T(8,128)(2,1)} %bitcast.171, bf16[1024,384]{1,0:T(8,128)(2,1)} %bitcast.174, bf16[1024,384]{1,0:T(8,128)(2,1)} %bitcast.168, bf16[512,384]{1,0:T(8,128)(2,1)} %bitcast.230, ...), custom_call_target="tpu_custom_call" | custom-call | flops 1 | bytes 1 | tf_op jit(solution)/shard_map/pallas_call | solution.py:222
  195.2 14.5 %collective-permute-done.29 = bf16[64,3072]{1,0:T(8,128)(2,1)S(1)} collective-permute-done((bf16[64,3072]{1,0:T(8,128)(2,1)}, bf16[64,3072]{1,0:T(8,128)(2,1)S(1)}, u32[]{:S(2)}, u32[]{:S(2)}) %collective-permute-start.29) | collective-permute-done | bytes 393248 | tf_op jit(solution)/shard_map/ppermute | solution.py:286
  211.5 5.3 %shard_map.87 = bf16[1536,384]{1,0:T(8,128)(2,1)} custom-call(s32[1]{0:T(128)} %constant.68.clone.1.column_ref, bf16[128,1536]{1,0:T(8,128)(2,1)} %bitcast.197, bf16[256,1536]{1,0:T(8,128)(2,1)} %bitcast.191, bf16[128,1536]{1,0:T(8,128)(2,1)} %bitcast.203, bf16[128,1536]{1,0:T(8,128)(2,1)} %bitcast.198, bf16[256,1536]{1,0:T(8,128)(2,1)} %bitcast.192, ...), custom_call_target="tpu_custom_call" | custom-call | flops 1 | bytes 1 | tf_op jit(solution)/shard_map/pallas_call | solution.py:188
  217.8 5.2 %shard_map.88 = f32[1536,384]{1,0:T(8,128)} custom-call(s32[1]{0:T(128)} %bitcast.48.column_ref, bf16[128,3072]{1,0:T(8,128)(2,1)} %bitcast.126, bf16[256,3072]{1,0:T(8,128)(2,1)} %bitcast.110, bf16[128,3072]{1,0:T(8,128)(2,1)} %bitcast.132, bf16[128,3072]{1,0:T(8,128)(2,1)} %bitcast.127, bf16[256,3072]{1,0:T(8,128)(2,1)} %bitcast.111, ...), custom_call_target="tpu_custom_call" | custom-call | flops 1 | bytes 1 | tf_op jit(solution)/shard_map/pallas_call | solution.py:188
  225.2 32.3 %collective-permute-done.33.refs_2_ = bf16[64,3072]{1,0:T(8,128)(2,1)S(1)} collective-permute-done((bf16[64,3072]{1,0:T(8,128)(2,1)}, bf16[64,3072]{1,0:T(8,128)(2,1)S(1)}, u32[]{:S(2)}, u32[]{:S(2)}) %collective-permute-start.33) | collective-permute-done | bytes 393248 | tf_op jit(solution)/shard_map/ppermute | solution.py:283
  264.0 13.4 %collective-permute-done.34.refs_1_ = bf16[64,3072]{1,0:T(8,128)(2,1)S(1)} collective-permute-done((bf16[64,3072]{1,0:T(8,128)(2,1)}, bf16[64,3072]{1,0:T(8,128)(2,1)S(1)}, u32[]{:S(2)}, u32[]{:S(2)}) %collective-permute-start.34) | collective-permute-done | bytes 393248 | tf_op jit(solution)/shard_map/ppermute | solution.py:283
  278.9 3.7 %shard_map.89 = bf16[4,64,3072]{2,1,0:T(8,128)(2,1)} custom-call(s32[4]{0:T(128)} %compare_select_fusion.3.where_ref, bf16[64,3072]{1,0:T(8,128)(2,1)} %add_convert_fusion.1.refs_0_, bf16[64,3072]{1,0:T(8,128)(2,1)} %copy-done.52, bf16[64,3072]{1,0:T(8,128)(2,1)} %copy-done.51, bf16[64,3072]{1,0:T(8,128)(2,1)} %copy-done.53), custom_call_target="tpu_custom_call" | custom-call | flops 1 | bytes 1 | tf_op jit(solution)/shard_map/pallas_call | solution.py:245
  285.0 25.2 %reduce-scatter.11.cloned.1.call-done = bf16[384,384]{1,0:T(8,128)(2,1)} async-done(((bf16[1536,384]{1,0:T(8,128)(2,1)}), bf16[384,384]{1,0:T(8,128)(2,1)}) %reduce-scatter.11.cloned.1.call-update) | async-done | bytes 294928 | tf_op jit(solution)/shard_map/reduce_scatter | solution.py:371
  (213 shorter events, 84.1 us)
Async XLA Ops:
  7.2 171.8 %reduce-scatter.5.cloned.1.call-start = ((), (), s32[]{:S(2)}) async-start(), calls=%async_computation.4 | async-start | bytes 1474560 | tf_op jit(solution)/shard_map/reduce_scatter | solution.py:371
  7.2 27.1 %collective-permute-start.3 = (bf16[3,3072,384]{2,1,0:T(8,128)(2,1)}, bf16[3,3072,384]{2,1,0:T(8,128)(2,1)}, u32[]{:S(2)}, u32[]{:S(2)}) collective-permute-start(bf16[3,3072,384]{2,1,0:T(8,128)(2,1)} %refs_6_.1), channel_id=1, source_target_pairs={{0,1},{1,0},{2,3},{3,2},{4,5},{5,4},{6,7},{7,6},{8,9},{9,8},{10,11... | collective-permute-start | bytes 21233672 | tf_op jit(solution)/shard_map/ppermute | solution.py:286
  13.8 20.5 %collective-permute-start = (bf16[64,3072]{1,0:T(8,128)(2,1)S(1)}, bf16[64,3072]{1,0:T(8,128)(2,1)S(1)}, u32[]{:S(2)}, u32[]{:S(2)}) collective-permute-start(bf16[64,3072]{1,0:T(8,128)(2,1)S(1)} %get-tuple-element.265), channel_id=1, source_target_pairs={{0,8},{4,12},{8,0},{12,4},{1,9},{5,13},{9,1},{13,5},{2,10},{6,14},... | collective-permute-start | bytes 1179656 | tf_op jit(solution)/shard_map/ppermute | solution.py:283
  34.4 22.0 %collective-permute-start.8 = (bf16[2,1,64,3072]{3,2,1,0:T(8,128)(2,1)S(1)}, bf16[2,1,64,3072]{3,2,1,0:T(8,128)(2,1)S(1)}, u32[]{:S(2)}, u32[]{:S(2)}) collective-permute-start(bf16[2,1,64,3072]{3,2,1,0:T(8,128)(2,1)S(1)} %pad_maximum_fusion.3), channel_id=1, source_target_pairs={{0,1},{1,0},{2,3},{3,2},{4,5},{5,4},{6,7},{7,6},{8,9},{9,8},{10,11... | collective-permute-start | bytes 2359304 | tf_op jit(solution)/shard_map/ppermute | solution.py:286
  36.8 19.6 %collective-permute-start.5 = (bf16[64,3072]{1,0:T(8,128)(2,1)}, bf16[64,3072]{1,0:T(8,128)(2,1)S(1)}, u32[]{:S(2)}, u32[]{:S(2)}) collective-permute-start(bf16[64,3072]{1,0:T(8,128)(2,1)} %get-tuple-element.129), channel_id=1, source_target_pairs={{0,12},{4,0},{8,4},{12,8},{1,13},{5,1},{9,5},{13,9},{2,14},{6,2},{... | collective-permute-start | bytes 1179656 | tf_op jit(solution)/shard_map/ppermute | solution.py:283
  56.5 22.5 %collective-permute-start.13 = (bf16[2,1,64,3072]{3,2,0,1:T(8,128)(2,1)S(1)}, bf16[2,1,64,3072]{3,2,0,1:T(8,128)(2,1)S(1)}, u32[]{:S(2)}, u32[]{:S(2)}) collective-permute-start(bf16[2,1,64,3072]{3,2,0,1:T(8,128)(2,1)S(1)} %pad_maximum_fusion.4), channel_id=1, source_target_pairs={{0,1},{1,0},{2,3},{3,2},{4,5},{5,4},{6,7},{7,6},{8,9},{9,8},{10,11... | collective-permute-start | bytes 2359304 | tf_op jit(solution)/shard_map/ppermute | solution.py:286
  56.7 22.3 %collective-permute-start.11 = (bf16[2,64,3072]{2,1,0:T(8,128)(2,1)S(1)}, bf16[2,64,3072]{2,1,0:T(8,128)(2,1)S(1)}, u32[]{:S(2)}, u32[]{:S(2)}) collective-permute-start(bf16[2,64,3072]{2,1,0:T(8,128)(2,1)S(1)} %get-tuple-element.278), channel_id=1, source_target_pairs={{0,2},{1,3},{2,0},{3,1},{4,6},{5,7},{6,4},{7,5},{8,10},{9,11},{10,... | collective-permute-start | bytes 2359304 | tf_op jit(solution)/shard_map/ppermute | solution.py:286
  79.3 23.3 %collective-permute-start.16 = (bf16[2,2,64,1536]{3,2,1,0:T(8,128)(2,1)S(1)}, bf16[2,2,64,1536]{3,2,1,0:T(8,128)(2,1)S(1)}, u32[]{:S(2)}, u32[]{:S(2)}) collective-permute-start(bf16[2,2,64,1536]{3,2,1,0:T(8,128)(2,1)S(1)} %fusion), channel_id=1, source_target_pairs={{0,16},{16,0},{1,17},{17,1},{2,18},{18,2},{3,19},{19,3},{4,20},{20... | collective-permute-start | bytes 2359304 | tf_op jit(solution)/shard_map/ppermute | solution.py:289
  80.7 21.9 %collective-permute-start.15 = (bf16[2,64,3072]{2,1,0:T(8,128)(2,1)S(1)}, bf16[2,64,3072]{2,1,0:T(8,128)(2,1)S(1)}, u32[]{:S(2)}, u32[]{:S(2)}) collective-permute-start(bf16[2,64,3072]{2,1,0:T(8,128)(2,1)S(1)} %get-tuple-element.276), channel_id=1, source_target_pairs={{0,2},{1,3},{2,0},{3,1},{4,6},{5,7},{6,4},{7,5},{8,10},{9,11},{10,... | collective-permute-start | bytes 2359304 | tf_op jit(solution)/shard_map/ppermute | solution.py:286
  82.3 20.3 %collective-permute-start.14 = (bf16[64,3072]{1,0:T(8,128)(2,1)S(1)}, bf16[64,3072]{1,0:T(8,128)(2,1)S(1)}, u32[]{:S(2)}, u32[]{:S(2)}) collective-permute-start(bf16[64,3072]{1,0:T(8,128)(2,1)S(1)} %copy-done.48), channel_id=1, source_target_pairs={{0,8},{4,12},{8,0},{12,4},{1,9},{5,13},{9,1},{13,5},{2,10},{6,14},... | collective-permute-start | bytes 1179656 | tf_op jit(solution)/shard_map/ppermute | solution.py:283
  126.4 20.2 %collective-permute-start.25 = (bf16[3,2,4,64,384]{4,3,2,1,0:T(8,128)(2,1)}, bf16[3,2,4,64,384]{4,3,2,1,0:T(8,128)(2,1)}, u32[]{:S(2)}, u32[]{:S(2)}) collective-permute-start(bf16[3,2,4,64,384]{4,3,2,1,0:T(8,128)(2,1)} %pad_maximum_fusion.2), channel_id=1, source_target_pairs={{0,1},{1,0},{2,3},{3,2},{4,5},{5,4},{6,7},{7,6},{8,9},{9,8},{10,11... | collective-permute-start | bytes 3538952 | tf_op jit(solution)/shard_map/ppermute | solution.py:286
  126.6 18.2 %collective-permute-start.26 = (bf16[2,2,64,1536]{3,2,1,0:T(8,128)(2,1)S(1)}, bf16[2,2,64,1536]{3,2,1,0:T(8,128)(2,1)}, u32[]{:S(2)}, u32[]{:S(2)}) collective-permute-start(bf16[2,2,64,1536]{3,2,1,0:T(8,128)(2,1)S(1)} %collective-permute-done.16), channel_id=1, source_target_pairs={{0,1},{1,0},{2,3},{3,2},{4,5},{5,4},{6,7},{7,6},{8,9},{9,8},{10,11... | collective-permute-start | bytes 2359304 | tf_op jit(solution)/shard_map/ppermute | solution.py:286
  126.9 19.7 %collective-permute-start.24 = (bf16[4,4,64,384]{3,2,1,0:T(8,128)(2,1)S(1)}, bf16[4,4,64,384]{3,2,1,0:T(8,128)(2,1)}, u32[]{:S(2)}, u32[]{:S(2)}) collective-permute-start(bf16[4,4,64,384]{3,2,1,0:T(8,128)(2,1)S(1)} %get-tuple-element.214), channel_id=1, source_target_pairs={{0,16},{16,0},{1,17},{17,1},{2,18},{18,2},{3,19},{19,3},{4,20},{20... | collective-permute-start | bytes 2359304 | tf_op jit(solution)/shard_map/ppermute | solution.py:289
  151.9 64.9 %reduce-scatter.7.cloned.1.call-start = ((), (), s32[]{:S(2)}) async-start(), calls=%async_computation.5 | async-start | bytes 1474560 | tf_op jit(solution)/shard_map/reduce_scatter | solution.py:371
  152.0 18.8 %collective-permute-start.27 = (bf16[4,4,64,384]{3,2,1,0:T(8,128)(2,1)S(1)}, bf16[4,4,64,384]{3,2,1,0:T(8,128)(2,1)S(1)}, u32[]{:S(2)}, u32[]{:S(2)}) collective-permute-start(bf16[4,4,64,384]{3,2,1,0:T(8,128)(2,1)S(1)} %copy-done.16), channel_id=1, source_target_pairs={{0,16},{16,0},{1,17},{17,1},{2,18},{18,2},{3,19},{19,3},{4,20},{20... | collective-permute-start | bytes 2359304 | tf_op jit(solution)/shard_map/ppermute | solution.py:289
  179.0 103.7 %reduce-scatter.9.cloned.1.call-start = ((), (), s32[]{:S(2)}) async-start(), calls=%async_computation.6 | async-start | bytes 1474560 | tf_op jit(solution)/shard_map/reduce_scatter | solution.py:371
  179.0 30.6 %collective-permute-start.28 = (bf16[4,4,64,384]{3,2,1,0:T(8,128)(2,1)S(1)}, bf16[4,4,64,384]{3,2,1,0:T(8,128)(2,1)S(1)}, u32[]{:S(2)}, u32[]{:S(2)}) collective-permute-start(bf16[4,4,64,384]{3,2,1,0:T(8,128)(2,1)S(1)} %copy-done.13), channel_id=1, source_target_pairs={{0,16},{16,0},{1,17},{17,1},{2,18},{18,2},{3,19},{19,3},{4,20},{20... | collective-permute-start | bytes 2359304 | tf_op jit(solution)/shard_map/ppermute | solution.py:289
  180.6 29.1 %collective-permute-start.30 = (bf16[128,3072]{1,0:T(8,128)(2,1)}, bf16[128,3072]{1,0:T(8,128)(2,1)S(1)}, u32[]{:S(2)}, u32[]{:S(2)}) collective-permute-start(bf16[128,3072]{1,0:T(8,128)(2,1)} %get-tuple-element.209), channel_id=1, source_target_pairs={{0,2},{1,3},{2,0},{3,1},{4,6},{5,7},{6,4},{7,5},{8,10},{9,11},{10,... | collective-permute-start | bytes 2359304 | tf_op jit(solution)/shard_map/ppermute | solution.py:286
  182.0 27.6 %collective-permute-start.29 = (bf16[64,3072]{1,0:T(8,128)(2,1)}, bf16[64,3072]{1,0:T(8,128)(2,1)S(1)}, u32[]{:S(2)}, u32[]{:S(2)}) collective-permute-start(bf16[64,3072]{1,0:T(8,128)(2,1)} %get-tuple-element.208), channel_id=1, source_target_pairs={{0,2},{1,3},{2,0},{3,1},{4,6},{5,7},{6,4},{7,5},{8,10},{9,11},{10,... | collective-permute-start | bytes 1179656 | tf_op jit(solution)/shard_map/ppermute | solution.py:286
  183.1 42.0 %collective-permute-start.32 = (bf16[64,3072]{1,0:T(8,128)(2,1)}, bf16[64,3072]{1,0:T(8,128)(2,1)}, u32[]{:S(2)}, u32[]{:S(2)}) collective-permute-start(bf16[64,3072]{1,0:T(8,128)(2,1)} %get-tuple-element.232), channel_id=1, source_target_pairs={{0,2},{1,3},{2,0},{3,1},{4,6},{5,7},{6,4},{7,5},{8,10},{9,11},{10,... | collective-permute-start | bytes 1179656 | tf_op jit(solution)/shard_map/ppermute | solution.py:286
  210.9 46.6 %collective-permute-start.31 = (bf16[1536,384]{1,0:T(8,128)(2,1)S(1)}, bf16[1536,384]{1,0:T(8,128)(2,1)S(1)}, u32[]{:S(2)}, u32[]{:S(2)}) collective-permute-start(bf16[1536,384]{1,0:T(8,128)(2,1)S(1)} %copy-done.38), channel_id=1, source_target_pairs={{0,16},{16,0},{1,17},{17,1},{2,18},{18,2},{3,19},{19,3},{4,20},{20... | collective-permute-start | bytes 3538952 | tf_op jit(solution)/shard_map/ppermute | solution.py:289
  216.8 93.4 %reduce-scatter.11.cloned.1.call-start = ((), (), s32[]{:S(2)}) async-start(), calls=%async_computation.7 | async-start | bytes 1474560 | tf_op jit(solution)/shard_map/reduce_scatter | solution.py:371
  222.9 34.6 %collective-permute-start.33 = (bf16[64,3072]{1,0:T(8,128)(2,1)}, bf16[64,3072]{1,0:T(8,128)(2,1)S(1)}, u32[]{:S(2)}, u32[]{:S(2)}) collective-permute-start(bf16[64,3072]{1,0:T(8,128)(2,1)} %add_convert_fusion.4), channel_id=1, source_target_pairs={{0,8},{4,12},{8,0},{12,4},{1,9},{5,13},{9,1},{13,5},{2,10},{6,14},... | collective-permute-start | bytes 1179656 | tf_op jit(solution)/shard_map/ppermute | solution.py:283
  258.2 19.2 %collective-permute-start.34 = (bf16[64,3072]{1,0:T(8,128)(2,1)}, bf16[64,3072]{1,0:T(8,128)(2,1)S(1)}, u32[]{:S(2)}, u32[]{:S(2)}) collective-permute-start(bf16[64,3072]{1,0:T(8,128)(2,1)} %get-tuple-element.244), channel_id=1, source_target_pairs={{0,12},{4,0},{8,4},{12,8},{1,13},{5,1},{9,5},{13,9},{2,14},{6,2},{... | collective-permute-start | bytes 1179656 | tf_op jit(solution)/shard_map/ppermute | solution.py:283
  (72 other events, 729.6 us)
Sparse Core Ops, SparseCore 0:
  152.0 26.8 reduce-scatter.4
  181.9 27.8 reduce-scatter.6
  217.0 40.3 reduce-scatter.8
  282.8 27.3 reduce-scatter.10

commit v3 on v2

--- a/solution.py
+++ b/solution.py
@@ -15,8 +15,7 @@
 
 
 FREE = pl.CostEstimate(flops=1, bytes_accessed=1, transcendentals=0)
-PARAMS = pltpu.CompilerParams(vmem_limit_bytes=60 * 1024 * 1024)
-SMALL = pltpu.CompilerParams(vmem_limit_bytes=40 * 1024 * 1024)
+MIB = 1024 * 1024
 
 
 def softmax_row(q, keys):
@@ -48,7 +47,7 @@
             att_ref[0, slots[f], :, cols] = weighted(probs_b, v).astype(BF16)
 
 
-def backward_kernel(frames, heads, slot_ref, q_ref, k_ref, v_ref, near_ref, far_ref, dq_ref, dk_ref, dv_ref):
+def backward_kernel(frames, heads, slot_ref, q_ref, k_ref, v_ref, near_ref, far_ref, dq_ref, dk_ref, dv_ref, give_ref):
     slots = [slot_ref[f] for f in range(frames)]
     for h in range(heads):
         cols = pl.ds(h * HS, HS)
@@ -74,33 +73,42 @@
             inner = weighted(probs, dprobs)
             dscores = rounded([p * (d - inner) for p, d in zip(probs, dprobs)])
             dq = weighted(dscores, k)
-            dq_ref[0, slots[f], :, cols] = (dq * SCALE).astype(BF16)
+            dq_ref[0, slots[f], :, cols] = give_ref[0, 0, slots[f], :, cols] = (dq * SCALE).astype(BF16)
             for g in range(f + 1):
                 add_k, add_v = dscores[g] * q[f], probs_b[g] * o[f]
                 dk[g] = add_k if dk[g] is None else dk[g] + add_k
                 dv[g] = add_v if dv[g] is None else dv[g] + add_v
         for g in range(frames):
-            dk_ref[0, slots[g], :, cols] = (dk[g] * SCALE).astype(BF16)
-            dv_ref[0, slots[g], :, cols] = dv[g].astype(BF16)
-
-
-def per_group(kernel, slots, args, count):
+            dk_ref[0, slots[g], :, cols] = give_ref[1, 0, slots[g], :, cols] = (dk[g] * SCALE).astype(BF16)
+            dv_ref[0, slots[g], :, cols] = give_ref[2, 0, slots[g], :, cols] = dv[g].astype(BF16)
+
+
+def per_group(kernel, slots, args, backward):
     groups, frames, patches, width = args[0].shape
-
     def block(shape):
         return pl.BlockSpec((1,) + shape[1:], lambda i, slot_ref: (i, 0, 0, 0))
 
     out = jax.ShapeDtypeStruct(args[0].shape, BF16)
+    count = 3 if backward else 1
+    outs, specs = [out] * count, [block(out.shape)] * count
+    if backward:
+        half = groups // 2
+        outs.append(jax.ShapeDtypeStruct((3, half) + out.shape[1:], BF16))
+        specs.append(
+            pl.BlockSpec(
+                (3, 1) + out.shape[1:], lambda i, slot_ref: (0, jnp.maximum(i - half, 0), 0, 0, 0)
+            )
+        )
     return pl.pallas_call(
         functools.partial(kernel, frames, width // HS),
         grid_spec=pltpu.PrefetchScalarGridSpec(
             num_scalar_prefetch=1,
             grid=(groups,),
             in_specs=[block(a.shape) for a in args],
-            out_specs=[block(out.shape)] * count,
+            out_specs=specs,
         ),
-        out_shape=[out] * count,
-        compiler_params=SMALL,
+        out_shape=outs,
+        compiler_params=pltpu.CompilerParams(vmem_limit_bytes=12 * MIB),
         cost_estimate=FREE,
     )(slots, *args)
 
@@ -118,15 +126,15 @@
 
 def in_order(sets):
     pieces = []
-    for e in range(2 * len(sets[0])):
+    for e in range(len(sets[0])):
         for held in sets:
-            array = held[e // 2]
+            array, block = held[e]
             size = array.shape[1] * array.shape[2]
-            pieces.append((array.reshape(-1, array.shape[-1]), size, e % 2))
+            pieces.append((array.reshape(-1, array.shape[-1]), size, block))
     return pieces
 
 
-def project(sets, weights):
+def project(sets, weights, grant=28):
     pieces = in_order(sets)
     count, model, width = weights.shape
     total = sum(size for _, size, _ in pieces)
@@ -153,38 +161,63 @@
     outs = pl.pallas_call(
         kernel,
         grid=(count,),
-        in_specs=[pl.BlockSpec((size, model), lambda i, at=at: (at, 0)) for _, size, at in pieces]
+        in_specs=[
+            pl.BlockSpec((size, model), lambda i, at=at: (at, 0), pipeline_mode=pl.Buffered(1))
+            for _, size, at in pieces
+        ]
         + [pl.BlockSpec((1, model, width), lambda i: (i, 0, 0))],
         out_specs=[pl.BlockSpec(out.shape, lambda i: (0, 0))] * count,
         out_shape=[out] * count,
         scratch_shapes=[pltpu.VMEM((total, model), BF16)],
-        compiler_params=SMALL,
+        compiler_params=pltpu.CompilerParams(vmem_limit_bytes=grant * MIB),
         cost_estimate=FREE,
     )(*[array for array, _, _ in pieces], weights)
-    rows = sets[0][0].shape[2]
-    return [o.reshape(2 * len(sets[0]), -1, rows, width) for o in outs]
-
-
-def outer(sets, grads, column, share, dtype, plus=None):
+    rows = sets[0][0][0].shape[2]
+    return [o.reshape(len(sets[0]), -1, rows, width) for o in outs]
+
+
+def outer(sets, grads, column, share, dtype, plus=None, window=None, also=None):
     pieces = in_order(sets)
-    width = grads[0].shape[-1]
+    more = in_order(also[0]) if also else []
+    width = grads[0][0].shape[-1]
     count = len(grads)
+    tall = sum(size for _, size, _ in pieces)
     wide = block_of(share, 768)
     steps = share // wide
     extra = [] if plus is None else [plus]
-
-    def kernel(column_ref, *refs):
+    shards, start = window or (1, 0)
+    high = share // shards
+    inside = wide // high
+
+    def kernel(scalars_ref, *refs):
         x = jnp.concatenate([ref[...] for ref in refs[: len(pieces)]], 0)
-        grad_refs = refs[len(pieces) : len(pieces) + count]
-        for grad_ref, out_ref in zip(grad_refs, refs[-count:]):
+        refs = refs[len(pieces) :]
+        if also:
+            x_more = jnp.concatenate([ref[...] for ref in refs[: len(more)]], 0)
+            more_ref, refs = refs[len(more)], refs[len(more) + 1 :]
+        grad_refs, out_refs = refs[:count], refs[count + len(extra) :]
+        for grad_ref, out_ref in zip(grad_refs, out_refs):
             total = mxu(x, grad_ref[...], (0, 0))
+            if also:
+                total = total + mxu(x_more, more_ref[...], (0, 0))
             if extra:
-                total = total + refs[len(pieces) + count][...]
-            out_ref[...] = total.astype(dtype)
-
-    grads = [g.reshape(-1, width) for g in grads]
+                total = total + refs[count][...]
+            total = total.astype(dtype)
+            out_ref[...] = total
+            if window:
+                for j in range(inside):
+                    at = pl.program_id(0) * inside + j - scalars_ref[1]
+
+                    @pl.when((at >= 0) & (at < shards - 1))
+                    def _():
+                        out_refs[1][at] = total[j * high : (j + 1) * high]
+
     out = jax.ShapeDtypeStruct((share, width), dtype)
     tile = pl.BlockSpec((wide, width), lambda i, c: (i, 0))
+    outs, specs = [out] * count, [tile] * count
+    if window:
+        outs.append(jax.ShapeDtypeStruct((shards - 1, high, width), dtype))
+        specs.append(pl.BlockSpec(outs[-1].shape, lambda i, c: (0, 0, 0)))
     return pl.pallas_call(
         kernel,
         grid_spec=pltpu.PrefetchScalarGridSpec(
@@ -194,26 +227,39 @@
                 pl.BlockSpec((size, wide), lambda i, c, at=at: (at, c[0] * steps + i))
                 for _, size, at in pieces
             ]
-            + [pl.BlockSpec(g.shape, lambda i, c: (0, 0)) for g in grads]
+            + [
+                pl.BlockSpec((size, wide), lambda i, c, at=at: (at, c[2] * steps + i))
+                for _, size, at in more
+            ]
+            + [pl.BlockSpec((tall, width), lambda i, c: (also[1][1], 0))] * bool(also)
+            + [pl.BlockSpec((tall, width), lambda i, c, at=at: (at, 0)) for _, at in grads]
             + [tile] * len(extra),
-            out_specs=[tile] * count,
+            out_specs=specs,
         ),
-        out_shape=[out] * count,
-        compiler_params=PARAMS,
+        out_shape=outs,
+        compiler_params=pltpu.CompilerParams(vmem_limit_bytes=58 * MIB),
         cost_estimate=FREE,
-    )(jnp.asarray(column, jnp.int32).reshape(1), *[array for array, _, _ in pieces], *grads, *extra)
-
-
-def backproject(grads, block, rows, weights, splits=None):
-    _, model, width = weights[0].shape
+    )(
+        jnp.stack([jnp.asarray(x, jnp.int32) for x in (column, start, also[2] if also else 0)]),
+        *[array for array, _, _ in pieces],
+        *[array for array, _, _ in more],
+        *([also[1][0].reshape(-1, width)] if also else []),
+        *[g.reshape(-1, width) for g, _ in grads],
+        *extra,
+    )
+
+
+def backproject(grads, more, block, rows, weights, splits):
+    count, model, width = weights[0].shape
     wide = block_of(model, 512)
-    splits = splits or [rows]
-    count = len(grads)
+    halves = more.size // (count * width * rows) * 2
 
     def kernel(*refs):
-        w_refs, out_refs = refs[count : count + len(weights)], refs[-len(splits) :]
-        matrices = [w_ref[s] for w_ref in w_refs for s in range(w_ref.shape[0])]
-        total = sum(mxu(ref[...], w, (1, 1)) for ref, w in zip(refs[:count], matrices))
+        more_ref, w_refs, out_refs = refs[count], refs[count + 1 : count + 3], refs[count + 3 :]
+        total = sum(
+            mxu(refs[s][...], w_refs[0][s], (1, 1)) + mxu(more_ref[s], w_refs[1][s], (1, 1))
+            for s in range(count)
+        )
         row = 0
         for size, out_ref in zip(splits, out_refs):
             out_ref[...] = total[row : row + size].astype(BF16)
@@ -222,13 +268,14 @@
     return pl.pallas_call(
         kernel,
         grid=(model // wide,),
-        in_specs=[pl.BlockSpec((rows, width), lambda i: (block, 0))] * count
-        + [pl.BlockSpec((w.shape[0], wide, width), lambda i: (0, i, 0)) for w in weights],
+        in_specs=[pl.BlockSpec((rows, width), lambda i, at=at: (halves * at + block, 0)) for _, at in grads]
+        + [pl.BlockSpec((count, rows, width), lambda i: (0, block, 0))]
+        + [pl.BlockSpec((count, wide, width), lambda i: (0, i, 0))] * 2,
         out_specs=[pl.BlockSpec((size, wide), lambda i: (0, i)) for size in splits],
         out_shape=[jax.ShapeDtypeStruct((size, model), BF16) for size in splits],
-        compiler_params=PARAMS,
+        compiler_params=pltpu.CompilerParams(vmem_limit_bytes=58 * MIB),
         cost_estimate=FREE,
-    )(*[g.reshape(-1, width) for g in grads], *weights)
+    )(*[g.reshape(-1, width) for g, _ in grads], more.reshape(count, -1, width), *weights)
 
 
 def placed_at(pieces, where):
@@ -251,17 +298,56 @@
             out_specs=pl.BlockSpec((1,) + shape, lambda i, w: (w[i], 0, 0)),
         ),
         out_shape=jax.ShapeDtypeStruct((count,) + shape, pieces[0].dtype),
-        compiler_params=PARAMS,
+        compiler_params=pltpu.CompilerParams(vmem_limit_bytes=6 * MIB),
         cost_estimate=FREE,
     )(where, *pieces)
 
 
+def finished(chains, at):
+    arrays = [x for chain in chains for x in chain]
+    _, rows, width = arrays[0].shape
+
+    def kernel(at_ref, *refs):
+        i = 0
+        for c, chain in enumerate(chains):
+            refs[-1][c] = sum(ref[0].astype(F32) for ref in refs[i : i + len(chain)])
+            i += len(chain)
+
+    return pl.pallas_call(
+        kernel,
+        grid_spec=pltpu.PrefetchScalarGridSpec(
+            num_scalar_prefetch=1,
+            grid=(1,),
+            in_specs=[
+                pl.BlockSpec((1, rows, width), lambda i, at_ref, j=j: (at_ref[j], 0, 0))
+                for j in range(len(arrays))
+            ],
+            out_specs=pl.BlockSpec((len(chains), rows, width), lambda i, at_ref: (0, 0, 0)),
+        ),
+        out_shape=jax.ShapeDtypeStruct((len(chains), rows, width), F32),
+        compiler_params=pltpu.CompilerParams(vmem_limit_bytes=60 * MIB),
+        cost_estimate=FREE,
+    )(jnp.stack(at).astype(jnp.int32), *arrays)
+
+
 def tie(x, *first):
     return lax.optimization_barrier((x, *first))[0]
 
 
+def paced(x):
+    mark = pl.pallas_call(
+        lambda x_ref, out_ref: out_ref.__setitem__(..., jnp.zeros_like(out_ref)),
+        in_specs=[pl.BlockSpec(memory_space=pl.ANY)],
+        out_shape=jax.ShapeDtypeStruct((8, 128), F32),
+        cost_estimate=pl.CostEstimate(flops=20 * 10**9, bytes_accessed=1, transcendentals=0),
+    )(x)
+    return tie(x, mark)
+
+
 def tie_all(*x):
-    return lax.optimization_barrier(x)
+    leaves, tree = jax.tree.flatten(x)
+    arrays = iter(lax.optimization_barrier([y for y in leaves if not isinstance(y, int)]))
+    return jax.tree.unflatten(tree, [y if isinstance(y, int) else next(arrays) for y in leaves])
 
 
 def body(sizes, inputs, upstream, qkv_weight, out_weight):
@@ -292,11 +378,11 @@
         x = x.reshape(n, rows, model)
         return lax.dynamic_index_in_dim(x, lax.rem(me + d, n), 0, keepdims=False)
 
-    def spread(held):
-        held = [held]
+    def spread(*held):
+        held = list(held)
         for bit in bits[1:]:
             held = held + [flip(h, bit) for h in held]
-        return held
+        return [(h, block) for h in held for block in range(h.shape[0])]
 
     share = model // n_dp
 
@@ -355,76 +441,127 @@
     here_bu = jnp.stack(near_bu)
     there_bu = flip(here_bu, bits[0])
     all_hu, all_cu = spread(pair_hu), spread(pair_cu)
-    from_hi, from_bi = spread(lent_hi), spread(lent_bi)
+    here_bu = spread(here_bu[None])
+    from_hi = spread(lent_hi)
     (o_near,) = project([all_hu, all_cu], out_weight[None])
-    there_bu, from_hi, from_bi, o_near, all_hu, all_cu, lent_ci = tie_all(
-        there_bu, from_hi, from_bi, o_near, all_hu, all_cu, lent_ci
-    )
-
-    all_bu = spread(jnp.stack([here_bu, there_bu]))
-    (o_far,) = project([all_bu], out_weight[None])
+    there_bu, from_hi, here_bu, o_near, all_hu, all_cu, lent_ci, lent_bi = tie_all(
+        there_bu, from_hi, here_bu, o_near, all_hu, all_cu, lent_ci, lent_bi
+    )
+
+    there_bu = spread(there_bu[None])
+    all_bu = [x for pair in zip(here_bu, there_bu) for x in pair]
+    (o_far,) = project([all_bu], out_weight[None], 58)
     ups = [all_hu, all_cu, all_bu]
-    grads = list(per_group(backward_kernel, slots, (q, k, v, o_near, o_far), 3))
-    grads = list(tie_all(*grads))
-
-    def along_ctx(term):
-        return lax.psum_scatter(term, "ctx", scatter_dimension=0, tiled=True)
-
-    def summed(a, b):
-        return (a.astype(F32) + b.astype(F32)).astype(BF16)
+    *grads, give = per_group(backward_kernel, slots, (q, k, v, o_near, o_far), True)
+    grads, give, lent_ci, lent_bi = tie_all(grads, give, lent_ci, lent_bi)
+
+    chains, arrived, first = [], [], []
+
+    def total(arrays):
+        return sum(x.astype(F32) for x in arrays)
+
+    def to_send(c, step):
+        count = n - 1 - step
+        start = jnp.where(me == step, step + 1, 0)
+        terms = [lax.dynamic_slice_in_dim(t, start, count, 0) for t in chains[c]]
+        if step:
+            at = jnp.where(me == step, 1, 0)
+            terms.append(lax.dynamic_slice_in_dim(arrived[c][-1], at, count, 0))
+        return total(terms).astype(BF16)
+
+    def begin(terms, send=None):
+        chains.append([t.reshape(n, share // n, width) for t in terms])
+        arrived.append([])
+        first.append(to_send(len(chains) - 1, 0) if send is None else send)
+
+    def crossed_term(came, plus, also=None):
+        window = (n, jnp.where(me == 0, 1, 0))
+        term, send = outer(lent, [(came, 0)], 0, share, BF16, plus, window, also)
+        begin([term], send)
+        return term
+
+    def advance(c):
+        step = len(arrived[c])
+        if step == n - 1:
+            return
+        send = to_send(c, step) if step else first[c]
+        came = lax.ppermute(send, "ctx", [(step, step + 1), (n - 1 - step, n - 2 - step)])
+        arrived[c].append(came if step else paced(came))
+
+    def ended(cs):
+        all_arrays, at = [], []
+        for c in cs:
+            all_arrays.append(chains[c] + arrived[c])
+            at += [me] * len(chains[c])
+            for step in range(n - 1):
+                at.append(jnp.where(me == step + 1, 0, n - 2 - step))
+        return finished(all_arrays, at)
 
     for _ in bits[2:]:
         raise NotImplementedError
     crossed = swap(grads[0])
-    got = flip(jnp.stack([g[n_space // 2 :] for g in grads]), bits[-1])
-    lent = [from_hi, spread(lent_ci), from_bi]
-    mine = outer(tokens, grads, me_dp, share, F32)
-    (att,) = per_group(forward_kernel, slots, (q, k, tie(v, mine[0])), 1)
-    (proj_send,) = outer(ups, [att], 1 - me_dp, share, BF16)
-    crossed, got, lent, mine, att, proj_send, grads = tie_all(
-        crossed, got, lent, mine, att, proj_send, grads
-    )
-
-    moving = swap(grads[1])
-    (term,) = outer(lent, [crossed], 0, share, BF16, mine[0])
-    sums = [along_ctx(term)]
-    parts = [tie(g, term) for g in grads] + [got[s] for s in range(3)]
-    home, mid, far = backproject(parts, 1, n * rows, weights, [rows, (n - 2) * rows, rows])
-    crossed, home, mid, far, mine, grads, parts = tie_all(
-        moving, home, mid, far, mine, grads, parts
-    )
-
-    moving = swap(grads[2])
-    far_there, mid_there = flip(far, bits[0]), flip(mid, bits[0])
-    (term,) = outer(lent, [crossed], 0, share, BF16, mine[1])
-    kept = backproject([tie(p, term) for p in parts], 0, n * rows, weights, [rows] * n)
-    sums.append(along_ctx(tie(term, sums[-1])))
-    crossed, far_there, mid_there, mine, kept, proj_send, sums[0] = tie_all(
-        moving, far_there, mid_there, mine, kept, proj_send, sums[0]
-    )
-
-    moving = swap(proj_send)
+    got = flip(give, bits[-1])
+    lent = [from_hi, spread(lent_ci), spread(lent_bi)]
+    grads = [(g, 0) for g in grads]
+    splits = [rows] * (n + 1) + [(n - 2) * rows, rows]
+    *kept, home, mid, far = backproject(grads, got, 0, 2 * n * rows, weights, splits)
+    far_there = flip(far, bits[0])
+    crossed_term(tie(crossed, far), None, (tokens, grads[0], me_dp))
+    lent, grads, chains, first, kept, home, mid, far_there = tie_all(
+        lent, grads, chains, first, kept, home, mid, far_there
+    )
+
+    crossed = swap(grads[1][0])
+    mid_there = flip(mid, bits[0])
+    advance(0)
+    back = {across[0]: shift(total([kept[n - 1], far_there]).astype(BF16), n - across[0])}
+    mine = outer(tokens, grads[1:], me_dp, share, F32)
+    crossed_term(tie(crossed, mine[0]), mine[0])
+    mid_there, back, home, kept, grads, mine, chains, arrived, first = tie_all(
+        mid_there, back, home, kept, grads, mine, chains, arrived, first
+    )
+
+    crossed = swap(grads[2][0])
     home_there = flip(home, bits[0])
-    back = {across[0]: shift(summed(kept[n - 1], far_there), n - across[0])}
+    for c in range(2):
+        advance(c)
     mid_sums = [
-        summed(kept[1 + i], mid_there[i * rows : (i + 1) * rows]) for i in range(n - 2)
+        total([kept[1 + i], mid_there[i * rows : (i + 1) * rows]]).astype(BF16)
+        for i in range(n - 2)
     ]
-    (term,) = outer(lent, [crossed], 0, share, BF16, mine[2])
-    (proj_mine,) = outer(ups, [tie(att, term)], me_dp, share, F32)
-    sums.append(along_ctx(tie(term, sums[-1])))
-    crossed, home_there, back, mid_sums, proj_mine, sums[1] = tie_all(
-        moving, home_there, back, mid_sums, proj_mine, sums[1]
-    )
-
-    for i, d in enumerate(others):
+    split = (n - 2) // 2
+    for i, d in enumerate(others[:split]):
         back[d] = shift(mid_sums[i], n - d)
-    back[0] = summed(kept[0], home_there)
-    term = summed(proj_mine, crossed)
+    (att,) = per_group(forward_kernel, slots, (q, k, tie(v, *mid_sums)), False)
+    (proj_send,) = outer(ups, [(att, 0)], 1 - me_dp, share, BF16)
+    crossed_term(tie(crossed, proj_send), mine[1])
+    home_there, back, kept, mid_sums, att, proj_send, chains, arrived, first = tie_all(
+        home_there, back, kept, mid_sums, att, proj_send, chains, arrived, first
+    )
+
+    crossed = swap(proj_send)
+    for c in range(3):
+        advance(c)
+    for i, d in enumerate(others[split:], split):
+        back[d] = shift(mid_sums[i], n - d)
+    back[0] = total([kept[0], home_there]).astype(BF16)
+    (proj_mine,) = outer(ups, [(tie(att, back[0]), 0)], me_dp, share, F32)
+    begin([proj_mine, crossed])
+    back, chains, arrived, first = tie_all(back, chains, arrived, first)
+
+    for c in range(4):
+        advance(c)
     where = lax.rem(jnp.arange(n, dtype=jnp.int32) + me, n)
     input_grad = placed_at([back[d] for d in range(n)], where)
-    sums.append(along_ctx(tie(term, sums[-1], input_grad)))
-    qkv_grad = jnp.stack([x.astype(F32) for x in sums[:3]])
-    return (input_grad.reshape(inputs.shape), qkv_grad, sums[3].astype(F32))
+    input_grad, chains, arrived = tie_all(input_grad, chains, arrived)
+    for _ in range(n - 3):
+        for c in range(1, 4):
+            advance(c)
+        input_grad, chains, arrived = tie_all(input_grad, chains, arrived)
+    advance(3)
+    qkv_grad = ended(range(3))
+    arrived[3][-1] = tie(arrived[3][-1], qkv_grad)
+    return (input_grad.reshape(inputs.shape), qkv_grad, ended([3])[0])
 
 
 def solution(mesh):

time: 319 us -> 291 us (0.912)
  waiting for transfers between devices: 157 us -> 113 us
  starting transfers between devices: 33.8 us -> 56.2 us
  between operations: 14.4 us -> 1.51 us
  Pallas kernels: 83.1 us -> 88.9 us
  other arithmetic: 12.2 us -> 15.8 us
  local copies, waits for them, and re-layouts: 18.2 us -> 15 us
    reduce_scatter x4 -> x0, waiting for transfers between devices: 27.2 us -> none  [along_ctx(): return lax.psum_scatter(term, 'ctx', scatter_dimension=0, tiled=True)]
    ppermute x9, waiting for transfers between devices: 81.5 us -> 56.1 us  [shift(): return lax.ppermute(x, 'ctx', [(i, (i + d) % n) for i in range(n)])]
    ppermute x0 -> x12, waiting for transfers between devices: none -> 22.7 us  [advance(): lax.ppermute(send, 'ctx', [(step, step + 1), (n - 1 - step, n - 2 - step)])]
    ppermute x0 -> x12, starting transfers between devices: none -> 21 us  [advance(): lax.ppermute(send, 'ctx', [(step, step + 1), (n - 1 - step, n - 2 - step)])]
    ppermute x20 -> x21, waiting for transfers between devices: 28.1 us -> 15.3 us  [flip(): return lax.ppermute(x, 'space', [(i, i ^ bit) for i in range(n_space)])]
    pallas_call x0 -> x2, Pallas kernels: none -> 7.26 us  [finished(): pl.pallas_call(kernel, grid_spec=pltpu.PrefetchScalarGridSpec(num_scalar_...]
    pallas_call x2 -> x1, Pallas kernels: 21.2 us -> 14.2 us  [backproject(): pl.pallas_call(kernel, grid=(model // wide,), in_specs=[pl.BlockSpec((row...]
    convert_element_type x5 -> x12, other arithmetic: 7.03 us -> 13.7 us  [the longest x9 8.72 us: to_send(): return total(terms).astype(BF16)]
  transfers between devices with their start and end apart: 40 -> 49, of which waited for: 19 -> 24; matrix products, arithmetic and copies ran while one was open for 5% -> 7% of each run, Pallas kernels for 23% -> 27%
where the time goes in v3:
time: 291 us
  waiting for transfers between devices  113 us (39%)
  Pallas kernels  88.9 us (31%)
  starting transfers between devices  56.2 us (19%)
  other arithmetic  15.8 us (5%)
  local copies, waits for them, and re-layouts  15 us (5%)
    ppermute x9, waiting for transfers between devices, shift(): return lax.ppermute(x, 'ctx', [(i, (i + d) % n) for i in range(n)])  56.1 us
    pallas_call x6, Pallas kernels, outer(): pl.pallas_call(kernel, grid_spec=pltpu.PrefetchScalarGridSpec(num_scalar_...  40.6 us
    ppermute x12, waiting for transfers between devices, advance(): lax.ppermute(send, 'ctx', [(step, step + 1), (n - 1 - step, n - 2 - step)])  22.7 us
    ppermute x12, starting transfers between devices, advance(): lax.ppermute(send, 'ctx', [(step, step + 1), (n - 1 - step, n - 2 - step)])  21 us
    ppermute x7, waiting for transfers between devices, swap(): return lax.ppermute(x, 'dp', [(0, 1), (1, 0)])  19.1 us
    ppermute x9, starting transfers between devices, shift(): return lax.ppermute(x, 'ctx', [(i, (i + d) % n) for i in range(n)])  17.9 us
    pallas_call x3, Pallas kernels, project(): pl.pallas_call(kernel, grid=(count,), in_specs=[pl.BlockSpec((size, model...  17.4 us
    ppermute x21, waiting for transfers between devices, flip(): return lax.ppermute(x, 'space', [(i, i ^ bit) for i in range(n_space)])  15.3 us
  transfers between devices with their start and end apart: 49, of which 24 were waited for; matrix products, arithmetic and copies ran while one was open for 7% of the time, Pallas kernels for 27%

profile of v3, /device:TPU:0, one launch (start us, length us, event | category | flops | bytes accessed | tf_op | source)
XLA Modules:
  0.0 290.6 jit_solution(16422832477872327045)
XLA Ops:
  10.3 5.9 %collective-permute-done.2 = bf16[1,64,3072]{2,1,0:T(8,128)(2,1)S(1)} collective-permute-done((bf16[1,64,3072]{2,1,0:T(8,128)(2,1)S(1)}, bf16[1,64,3072]{2,1,0:T(8,128)(2,1)S(1)}, u32[]{:S(2)}, u32[]{:S(2)}) %collective-permute-start.2) | collective-permute-done | bytes 393248 | tf_op jit(solution)/shard_map/ppermute | solution.py:372
  16.2 11.6 %collective-permute-done = bf16[64,3072]{1,0:T(8,128)(2,1)S(1)} collective-permute-done((bf16[64,3072]{1,0:T(8,128)(2,1)S(1)}, bf16[64,3072]{1,0:T(8,128)(2,1)S(1)}, u32[]{:S(2)}, u32[]{:S(2)}) %collective-permute-start) | collective-permute-done | bytes 393248 | tf_op jit(solution)/shard_map/ppermute | solution.py:369
  33.9 5.6 %collective-permute-done.7 = bf16[2,1,64,1536]{3,2,1,0:T(8,128)(2,1)S(1)} collective-permute-done((bf16[2,1,64,1536]{3,2,1,0:T(8,128)(2,1)S(1)}, bf16[2,1,64,1536]{3,2,1,0:T(8,128)(2,1)S(1)}, u32[]{:S(2)}, u32[]{:S(2)}) %collective-permute-start.7) | collective-permute-done | bytes 393248 | tf_op jit(solution)/shard_map/ppermute | solution.py:375
  43.5 6.3 %collective-permute-done.5 = bf16[64,3072]{1,0:T(8,128)(2,1)S(1)} collective-permute-done((bf16[64,3072]{1,0:T(8,128)(2,1)}, bf16[64,3072]{1,0:T(8,128)(2,1)S(1)}, u32[]{:S(2)}, u32[]{:S(2)}) %collective-permute-start.5) | collective-permute-done | bytes 393248 | tf_op jit(solution)/shard_map/ppermute | solution.py:369
  54.7 7.2 %collective-permute-done.12 = bf16[2,1,64,1536]{3,2,0,1:T(8,128)(2,1)S(1)} collective-permute-done((bf16[2,1,64,1536]{3,2,0,1:T(8,128)(2,1)S(1)}, bf16[2,1,64,1536]{3,2,0,1:T(8,128)(2,1)S(1)}, u32[]{:S(2)}, u32[]{:S(2)}) %collective-permute-start.12) | collective-permute-done | bytes 393248 | tf_op jit(solution)/shard_map/ppermute | solution.py:375
  64.2 8.7 %collective-permute-done.9 = bf16[64,3072]{1,0:T(8,128)(2,1)S(1)} collective-permute-done((bf16[64,3072]{1,0:T(8,128)(2,1)S(1)}, bf16[64,3072]{1,0:T(8,128)(2,1)S(1)}, u32[]{:S(2)}, u32[]{:S(2)}) %collective-permute-start.9) | collective-permute-done | bytes 393248 | tf_op jit(solution)/shard_map/ppermute | solution.py:369
  77.5 10.9 %shard_map.76 = (bf16[1024,384]{1,0:T(8,128)(2,1)S(1)}, bf16[1024,384]{1,0:T(8,128)(2,1)S(1)}, bf16[1024,384]{1,0:T(8,128)(2,1)S(1)}) custom-call(bf16[128,3072]{1,0:T(8,128)(2,1)S(1)} %bitcast.138, bf16[256,3072]{1,0:T(8,128)(2,1)S(1)} %bitcast.120, bf16[128,3072]{1,0:T(8,128)(2,1)S(1)} %bitcast.144, bf16[128,3072]{1,0:T(8,128)(2,1)S(1)} %bitcast.139, ...), custom_call_target="tpu_custom_call" | custom-call | flops 1 | bytes 1 | tf_op jit(solution)/shard_map/pallas_call | solution.py:161
  88.5 7.5 %collective-permute-done.14 = bf16[64,3072]{1,0:T(8,128)(2,1)S(1)} collective-permute-done((bf16[64,3072]{1,0:T(8,128)(2,1)S(1)}, bf16[64,3072]{1,0:T(8,128)(2,1)S(1)}, u32[]{:S(2)}, u32[]{:S(2)}) %collective-permute-start.14) | collective-permute-done | bytes 393248 | tf_op jit(solution)/shard_map/ppermute | solution.py:369
  115.7 4.6 %shard_map.79 = (bf16[4,4,64,384]{3,2,1,0:T(8,128)(2,1)S(1)}, bf16[4,4,64,384]{3,2,1,0:T(8,128)(2,1)S(1)}, bf16[4,4,64,384]{3,2,1,0:T(8,128)(2,1)S(1)}, bf16[3,2,4,64,384]{4,3,2,1,0:T(8,128)(2,1)S(1)}) custom-call(s32[4]{0:T(128)S(1)} %gather_fusion, bf16[4,4,64,384]{3,2,1,0:T(8,128)(2,1)S(1)} %bitcast.186, bf16[4,4,64,384]{3,2,1,0:T(8,128)(2,1)S(1)} %bitcast.188, ...), custom_call_target="tpu_custom_call" | custom-call | flops 1 | bytes 1 | tf_op jit(solution)/shard_map/pallas_call | solution.py:102
  126.1 14.2 %shard_map.80 = (bf16[64,3072]{1,0:T(8,128)(2,1)}, bf16[64,3072]{1,0:T(8,128)(2,1)}, bf16[64,3072]{1,0:T(8,128)(2,1)}, bf16[64,3072]{1,0:T(8,128)(2,1)}, bf16[64...) custom-call(bf16[1024,384]{1,0:T(8,128)(2,1)} %bitcast.180, bf16[1024,384]{1,0:T(8,128)(2,1)} %bitcast.184, ...), custom_call_target="tpu_custom_call" | custom-call | flops 1 | bytes 1 | tf_op jit(solution)/shard_map/pallas_call | solution.py:268
  142.2 8.8 %shard_map.81 = (bf16[1536,384]{1,0:T(8,128)(2,1)}, bf16[3,384,384]{2,1,0:T(8,128)(2,1)}) custom-call(s32[3]{0:T(128)} %pad_add_fusion.scalars_ref, bf16[128,1536]{1,0:T(8,128)(2,1)} %bitcast.198, bf16[256,1536]{1,0:T(8,128)(2,1)} %bitcast.53.refs_1_.refs_4_, bf16[128,1536]{1,0:T(8,128)(2,1)} %bitcast.204, bf16[128,1536]{1,0:T(8,128)(2,1)} %bitcast.199, ...), custom_call_target="tpu_custom_call" | custom-call | flops 1 | bytes 1 | tf_op jit(solution)/shard_map/pallas_call | solution.py:221
  159.1 7.6 %shard_map.82 = (f32[1536,384]{1,0:T(8,128)}, f32[1536,384]{1,0:T(8,128)}) custom-call(s32[3]{0:T(128)} %stack.139.scalars_ref, bf16[128,3072]{1,0:T(8,128)(2,1)} %bitcast.142, bf16[256,3072]{1,0:T(8,128)(2,1)} %bitcast.124, bf16[128,3072]{1,0:T(8,128)(2,1)} %bitcast.148, bf16[128,3072]{1,0:T(8,128)(2,1)} %bitcast.143, bf16[256,3072]{1,0:T(8,128)(2,1)} %bitcast.125, ...), custom_call_target="tpu_custom_call" | custom-call | flops 1 | bytes 1 | tf_op jit(solution)/shard_map/pallas_call | solution.py:221
  170.6 6.4 %shard_map.83 = (bf16[1536,384]{1,0:T(8,128)(2,1)}, bf16[3,384,384]{2,1,0:T(8,128)(2,1)}) custom-call(s32[3]{0:T(128)} %pad_add_fusion.2.scalars_ref, bf16[128,1536]{1,0:T(8,128)(2,1)} %bitcast.200, bf16[256,1536]{1,0:T(8,128)(2,1)} %bitcast.69.refs_1_, bf16[128,1536]{1,0:T(8,128)(2,1)} %bitcast.206, bf16[128,1536]{1,0:T(8,128)(2,1)} %bitcast.201, ...), custom_call_target="tpu_custom_call" | custom-call | flops 1 | bytes 1 | tf_op jit(solution)/shard_map/pallas_call | solution.py:221
  177.1 4.2 %collective-permute-done.30.refs_2_ = bf16[64,3072]{1,0:T(8,128)(2,1)S(1)} collective-permute-done((bf16[64,3072]{1,0:T(8,128)(2,1)}, bf16[64,3072]{1,0:T(8,128)(2,1)S(1)}, u32[]{:S(2)}, u32[]{:S(2)}) %collective-permute-start.30) | collective-permute-done | bytes 393248 | tf_op jit(solution)/shard_map/ppermute | solution.py:369
  185.7 6.3 %collective-permute-start.37 = (bf16[3,384,384]{2,1,0:T(8,128)(2,1)}, bf16[3,384,384]{2,1,0:T(8,128)(2,1)S(1)}, u32[]{:S(2)}, u32[]{:S(2)}) collective-permute-start(bf16[3,384,384]{2,1,0:T(8,128)(2,1)} %get-tuple-element.319), channel_id=1, source_target_pairs={{0,4},{12,8},{1,5},{13,9},{2,6},{14,10},{3,7},{15,11},{16,20},{28,... | collective-permute-start | bytes 2654216 | tf_op jit(solution)/shard_map/ppermute | solution.py:488
  200.9 5.5 %shard_map.85 = bf16[1536,384]{1,0:T(8,128)(2,1)} custom-call(s32[3]{0:T(128)} %stack.142.scalars_ref, bf16[128,3072]{1,0:T(8,128)(2,1)} %bitcast.152, bf16[256,3072]{1,0:T(8,128)(2,1)} %bitcast.116, bf16[64,3072]{1,0:T(8,128)(2,1)} %copy-done.37, bf16[128,3072]{1,0:T(8,128)(2,1)} %bitcast.153, bf16[256,3072]{1,0:T(8,128)(2,1)} %bitcast.117, ...), custom_call_target="tpu_custom_call" | custom-call | flops 1 | bytes 1 | tf_op jit(solution)/shard_map/pallas_call | solution.py:221
  206.5 6.5 %shard_map.86 = (bf16[1536,384]{1,0:T(8,128)(2,1)}, bf16[3,384,384]{2,1,0:T(8,128)(2,1)}) custom-call(s32[3]{0:T(128)} %pad_add_fusion.2.scalars_ref, bf16[128,1536]{1,0:T(8,128)(2,1)} %bitcast.202, bf16[256,1536]{1,0:T(8,128)(2,1)} %bitcast.69.refs_1_, bf16[128,1536]{1,0:T(8,128)(2,1)} %bitcast.208, bf16[128,1536]{1,0:T(8,128)(2,1)} %bitcast.203, ...), custom_call_target="tpu_custom_call" | custom-call | flops 1 | bytes 1 | tf_op jit(solution)/shard_map/pallas_call | solution.py:221
  213.0 4.8 %collective-permute-done.34.refs_1_ = bf16[64,3072]{1,0:T(8,128)(2,1)S(1)} collective-permute-done((bf16[64,3072]{1,0:T(8,128)(2,1)}, bf16[64,3072]{1,0:T(8,128)(2,1)S(1)}, u32[]{:S(2)}, u32[]{:S(2)}) %collective-permute-start.34) | collective-permute-done | bytes 393248 | tf_op jit(solution)/shard_map/ppermute | solution.py:369
  226.1 4.9 %collective-permute-start.38 = (bf16[64,3072]{1,0:T(8,128)(2,1)S(1)}, bf16[64,3072]{1,0:T(8,128)(2,1)S(1)}, u32[]{:S(2)}, u32[]{:S(2)}) collective-permute-start(bf16[64,3072]{1,0:T(8,128)(2,1)S(1)} %get-tuple-element.325), channel_id=1, source_target_pairs={{0,4},{4,8},{8,12},{12,0},{1,5},{5,9},{9,13},{13,1},{2,6},{6,10},{... | collective-permute-start | bytes 1179656 | tf_op jit(solution)/shard_map/ppermute | solution.py:369
  232.2 5.8 %shard_map.87 = f32[1536,384]{1,0:T(8,128)} custom-call(s32[3]{0:T(128)} %stack.139.scalars_ref, bf16[128,3072]{1,0:T(8,128)(2,1)} %bitcast.154, bf16[256,3072]{1,0:T(8,128)(2,1)} %bitcast.118, bf16[64,3072]{1,0:T(8,128)(2,1)} %copy-done.37, bf16[128,3072]{1,0:T(8,128)(2,1)} %bitcast.155, bf16[256,3072]{1,0:T(8,128)(2,1)} %bitcast.119, ...), custom_call_target="tpu_custom_call" | custom-call | flops 1 | bytes 1 | tf_op jit(solution)/shard_map/pallas_call | solution.py:221
  244.5 6.7 %collective-permute-done.38.refs_3_ = bf16[64,3072]{1,0:T(8,128)(2,1)S(1)} collective-permute-done((bf16[64,3072]{1,0:T(8,128)(2,1)S(1)}, bf16[64,3072]{1,0:T(8,128)(2,1)S(1)}, u32[]{:S(2)}, u32[]{:S(2)}) %collective-permute-start.38) | collective-permute-done | bytes 393248 | tf_op jit(solution)/shard_map/ppermute | solution.py:369
  257.3 7.7 %collective-permute-done.45.refs_2_ = bf16[3,384,384]{2,1,0:T(8,128)(2,1)S(1)} collective-permute-done((bf16[3,384,384]{2,1,0:T(8,128)(2,1)S(1)}, bf16[3,384,384]{2,1,0:T(8,128)(2,1)S(1)}, u32[]{:S(2)}, u32[]{:S(2)}) %collective-permute-start.45) | collective-permute-done | bytes 884768 | tf_op jit(solution)/shard_map/ppermute | solution.py:488
  267.6 10.1 %collective-permute-done.46.refs_11_ = bf16[1,384,384]{2,1,0:T(8,128)(2,1)S(1)} collective-permute-done((bf16[1,384,384]{2,1,0:T(8,128)(2,1)S(1)}, bf16[1,384,384]{2,1,0:T(8,128)(2,1)S(1)}, u32[]{:S(2)}, u32[]{:S(2)}) %collective-permute-start.46) | collective-permute-done | bytes 294944 | tf_op jit(solution)/shard_map/ppermute | solution.py:488
  280.5 4.2 %shard_map.89 = f32[3,384,384]{2,1,0:T(8,128)} custom-call(s32[12]{0:T(128)} %stack.146.at_ref, bf16[4,384,384]{2,1,0:T(8,128)(2,1)} %bitcast.221, bf16[3,384,384]{2,1,0:T(8,128)(2,1)} %collective-permute-done.32.refs_1_, bf16[2,384,384]{2,1,0:T(8,128)(2,1)} %collective-permute-done.36.refs_2_, bf16[1,384,384]{2,1,0:T(8,128)(2,1)} %collective-permute-done.40.refs_3_, ...), custom_call_target="tpu_custom_call" | custom-call | flops 1 | bytes 1 | tf_op jit(solution)/shard_map/pallas_call | solution.py:316
  (246 shorter events, 117.0 us)
Async XLA Ops:
  0.6 27.1 %collective-permute-start.3 = (bf16[3,3072,384]{2,1,0:T(8,128)(2,1)}, bf16[3,3072,384]{2,1,0:T(8,128)(2,1)}, u32[]{:S(2)}, u32[]{:S(2)}) collective-permute-start(bf16[3,3072,384]{2,1,0:T(8,128)(2,1)} %refs_4_), channel_id=1, source_target_pairs={{0,1},{1,0},{2,3},{3,2},{4,5},{5,4},{6,7},{7,6},{8,9},{9,8},{10,11... | collective-permute-start | bytes 21233672 | tf_op jit(solution)/shard_map/ppermute | solution.py:372
  7.2 20.5 %collective-permute-start = (bf16[64,3072]{1,0:T(8,128)(2,1)S(1)}, bf16[64,3072]{1,0:T(8,128)(2,1)S(1)}, u32[]{:S(2)}, u32[]{:S(2)}) collective-permute-start(bf16[64,3072]{1,0:T(8,128)(2,1)S(1)} %get-tuple-element.397), channel_id=1, source_target_pairs={{0,8},{4,12},{8,0},{12,4},{1,9},{5,13},{9,1},{13,5},{2,10},{6,14},... | collective-permute-start | bytes 1179656 | tf_op jit(solution)/shard_map/ppermute | solution.py:369
  27.8 22.0 %collective-permute-start.8 = (bf16[2,1,64,3072]{3,2,1,0:T(8,128)(2,1)S(1)}, bf16[2,1,64,3072]{3,2,1,0:T(8,128)(2,1)S(1)}, u32[]{:S(2)}, u32[]{:S(2)}) collective-permute-start(bf16[2,1,64,3072]{3,2,1,0:T(8,128)(2,1)S(1)} %pad_maximum_fusion.2), channel_id=1, source_target_pairs={{0,1},{1,0},{2,3},{3,2},{4,5},{5,4},{6,7},{7,6},{8,9},{9,8},{10,11... | collective-permute-start | bytes 2359304 | tf_op jit(solution)/shard_map/ppermute | solution.py:372
  30.2 19.6 %collective-permute-start.5 = (bf16[64,3072]{1,0:T(8,128)(2,1)}, bf16[64,3072]{1,0:T(8,128)(2,1)S(1)}, u32[]{:S(2)}, u32[]{:S(2)}) collective-permute-start(bf16[64,3072]{1,0:T(8,128)(2,1)} %get-tuple-element.195), channel_id=1, source_target_pairs={{0,12},{4,0},{8,4},{12,8},{1,13},{5,1},{9,5},{13,9},{2,14},{6,2},{... | collective-permute-start | bytes 1179656 | tf_op jit(solution)/shard_map/ppermute | solution.py:369
  49.9 23.1 %collective-permute-start.13 = (bf16[2,1,64,3072]{3,2,0,1:T(8,128)(2,1)S(1)}, bf16[2,1,64,3072]{3,2,0,1:T(8,128)(2,1)S(1)}, u32[]{:S(2)}, u32[]{:S(2)}) collective-permute-start(bf16[2,1,64,3072]{3,2,0,1:T(8,128)(2,1)S(1)} %pad_maximum_fusion.3), channel_id=1, source_target_pairs={{0,1},{1,0},{2,3},{3,2},{4,5},{5,4},{6,7},{7,6},{8,9},{9,8},{10,11... | collective-permute-start | bytes 2359304 | tf_op jit(solution)/shard_map/ppermute | solution.py:372
  50.1 22.9 %collective-permute-start.11 = (bf16[2,64,3072]{2,1,0:T(8,128)(2,1)S(1)}, bf16[2,64,3072]{2,1,0:T(8,128)(2,1)S(1)}, u32[]{:S(2)}, u32[]{:S(2)}) collective-permute-start(bf16[2,64,3072]{2,1,0:T(8,128)(2,1)S(1)} %get-tuple-element.404), channel_id=1, source_target_pairs={{0,2},{1,3},{2,0},{3,1},{4,6},{5,7},{6,4},{7,5},{8,10},{9,11},{10,... | collective-permute-start | bytes 2359304 | tf_op jit(solution)/shard_map/ppermute | solution.py:372
  73.3 22.6 %collective-permute-start.16 = (bf16[2,2,64,1536]{3,2,1,0:T(8,128)(2,1)S(1)}, bf16[2,2,64,1536]{3,2,1,0:T(8,128)(2,1)}, u32[]{:S(2)}, u32[]{:S(2)}) collective-permute-start(bf16[2,2,64,1536]{3,2,1,0:T(8,128)(2,1)S(1)} %fusion), channel_id=1, source_target_pairs={{0,16},{16,0},{1,17},{17,1},{2,18},{18,2},{3,19},{19,3},{4,20},{20... | collective-permute-start | bytes 2359304 | tf_op jit(solution)/shard_map/ppermute | solution.py:375
  74.2 21.8 %collective-permute-start.15 = (bf16[2,64,3072]{2,1,0:T(8,128)(2,1)S(1)}, bf16[2,64,3072]{2,1,0:T(8,128)(2,1)S(1)}, u32[]{:S(2)}, u32[]{:S(2)}) collective-permute-start(bf16[2,64,3072]{2,1,0:T(8,128)(2,1)S(1)} %get-tuple-element.402), channel_id=1, source_target_pairs={{0,2},{1,3},{2,0},{3,1},{4,6},{5,7},{6,4},{7,5},{8,10},{9,11},{10,... | collective-permute-start | bytes 2359304 | tf_op jit(solution)/shard_map/ppermute | solution.py:372
  75.7 20.3 %collective-permute-start.14 = (bf16[64,3072]{1,0:T(8,128)(2,1)S(1)}, bf16[64,3072]{1,0:T(8,128)(2,1)S(1)}, u32[]{:S(2)}, u32[]{:S(2)}) collective-permute-start(bf16[64,3072]{1,0:T(8,128)(2,1)S(1)} %copy-done.53), channel_id=1, source_target_pairs={{0,8},{4,12},{8,0},{12,4},{1,9},{5,13},{9,1},{13,5},{2,10},{6,14},... | collective-permute-start | bytes 1179656 | tf_op jit(solution)/shard_map/ppermute | solution.py:369
  122.3 19.9 %collective-permute-start.26 = (bf16[4,4,64,384]{3,2,1,0:T(8,128)(2,1)S(1)}, bf16[4,4,64,384]{3,2,1,0:T(8,128)(2,1)}, u32[]{:S(2)}, u32[]{:S(2)}) collective-permute-start(bf16[4,4,64,384]{3,2,1,0:T(8,128)(2,1)S(1)} %get-tuple-element.253), channel_id=1, source_target_pairs={{0,16},{16,0},{1,17},{17,1},{2,18},{18,2},{3,19},{19,3},{4,20},{20... | collective-permute-start | bytes 2359304 | tf_op jit(solution)/shard_map/ppermute | solution.py:375
  122.9 19.3 %collective-permute-start.24 = (bf16[2,2,64,1536]{3,2,1,0:T(8,128)(2,1)}, bf16[2,2,64,1536]{3,2,1,0:T(8,128)(2,1)}, u32[]{:S(2)}, u32[]{:S(2)}) collective-permute-start(bf16[2,2,64,1536]{3,2,1,0:T(8,128)(2,1)} %collective-permute-done.16), channel_id=1, source_target_pairs={{0,1},{1,0},{2,3},{3,2},{4,5},{5,4},{6,7},{7,6},{8,9},{9,8},{10,11... | collective-permute-start | bytes 2359304 | tf_op jit(solution)/shard_map/ppermute | solution.py:372
  152.4 24.7 %collective-permute-start.32 = (bf16[3,384,384]{2,1,0:T(8,128)(2,1)}, bf16[3,384,384]{2,1,0:T(8,128)(2,1)}, u32[]{:S(2)}, u32[]{:S(2)}) collective-permute-start(bf16[3,384,384]{2,1,0:T(8,128)(2,1)} %get-tuple-element.295), channel_id=1, source_target_pairs={{0,4},{12,8},{1,5},{13,9},{2,6},{14,10},{3,7},{15,11},{16,20},{28,... | collective-permute-start | bytes 2654216 | tf_op jit(solution)/shard_map/ppermute | solution.py:488
  155.4 25.9 %collective-permute-start.29 = (bf16[128,3072]{1,0:T(8,128)(2,1)}, bf16[128,3072]{1,0:T(8,128)(2,1)}, u32[]{:S(2)}, u32[]{:S(2)}) collective-permute-start(bf16[128,3072]{1,0:T(8,128)(2,1)} %get-tuple-element.269), channel_id=1, source_target_pairs={{0,2},{1,3},{2,0},{3,1},{4,6},{5,7},{6,4},{7,5},{8,10},{9,11},{10,... | collective-permute-start | bytes 2359304 | tf_op jit(solution)/shard_map/ppermute | solution.py:372
  158.0 23.3 %collective-permute-start.30 = (bf16[64,3072]{1,0:T(8,128)(2,1)}, bf16[64,3072]{1,0:T(8,128)(2,1)S(1)}, u32[]{:S(2)}, u32[]{:S(2)}) collective-permute-start(bf16[64,3072]{1,0:T(8,128)(2,1)} %add_convert_fusion.8), channel_id=1, source_target_pairs={{0,8},{4,12},{8,0},{12,4},{1,9},{5,13},{9,1},{13,5},{2,10},{6,14},... | collective-permute-start | bytes 1179656 | tf_op jit(solution)/shard_map/ppermute | solution.py:369
  183.4 34.4 %collective-permute-start.36 = (bf16[2,384,384]{2,1,0:T(8,128)(2,1)}, bf16[2,384,384]{2,1,0:T(8,128)(2,1)}, u32[]{:S(2)}, u32[]{:S(2)}) collective-permute-start(bf16[2,384,384]{2,1,0:T(8,128)(2,1)} %add_convert_fusion.4), channel_id=1, source_target_pairs={{4,8},{8,4},{5,9},{9,5},{6,10},{10,6},{7,11},{11,7},{20,24},{24,20... | collective-permute-start | bytes 1769480 | tf_op jit(solution)/shard_map/ppermute | solution.py:488
  184.8 21.6 %collective-permute-start.35 = (bf16[4,4,64,384]{3,2,1,0:T(8,128)(2,1)S(1)}, bf16[4,4,64,384]{3,2,1,0:T(8,128)(2,1)}, u32[]{:S(2)}, u32[]{:S(2)}) collective-permute-start(bf16[4,4,64,384]{3,2,1,0:T(8,128)(2,1)S(1)} %copy-done.14), channel_id=1, source_target_pairs={{0,16},{16,0},{1,17},{17,1},{2,18},{18,2},{3,19},{19,3},{4,20},{20... | collective-permute-start | bytes 2359304 | tf_op jit(solution)/shard_map/ppermute | solution.py:375
  185.7 27.2 %collective-permute-start.37 = (bf16[3,384,384]{2,1,0:T(8,128)(2,1)}, bf16[3,384,384]{2,1,0:T(8,128)(2,1)S(1)}, u32[]{:S(2)}, u32[]{:S(2)}) collective-permute-start(bf16[3,384,384]{2,1,0:T(8,128)(2,1)} %get-tuple-element.319), channel_id=1, source_target_pairs={{0,4},{12,8},{1,5},{13,9},{2,6},{14,10},{3,7},{15,11},{16,20},{28,... | collective-permute-start | bytes 2654216 | tf_op jit(solution)/shard_map/ppermute | solution.py:488
  194.1 23.7 %collective-permute-start.34 = (bf16[64,3072]{1,0:T(8,128)(2,1)}, bf16[64,3072]{1,0:T(8,128)(2,1)S(1)}, u32[]{:S(2)}, u32[]{:S(2)}) collective-permute-start(bf16[64,3072]{1,0:T(8,128)(2,1)} %get-tuple-element.400), channel_id=1, source_target_pairs={{0,12},{4,0},{8,4},{12,8},{1,13},{5,1},{9,5},{13,9},{2,14},{6,2},{... | collective-permute-start | bytes 1179656 | tf_op jit(solution)/shard_map/ppermute | solution.py:369
  195.8 22.0 %collective-permute-start.33 = (bf16[64,3072]{1,0:T(8,128)(2,1)}, bf16[64,3072]{1,0:T(8,128)(2,1)}, u32[]{:S(2)}, u32[]{:S(2)}) collective-permute-start(bf16[64,3072]{1,0:T(8,128)(2,1)} %get-tuple-element.297), channel_id=1, source_target_pairs={{0,2},{1,3},{2,0},{3,1},{4,6},{5,7},{6,4},{7,5},{8,10},{9,11},{10,... | collective-permute-start | bytes 1179656 | tf_op jit(solution)/shard_map/ppermute | solution.py:372
  217.8 24.5 %collective-permute-start.39 = (bf16[1536,384]{1,0:T(8,128)(2,1)}, bf16[1536,384]{1,0:T(8,128)(2,1)S(1)}, u32[]{:S(2)}, u32[]{:S(2)}) collective-permute-start(bf16[1536,384]{1,0:T(8,128)(2,1)} %shard_map.85), channel_id=1, source_target_pairs={{0,16},{16,0},{1,17},{17,1},{2,18},{18,2},{3,19},{19,3},{4,20},{20... | collective-permute-start | bytes 3538952 | tf_op jit(solution)/shard_map/ppermute | solution.py:375
  218.8 21.8 %collective-permute-start.42 = (bf16[3,384,384]{2,1,0:T(8,128)(2,1)}, bf16[3,384,384]{2,1,0:T(8,128)(2,1)S(1)}, u32[]{:S(2)}, u32[]{:S(2)}) collective-permute-start(bf16[3,384,384]{2,1,0:T(8,128)(2,1)} %get-tuple-element.335), channel_id=1, source_target_pairs={{0,4},{12,8},{1,5},{13,9},{2,6},{14,10},{3,7},{15,11},{16,20},{28,... | collective-permute-start | bytes 2654216 | tf_op jit(solution)/shard_map/ppermute | solution.py:488
  222.3 28.9 %collective-permute-start.41 = (bf16[2,384,384]{2,1,0:T(8,128)(2,1)}, bf16[2,384,384]{2,1,0:T(8,128)(2,1)S(1)}, u32[]{:S(2)}, u32[]{:S(2)}) collective-permute-start(bf16[2,384,384]{2,1,0:T(8,128)(2,1)} %add_convert_fusion.3), channel_id=1, source_target_pairs={{4,8},{8,4},{5,9},{9,5},{6,10},{10,6},{7,11},{11,7},{20,24},{24,20... | collective-permute-start | bytes 1769480 | tf_op jit(solution)/shard_map/ppermute | solution.py:488
  224.8 19.6 %collective-permute-start.40 = (bf16[1,384,384]{2,1,0:T(8,128)(2,1)}, bf16[1,384,384]{2,1,0:T(8,128)(2,1)}, u32[]{:S(2)}, u32[]{:S(2)}) collective-permute-start(bf16[1,384,384]{2,1,0:T(8,128)(2,1)} %add_convert_fusion.12), channel_id=1, source_target_pairs={{8,12},{4,0},{9,13},{5,1},{10,14},{6,2},{11,15},{7,3},{24,28},{20,... | collective-permute-start | bytes 884744 | tf_op jit(solution)/shard_map/ppermute | solution.py:488
  226.1 25.1 %collective-permute-start.38 = (bf16[64,3072]{1,0:T(8,128)(2,1)S(1)}, bf16[64,3072]{1,0:T(8,128)(2,1)S(1)}, u32[]{:S(2)}, u32[]{:S(2)}) collective-permute-start(bf16[64,3072]{1,0:T(8,128)(2,1)S(1)} %get-tuple-element.325), channel_id=1, source_target_pairs={{0,4},{4,8},{8,12},{12,0},{1,5},{5,9},{9,13},{13,1},{2,6},{6,10},{... | collective-permute-start | bytes 1179656 | tf_op jit(solution)/shard_map/ppermute | solution.py:369
  (86 other events, 844.4 us)

commit v4 on v3

--- a/solution.py
+++ b/solution.py
@@ -303,16 +303,18 @@
     )(where, *pieces)
 
 
-def finished(chains, at):
+def finished(chains, at, counts):
     arrays = [x for chain in chains for x in chain]
     _, rows, width = arrays[0].shape
 
     def kernel(at_ref, *refs):
+        out_refs = [(ref, j) for ref, count in zip(refs[len(arrays) :], counts) for j in range(count)]
         i = 0
-        for c, chain in enumerate(chains):
-            refs[-1][c] = sum(ref[0].astype(F32) for ref in refs[i : i + len(chain)])
+        for (out_ref, j), chain in zip(out_refs, chains):
+            out_ref[j] = sum(ref[0].astype(F32) for ref in refs[i : i + len(chain)])
             i += len(chain)
 
+    shapes = [(count, rows, width) for count in counts]
     return pl.pallas_call(
         kernel,
         grid_spec=pltpu.PrefetchScalarGridSpec(
@@ -322,9 +324,9 @@
                 pl.BlockSpec((1, rows, width), lambda i, at_ref, j=j: (at_ref[j], 0, 0))
                 for j in range(len(arrays))
             ],
-            out_specs=pl.BlockSpec((len(chains), rows, width), lambda i, at_ref: (0, 0, 0)),
+            out_specs=[pl.BlockSpec(shape, lambda i, at_ref: (0, 0, 0)) for shape in shapes],
         ),
-        out_shape=jax.ShapeDtypeStruct((len(chains), rows, width), F32),
+        out_shape=[jax.ShapeDtypeStruct(shape, F32) for shape in shapes],
         compiler_params=pltpu.CompilerParams(vmem_limit_bytes=60 * MIB),
         cost_estimate=FREE,
     )(jnp.stack(at).astype(jnp.int32), *arrays)
@@ -337,9 +339,11 @@
 def paced(x):
     mark = pl.pallas_call(
         lambda x_ref, out_ref: out_ref.__setitem__(..., jnp.zeros_like(out_ref)),
-        in_specs=[pl.BlockSpec(memory_space=pl.ANY)],
+        grid=(1,),
+        in_specs=[pl.BlockSpec((1, 16, 128), lambda i: (0, 0, 0))],
+        out_specs=pl.BlockSpec((8, 128), lambda i: (0, 0)),
         out_shape=jax.ShapeDtypeStruct((8, 128), F32),
-        cost_estimate=pl.CostEstimate(flops=20 * 10**9, bytes_accessed=1, transcendentals=0),
+        cost_estimate=pl.CostEstimate(flops=100 * 10**9, bytes_accessed=1, transcendentals=0),
     )(x)
     return tie(x, mark)
 
@@ -395,10 +399,11 @@
     def moved(pieces, ds):
         return [shift(p, d) for p, d in zip(pieces, ds)]
 
-    here_hi, here_hu = to(inputs, 0)[None], to(upstream, 0)[None]
-    send_ci, send_cu, send_bu = cut(inputs, others), cut(upstream, others), cut(upstream, across)
-
-    near_bi = moved(cut(inputs, across), across)
+    send_bi = cut(inputs, across)
+    near_bi = moved(send_bi, across)
+    later_in, later_up = tie(inputs, *send_bi), tie(upstream, *send_bi)
+    here_hi, here_hu = to(later_in, 0)[None], to(later_up, 0)[None]
+    send_ci, send_cu, send_bu = cut(later_in, others), cut(later_up, others), cut(later_up, across)
     there_hi, there_hu = flip(here_hi, bits[0]), flip(here_hu, bits[0])
     weights = [qkv_weight, flip(qkv_weight, bits[-1])]
     near_bi, there_hi, there_hu, weights, send_ci, send_cu, send_bu = tie_all(
@@ -474,6 +479,10 @@
         arrived.append([])
         first.append(to_send(len(chains) - 1, 0) if send is None else send)
 
+    def prepare(c):
+        arrived[c][-1] = tie(arrived[c][-1], chains[-1][0])
+        first[c] = to_send(c, len(arrived[c]))
+
     def crossed_term(came, plus, also=None):
         window = (n, jnp.where(me == 0, 1, 0))
         term, send = outer(lent, [(came, 0)], 0, share, BF16, plus, window, also)
@@ -484,18 +493,13 @@
         step = len(arrived[c])
         if step == n - 1:
             return
-        send = to_send(c, step) if step else first[c]
+        send = to_send(c, step) if first[c] is None else first[c]
+        first[c] = None
         came = lax.ppermute(send, "ctx", [(step, step + 1), (n - 1 - step, n - 2 - step)])
         arrived[c].append(came if step else paced(came))
 
-    def ended(cs):
-        all_arrays, at = [], []
-        for c in cs:
-            all_arrays.append(chains[c] + arrived[c])
-            at += [me] * len(chains[c])
-            for step in range(n - 1):
-                at.append(jnp.where(me == step + 1, 0, n - 2 - step))
-        return finished(all_arrays, at)
+    def mine_of(step):
+        return jnp.where(me == step + 1, 0, n - 2 - step)
 
     for _ in bits[2:]:
         raise NotImplementedError
@@ -517,30 +521,34 @@
     back = {across[0]: shift(total([kept[n - 1], far_there]).astype(BF16), n - across[0])}
     mine = outer(tokens, grads[1:], me_dp, share, F32)
     crossed_term(tie(crossed, mine[0]), mine[0])
-    mid_there, back, home, kept, grads, mine, chains, arrived, first = tie_all(
-        mid_there, back, home, kept, grads, mine, chains, arrived, first
-    )
-
-    crossed = swap(grads[2][0])
-    home_there = flip(home, bits[0])
-    for c in range(2):
-        advance(c)
+    prepare(0)
+    mid_there = tie(mid_there, chains[-1][0])
     mid_sums = [
         total([kept[1 + i], mid_there[i * rows : (i + 1) * rows]]).astype(BF16)
         for i in range(n - 2)
     ]
+    mid_sums, back, home, kept, grads, mine, chains, arrived, first = tie_all(
+        mid_sums, back, home, kept, grads, mine, chains, arrived, first
+    )
+
+    crossed = swap(grads[2][0])
+    home_there = flip(home, bits[0])
+    for c in (1, 0):
+        advance(c)
     split = (n - 2) // 2
     for i, d in enumerate(others[:split]):
         back[d] = shift(mid_sums[i], n - d)
     (att,) = per_group(forward_kernel, slots, (q, k, tie(v, *mid_sums)), False)
     (proj_send,) = outer(ups, [(att, 0)], 1 - me_dp, share, BF16)
     crossed_term(tie(crossed, proj_send), mine[1])
+    if n > 3:
+        prepare(0)
     home_there, back, kept, mid_sums, att, proj_send, chains, arrived, first = tie_all(
         home_there, back, kept, mid_sums, att, proj_send, chains, arrived, first
     )
 
     crossed = swap(proj_send)
-    for c in range(3):
+    for c in (2, 1, 0):
         advance(c)
     for i, d in enumerate(others[split:], split):
         back[d] = shift(mid_sums[i], n - d)
@@ -549,19 +557,25 @@
     begin([proj_mine, crossed])
     back, chains, arrived, first = tie_all(back, chains, arrived, first)
 
-    for c in range(4):
+    for c in (3, 2, 1, 0):
         advance(c)
     where = lax.rem(jnp.arange(n, dtype=jnp.int32) + me, n)
     input_grad = placed_at([back[d] for d in range(n)], where)
     input_grad, chains, arrived = tie_all(input_grad, chains, arrived)
     for _ in range(n - 3):
-        for c in range(1, 4):
+        for c in (3, 2, 1):
             advance(c)
         input_grad, chains, arrived = tie_all(input_grad, chains, arrived)
     advance(3)
-    qkv_grad = ended(range(3))
-    arrived[3][-1] = tie(arrived[3][-1], qkv_grad)
-    return (input_grad.reshape(inputs.shape), qkv_grad, ended([3])[0])
+    arrays, at = [], []
+    for c in range(4):
+        came = arrived[c][: n - 1 if c < 3 else n - 2]
+        arrays.append(chains[c] + came)
+        at += [me] * len(chains[c]) + [mine_of(step) for step in range(len(came))]
+    qkv_grad, proj_grad = finished(arrays, at, [3, 1])
+    came = tie(arrived[3][-1], qkv_grad)
+    proj_grad = proj_grad[0] + lax.dynamic_index_in_dim(came, mine_of(n - 2), 0, keepdims=False).astype(F32)
+    return (input_grad.reshape(inputs.shape), qkv_grad, proj_grad)
 
 
 def solution(mesh):

time: 291 us -> 290 us (level)
  waiting for transfers between devices: 113 us -> 107 us
    ppermute x9, waiting for transfers between devices: 56.1 us -> 41.8 us  [shift(): return lax.ppermute(x, 'ctx', [(i, (i + d) % n) for i in range(n)])]
    ppermute x21, waiting for transfers between devices: 15.3 us -> 21.6 us  [flip(): return lax.ppermute(x, 'space', [(i, i ^ bit) for i in range(n_space)])]
    pallas_call x2 -> x1, Pallas kernels: 7.26 us -> 4.86 us  [finished(): pl.pallas_call(kernel, grid_spec=pltpu.PrefetchScalarGridSpec(num_scalar_...]
  transfers between devices with their start and end apart: 49 -> 49, of which waited for: 24 -> 24; matrix products, arithmetic and copies ran while one was open for 7% -> 8% of each run, Pallas kernels for 27% -> 27%
where the time goes in v4:
time: 290 us; the launch traced here: 289 us
  waiting for transfers between devices  107 us (37%)
  Pallas kernels  87.5 us (30%)
  starting transfers between devices  59.1 us (20%)
  other arithmetic  18.2 us (6%)
  local copies, waits for them, and re-layouts  15.6 us (5%)
    ppermute x9, waiting for transfers between devices, shift(): return lax.ppermute(x, 'ctx', [(i, (i + d) % n) for i in range(n)])  41.8 us
    pallas_call x6, Pallas kernels, outer(): pl.pallas_call(kernel, grid_spec=pltpu.PrefetchScalarGridSpec(num_scalar_...  40.5 us
    ppermute x12, waiting for transfers between devices, advance(): lax.ppermute(send, 'ctx', [(step, step + 1), (n - 1 - step, n - 2 - step)])  25.3 us
    ppermute x21, waiting for transfers between devices, flip(): return lax.ppermute(x, 'space', [(i, i ^ bit) for i in range(n_space)])  21.6 us
    ppermute x9, starting transfers between devices, shift(): return lax.ppermute(x, 'ctx', [(i, (i + d) % n) for i in range(n)])  19 us
    ppermute x12, starting transfers between devices, advance(): lax.ppermute(send, 'ctx', [(step, step + 1), (n - 1 - step, n - 2 - step)])  19 us
    ppermute x7, waiting for transfers between devices, swap(): return lax.ppermute(x, 'dp', [(0, 1), (1, 0)])  18 us
    pallas_call x3, Pallas kernels, project(): pl.pallas_call(kernel, grid=(count,), in_specs=[pl.BlockSpec((size, model...  17.4 us
  transfers between devices with their start and end apart: 49, of which 24 were waited for; matrix products, arithmetic and copies ran while one was open for 8% of the time, Pallas kernels for 27%

profile of v4, /device:TPU:0, one launch (start us, length us, event | category | flops | bytes accessed | tf_op | source)
XLA Modules:
  0.0 288.6 jit_solution(7015218203956963027)
XLA Ops:
  11.2 6.1 %collective-permute-done.2 = bf16[1,64,3072]{2,1,0:T(8,128)(2,1)} collective-permute-done((bf16[1,64,3072]{2,1,0:T(8,128)(2,1)S(1)}, bf16[1,64,3072]{2,1,0:T(8,128)(2,1)}, u32[]{:S(2)}, u32[]{:S(2)}) %collective-permute-start.2) | collective-permute-done | bytes 393248 | tf_op jit(solution)/shard_map/ppermute | solution.py:376
  17.4 8.1 %collective-permute-done.1 = bf16[1,64,3072]{2,1,0:T(8,128)(2,1)S(1)} collective-permute-done((bf16[1,64,3072]{2,1,0:T(8,128)(2,1)S(1)}, bf16[1,64,3072]{2,1,0:T(8,128)(2,1)S(1)}, u32[]{:S(2)}, u32[]{:S(2)}) %collective-permute-start.1) | collective-permute-done | bytes 393248 | tf_op jit(solution)/shard_map/ppermute | solution.py:376
  40.6 4.1 %collective-permute-done.4 = bf16[64,3072]{1,0:T(8,128)(2,1)S(1)} collective-permute-done((bf16[64,3072]{1,0:T(8,128)(2,1)}, bf16[64,3072]{1,0:T(8,128)(2,1)S(1)}, u32[]{:S(2)}, u32[]{:S(2)}) %collective-permute-start.4) | collective-permute-done | bytes 393248 | tf_op jit(solution)/shard_map/ppermute | solution.py:373
  44.7 6.0 %collective-permute-done.5 = bf16[64,3072]{1,0:T(8,128)(2,1)S(1)} collective-permute-done((bf16[64,3072]{1,0:T(8,128)(2,1)S(1)}, bf16[64,3072]{1,0:T(8,128)(2,1)S(1)}, u32[]{:S(2)}, u32[]{:S(2)}) %collective-permute-start.5) | collective-permute-done | bytes 393248 | tf_op jit(solution)/shard_map/ppermute | solution.py:373
  56.6 7.3 %collective-permute-done.12 = bf16[2,1,64,1536]{3,2,0,1:T(8,128)(2,1)S(1)} collective-permute-done((bf16[2,1,64,1536]{3,2,0,1:T(8,128)(2,1)S(1)}, bf16[2,1,64,1536]{3,2,0,1:T(8,128)(2,1)S(1)}, u32[]{:S(2)}, u32[]{:S(2)}) %collective-permute-start.12) | collective-permute-done | bytes 393248 | tf_op jit(solution)/shard_map/ppermute | solution.py:379
  66.1 8.3 %collective-permute-done.9 = bf16[64,3072]{1,0:T(8,128)(2,1)S(1)} collective-permute-done((bf16[64,3072]{1,0:T(8,128)(2,1)S(1)}, bf16[64,3072]{1,0:T(8,128)(2,1)S(1)}, u32[]{:S(2)}, u32[]{:S(2)}) %collective-permute-start.9) | collective-permute-done | bytes 393248 | tf_op jit(solution)/shard_map/ppermute | solution.py:373
  78.8 10.9 %shard_map.76 = (bf16[1024,384]{1,0:T(8,128)(2,1)S(1)}, bf16[1024,384]{1,0:T(8,128)(2,1)S(1)}, bf16[1024,384]{1,0:T(8,128)(2,1)S(1)}) custom-call(bf16[128,3072]{1,0:T(8,128)(2,1)S(1)} %bitcast.139, bf16[256,3072]{1,0:T(8,128)(2,1)S(1)} %bitcast.121, bf16[128,3072]{1,0:T(8,128)(2,1)S(1)} %bitcast.145, bf16[128,3072]{1,0:T(8,128)(2,1)S(1)} %bitcast.140, ...), custom_call_target="tpu_custom_call" | custom-call | flops 1 | bytes 1 | tf_op jit(solution)/shard_map/pallas_call | solution.py:161
  89.8 7.5 %collective-permute-done.14 = bf16[64,3072]{1,0:T(8,128)(2,1)S(1)} collective-permute-done((bf16[64,3072]{1,0:T(8,128)(2,1)S(1)}, bf16[64,3072]{1,0:T(8,128)(2,1)S(1)}, u32[]{:S(2)}, u32[]{:S(2)}) %collective-permute-start.14) | collective-permute-done | bytes 393248 | tf_op jit(solution)/shard_map/ppermute | solution.py:373
  116.9 4.6 %shard_map.79 = (bf16[4,4,64,384]{3,2,1,0:T(8,128)(2,1)S(1)}, bf16[4,4,64,384]{3,2,1,0:T(8,128)(2,1)S(1)}, bf16[4,4,64,384]{3,2,1,0:T(8,128)(2,1)S(1)}, bf16[3,2,4,64,384]{4,3,2,1,0:T(8,128)(2,1)S(1)}) custom-call(s32[4]{0:T(128)S(1)} %gather_fusion, bf16[4,4,64,384]{3,2,1,0:T(8,128)(2,1)S(1)} %bitcast.187, bf16[4,4,64,384]{3,2,1,0:T(8,128)(2,1)S(1)} %bitcast.189, ...), custom_call_target="tpu_custom_call" | custom-call | flops 1 | bytes 1 | tf_op jit(solution)/shard_map/pallas_call | solution.py:102
  127.3 14.2 %shard_map.80 = (bf16[64,3072]{1,0:T(8,128)(2,1)}, bf16[64,3072]{1,0:T(8,128)(2,1)}, bf16[64,3072]{1,0:T(8,128)(2,1)}, bf16[64,3072]{1,0:T(8,128)(2,1)}, bf16[64...) custom-call(bf16[1024,384]{1,0:T(8,128)(2,1)} %bitcast.181, bf16[1024,384]{1,0:T(8,128)(2,1)} %bitcast.185, ...), custom_call_target="tpu_custom_call" | custom-call | flops 1 | bytes 1 | tf_op jit(solution)/shard_map/pallas_call | solution.py:268
  144.2 8.7 %shard_map.81 = (bf16[1536,384]{1,0:T(8,128)(2,1)}, bf16[3,384,384]{2,1,0:T(8,128)(2,1)}) custom-call(s32[3]{0:T(128)} %pad_add_fusion.scalars_ref, bf16[128,1536]{1,0:T(8,128)(2,1)} %bitcast.199, bf16[256,1536]{1,0:T(8,128)(2,1)} %bitcast.53.refs_1_.refs_4_, bf16[128,1536]{1,0:T(8,128)(2,1)} %bitcast.205, bf16[128,1536]{1,0:T(8,128)(2,1)} %bitcast.200, ...), custom_call_target="tpu_custom_call" | custom-call | flops 1 | bytes 1 | tf_op jit(solution)/shard_map/pallas_call | solution.py:221
  159.9 7.6 %shard_map.82 = (f32[1536,384]{1,0:T(8,128)}, f32[1536,384]{1,0:T(8,128)}) custom-call(s32[3]{0:T(128)} %stack.136.scalars_ref, bf16[128,3072]{1,0:T(8,128)(2,1)} %bitcast.143, bf16[256,3072]{1,0:T(8,128)(2,1)} %bitcast.125, bf16[128,3072]{1,0:T(8,128)(2,1)} %bitcast.149, bf16[128,3072]{1,0:T(8,128)(2,1)} %bitcast.144, bf16[256,3072]{1,0:T(8,128)(2,1)} %bitcast.126, ...), custom_call_target="tpu_custom_call" | custom-call | flops 1 | bytes 1 | tf_op jit(solution)/shard_map/pallas_call | solution.py:221
  167.5 4.8 %collective-permute-done.30 = bf16[4,4,64,384]{3,2,1,0:T(8,128)(2,1)S(1)} collective-permute-done((bf16[4,4,64,384]{3,2,1,0:T(8,128)(2,1)S(1)}, bf16[4,4,64,384]{3,2,1,0:T(8,128)(2,1)S(1)}, u32[]{:S(2)}, u32[]{:S(2)}) %collective-permute-start.30) | collective-permute-done | bytes 786464 | tf_op jit(solution)/shard_map/ppermute | solution.py:379
  173.1 6.4 %shard_map.83 = (bf16[1536,384]{1,0:T(8,128)(2,1)}, bf16[3,384,384]{2,1,0:T(8,128)(2,1)}) custom-call(s32[3]{0:T(128)} %pad_add_fusion.2.scalars_ref, bf16[128,1536]{1,0:T(8,128)(2,1)} %bitcast.201, bf16[256,1536]{1,0:T(8,128)(2,1)} %bitcast.67.refs_1_, bf16[128,1536]{1,0:T(8,128)(2,1)} %bitcast.207, bf16[128,1536]{1,0:T(8,128)(2,1)} %bitcast.202, ...), custom_call_target="tpu_custom_call" | custom-call | flops 1 | bytes 1 | tf_op jit(solution)/shard_map/pallas_call | solution.py:221
  185.6 5.2 %collective-permute-start.37 = (bf16[3,384,384]{2,1,0:T(8,128)(2,1)}, bf16[3,384,384]{2,1,0:T(8,128)(2,1)}, u32[]{:S(2)}, u32[]{:S(2)}) collective-permute-start(bf16[3,384,384]{2,1,0:T(8,128)(2,1)} %get-tuple-element.332), channel_id=1, source_target_pairs={{0,4},{12,8},{1,5},{13,9},{2,6},{14,10},{3,7},{15,11},{16,20},{28,... | collective-permute-start | bytes 2654216 | tf_op jit(solution)/shard_map/ppermute | solution.py:498
  199.6 5.5 %shard_map.85 = bf16[1536,384]{1,0:T(8,128)(2,1)} custom-call(s32[3]{0:T(128)} %stack.138.scalars_ref, bf16[128,3072]{1,0:T(8,128)(2,1)} %bitcast.153, bf16[256,3072]{1,0:T(8,128)(2,1)} %bitcast.117, bf16[64,3072]{1,0:T(8,128)(2,1)} %copy-done.36, bf16[128,3072]{1,0:T(8,128)(2,1)} %bitcast.154, bf16[256,3072]{1,0:T(8,128)(2,1)} %bitcast.118, ...), custom_call_target="tpu_custom_call" | custom-call | flops 1 | bytes 1 | tf_op jit(solution)/shard_map/pallas_call | solution.py:221
  205.2 6.5 %shard_map.86 = (bf16[1536,384]{1,0:T(8,128)(2,1)}, bf16[3,384,384]{2,1,0:T(8,128)(2,1)}) custom-call(s32[3]{0:T(128)} %pad_add_fusion.2.scalars_ref, bf16[128,1536]{1,0:T(8,128)(2,1)} %bitcast.203, bf16[256,1536]{1,0:T(8,128)(2,1)} %bitcast.67.refs_1_, bf16[128,1536]{1,0:T(8,128)(2,1)} %bitcast.209, bf16[128,1536]{1,0:T(8,128)(2,1)} %bitcast.204, ...), custom_call_target="tpu_custom_call" | custom-call | flops 1 | bytes 1 | tf_op jit(solution)/shard_map/pallas_call | solution.py:221
  220.6 4.7 %collective-permute-start.38 = (bf16[64,3072]{1,0:T(8,128)(2,1)}, bf16[64,3072]{1,0:T(8,128)(2,1)S(1)}, u32[]{:S(2)}, u32[]{:S(2)}) collective-permute-start(bf16[64,3072]{1,0:T(8,128)(2,1)} %get-tuple-element.338), channel_id=1, source_target_pairs={{0,4},{4,8},{8,12},{12,0},{1,5},{5,9},{9,13},{13,1},{2,6},{6,10},{... | collective-permute-start | bytes 1179656 | tf_op jit(solution)/shard_map/ppermute | solution.py:373
  227.7 5.8 %shard_map.87 = f32[1536,384]{1,0:T(8,128)} custom-call(s32[3]{0:T(128)} %stack.136.scalars_ref, bf16[128,3072]{1,0:T(8,128)(2,1)} %bitcast.155, bf16[256,3072]{1,0:T(8,128)(2,1)} %bitcast.119, bf16[64,3072]{1,0:T(8,128)(2,1)} %copy-done.36, bf16[128,3072]{1,0:T(8,128)(2,1)} %bitcast.156, bf16[256,3072]{1,0:T(8,128)(2,1)} %bitcast.120, ...), custom_call_target="tpu_custom_call" | custom-call | flops 1 | bytes 1 | tf_op jit(solution)/shard_map/pallas_call | solution.py:221
  233.5 4.8 %collective-permute-done.42.refs_9_ = bf16[3,384,384]{2,1,0:T(8,128)(2,1)S(1)} collective-permute-done((bf16[3,384,384]{2,1,0:T(8,128)(2,1)}, bf16[3,384,384]{2,1,0:T(8,128)(2,1)S(1)}, u32[]{:S(2)}, u32[]{:S(2)}) %collective-permute-start.42) | collective-permute-done | bytes 884768 | tf_op jit(solution)/shard_map/ppermute | solution.py:498
  242.8 6.3 %collective-permute-done.38.refs_3_ = bf16[64,3072]{1,0:T(8,128)(2,1)S(1)} collective-permute-done((bf16[64,3072]{1,0:T(8,128)(2,1)}, bf16[64,3072]{1,0:T(8,128)(2,1)S(1)}, u32[]{:S(2)}, u32[]{:S(2)}) %collective-permute-start.38) | collective-permute-done | bytes 393248 | tf_op jit(solution)/shard_map/ppermute | solution.py:373
  256.1 8.3 %collective-permute-done.45.refs_14_ = bf16[3,384,384]{2,1,0:T(8,128)(2,1)S(1)} collective-permute-done((bf16[3,384,384]{2,1,0:T(8,128)(2,1)S(1)}, bf16[3,384,384]{2,1,0:T(8,128)(2,1)S(1)}, u32[]{:S(2)}, u32[]{:S(2)}) %collective-permute-start.45) | collective-permute-done | bytes 884768 | tf_op jit(solution)/shard_map/ppermute | solution.py:498
  267.5 9.4 %collective-permute-done.46.refs_11_ = bf16[1,384,384]{2,1,0:T(8,128)(2,1)S(1)} collective-permute-done((bf16[1,384,384]{2,1,0:T(8,128)(2,1)S(1)}, bf16[1,384,384]{2,1,0:T(8,128)(2,1)S(1)}, u32[]{:S(2)}, u32[]{:S(2)}) %collective-permute-start.46) | collective-permute-done | bytes 294944 | tf_op jit(solution)/shard_map/ppermute | solution.py:498
  279.0 4.9 %shard_map.89 = (f32[3,384,384]{2,1,0:T(8,128)}, f32[1,384,384]{2,1,0:T(8,128)}) custom-call(s32[16]{0:T(128)} %stack.142.at_ref, bf16[4,384,384]{2,1,0:T(8,128)(2,1)} %bitcast.222, bf16[3,384,384]{2,1,0:T(8,128)(2,1)} %copy-done.39, bf16[2,384,384]{2,1,0:T(8,128)(2,1)} %collective-permute-done.36.refs_2_, ...), custom_call_target="tpu_custom_call" | custom-call | flops 1 | bytes 1 | tf_op jit(solution)/shard_map/pallas_call | solution.py:318
  (246 shorter events, 121.2 us)
Async XLA Ops:
  0.6 28.2 %collective-permute-start.3 = (bf16[3,3072,384]{2,1,0:T(8,128)(2,1)}, bf16[3,3072,384]{2,1,0:T(8,128)(2,1)}, u32[]{:S(2)}, u32[]{:S(2)}) collective-permute-start(bf16[3,3072,384]{2,1,0:T(8,128)(2,1)} %refs_4_), channel_id=1, source_target_pairs={{0,1},{1,0},{2,3},{3,2},{4,5},{5,4},{6,7},{7,6},{8,9},{9,8},{10,11... | collective-permute-start | bytes 21233672 | tf_op jit(solution)/shard_map/ppermute | solution.py:376
  8.1 20.7 %collective-permute-start = (bf16[64,3072]{1,0:T(8,128)(2,1)S(1)}, bf16[64,3072]{1,0:T(8,128)(2,1)S(1)}, u32[]{:S(2)}, u32[]{:S(2)}) collective-permute-start(bf16[64,3072]{1,0:T(8,128)(2,1)S(1)} %dynamic-slice_bitcast_fusion.5), channel_id=1, source_target_pairs={{0,8},{4,12},{8,0},{12,4},{1,9},{5,13},{9,1},{13,5},{2,10},{6,14},... | collective-permute-start | bytes 1179656 | tf_op jit(solution)/shard_map/ppermute | solution.py:373
  28.9 21.8 %collective-permute-start.8 = (bf16[2,1,64,3072]{3,2,1,0:T(8,128)(2,1)S(1)}, bf16[2,1,64,3072]{3,2,1,0:T(8,128)(2,1)S(1)}, u32[]{:S(2)}, u32[]{:S(2)}) collective-permute-start(bf16[2,1,64,3072]{3,2,1,0:T(8,128)(2,1)S(1)} %pad_maximum_fusion.2), channel_id=1, source_target_pairs={{0,1},{1,0},{2,3},{3,2},{4,5},{5,4},{6,7},{7,6},{8,9},{9,8},{10,11... | collective-permute-start | bytes 2359304 | tf_op jit(solution)/shard_map/ppermute | solution.py:376
  31.3 19.4 %collective-permute-start.5 = (bf16[64,3072]{1,0:T(8,128)(2,1)S(1)}, bf16[64,3072]{1,0:T(8,128)(2,1)S(1)}, u32[]{:S(2)}, u32[]{:S(2)}) collective-permute-start(bf16[64,3072]{1,0:T(8,128)(2,1)S(1)} %get-tuple-element.205), channel_id=1, source_target_pairs={{0,12},{4,0},{8,4},{12,8},{1,13},{5,1},{9,5},{13,9},{2,14},{6,2},{... | collective-permute-start | bytes 1179656 | tf_op jit(solution)/shard_map/ppermute | solution.py:373
  50.8 23.5 %collective-permute-start.13 = (bf16[2,1,64,3072]{3,2,0,1:T(8,128)(2,1)S(1)}, bf16[2,1,64,3072]{3,2,0,1:T(8,128)(2,1)S(1)}, u32[]{:S(2)}, u32[]{:S(2)}) collective-permute-start(bf16[2,1,64,3072]{3,2,0,1:T(8,128)(2,1)S(1)} %pad_maximum_fusion.3), channel_id=1, source_target_pairs={{0,1},{1,0},{2,3},{3,2},{4,5},{5,4},{6,7},{7,6},{8,9},{9,8},{10,11... | collective-permute-start | bytes 2359304 | tf_op jit(solution)/shard_map/ppermute | solution.py:376
  51.0 23.3 %collective-permute-start.11 = (bf16[2,64,3072]{2,1,0:T(8,128)(2,1)S(1)}, bf16[2,64,3072]{2,1,0:T(8,128)(2,1)S(1)}, u32[]{:S(2)}, u32[]{:S(2)}) collective-permute-start(bf16[2,64,3072]{2,1,0:T(8,128)(2,1)S(1)} %get-tuple-element.419), channel_id=1, source_target_pairs={{0,2},{1,3},{2,0},{3,1},{4,6},{5,7},{6,4},{7,5},{8,10},{9,11},{10,... | collective-permute-start | bytes 2359304 | tf_op jit(solution)/shard_map/ppermute | solution.py:376
  74.7 22.6 %collective-permute-start.16 = (bf16[2,2,64,1536]{3,2,1,0:T(8,128)(2,1)S(1)}, bf16[2,2,64,1536]{3,2,1,0:T(8,128)(2,1)}, u32[]{:S(2)}, u32[]{:S(2)}) collective-permute-start(bf16[2,2,64,1536]{3,2,1,0:T(8,128)(2,1)S(1)} %fusion), channel_id=1, source_target_pairs={{0,16},{16,0},{1,17},{17,1},{2,18},{18,2},{3,19},{19,3},{4,20},{20... | collective-permute-start | bytes 2359304 | tf_op jit(solution)/shard_map/ppermute | solution.py:379
  76.3 21.0 %collective-permute-start.15 = (bf16[2,64,3072]{2,1,0:T(8,128)(2,1)S(1)}, bf16[2,64,3072]{2,1,0:T(8,128)(2,1)S(1)}, u32[]{:S(2)}, u32[]{:S(2)}) collective-permute-start(bf16[2,64,3072]{2,1,0:T(8,128)(2,1)S(1)} %get-tuple-element.417), channel_id=1, source_target_pairs={{0,2},{1,3},{2,0},{3,1},{4,6},{5,7},{6,4},{7,5},{8,10},{9,11},{10,... | collective-permute-start | bytes 2359304 | tf_op jit(solution)/shard_map/ppermute | solution.py:376
  77.0 20.3 %collective-permute-start.14 = (bf16[64,3072]{1,0:T(8,128)(2,1)S(1)}, bf16[64,3072]{1,0:T(8,128)(2,1)S(1)}, u32[]{:S(2)}, u32[]{:S(2)}) collective-permute-start(bf16[64,3072]{1,0:T(8,128)(2,1)S(1)} %copy-done.53), channel_id=1, source_target_pairs={{0,8},{4,12},{8,0},{12,4},{1,9},{5,13},{9,1},{13,5},{2,10},{6,14},... | collective-permute-start | bytes 1179656 | tf_op jit(solution)/shard_map/ppermute | solution.py:373
  123.5 20.6 %collective-permute-start.26 = (bf16[4,4,64,384]{3,2,1,0:T(8,128)(2,1)S(1)}, bf16[4,4,64,384]{3,2,1,0:T(8,128)(2,1)}, u32[]{:S(2)}, u32[]{:S(2)}) collective-permute-start(bf16[4,4,64,384]{3,2,1,0:T(8,128)(2,1)S(1)} %get-tuple-element.263), channel_id=1, source_target_pairs={{0,16},{16,0},{1,17},{17,1},{2,18},{18,2},{3,19},{19,3},{4,20},{20... | collective-permute-start | bytes 2359304 | tf_op jit(solution)/shard_map/ppermute | solution.py:379
  124.8 19.3 %collective-permute-start.24 = (bf16[2,2,64,1536]{3,2,1,0:T(8,128)(2,1)}, bf16[2,2,64,1536]{3,2,1,0:T(8,128)(2,1)}, u32[]{:S(2)}, u32[]{:S(2)}) collective-permute-start(bf16[2,2,64,1536]{3,2,1,0:T(8,128)(2,1)} %collective-permute-done.16), channel_id=1, source_target_pairs={{0,1},{1,0},{2,3},{3,2},{4,5},{5,4},{6,7},{7,6},{8,9},{9,8},{10,11... | collective-permute-start | bytes 2359304 | tf_op jit(solution)/shard_map/ppermute | solution.py:376
  153.0 19.2 %collective-permute-start.30 = (bf16[4,4,64,384]{3,2,1,0:T(8,128)(2,1)S(1)}, bf16[4,4,64,384]{3,2,1,0:T(8,128)(2,1)S(1)}, u32[]{:S(2)}, u32[]{:S(2)}) collective-permute-start(bf16[4,4,64,384]{3,2,1,0:T(8,128)(2,1)S(1)} %copy-done.16), channel_id=1, source_target_pairs={{0,16},{16,0},{1,17},{17,1},{2,18},{18,2},{3,19},{19,3},{4,20},{20... | collective-permute-start | bytes 2359304 | tf_op jit(solution)/shard_map/ppermute | solution.py:379
  154.3 25.2 %collective-permute-start.29 = (bf16[128,3072]{1,0:T(8,128)(2,1)S(1)}, bf16[128,3072]{1,0:T(8,128)(2,1)}, u32[]{:S(2)}, u32[]{:S(2)}) collective-permute-start(bf16[128,3072]{1,0:T(8,128)(2,1)S(1)} %copy-done.58), channel_id=1, source_target_pairs={{0,2},{1,3},{2,0},{3,1},{4,6},{5,7},{6,4},{7,5},{8,10},{9,11},{10,... | collective-permute-start | bytes 2359304 | tf_op jit(solution)/shard_map/ppermute | solution.py:376
  155.7 26.3 %collective-permute-start.32 = (bf16[3,384,384]{2,1,0:T(8,128)(2,1)}, bf16[3,384,384]{2,1,0:T(8,128)(2,1)S(1)}, u32[]{:S(2)}, u32[]{:S(2)}) collective-permute-start(bf16[3,384,384]{2,1,0:T(8,128)(2,1)} %get-tuple-element.306), channel_id=1, source_target_pairs={{0,4},{12,8},{1,5},{13,9},{2,6},{14,10},{3,7},{15,11},{16,20},{28,... | collective-permute-start | bytes 2654216 | tf_op jit(solution)/shard_map/ppermute | solution.py:498
  159.9 24.5 %collective-permute-start.31 = (bf16[64,3072]{1,0:T(8,128)(2,1)}, bf16[64,3072]{1,0:T(8,128)(2,1)S(1)}, u32[]{:S(2)}, u32[]{:S(2)}) collective-permute-start(bf16[64,3072]{1,0:T(8,128)(2,1)} %add_convert_fusion.6), channel_id=1, source_target_pairs={{0,8},{4,12},{8,0},{12,4},{1,9},{5,13},{9,1},{13,5},{2,10},{6,14},... | collective-permute-start | bytes 1179656 | tf_op jit(solution)/shard_map/ppermute | solution.py:373
  184.4 20.8 %collective-permute-start.35 = (bf16[4,4,64,384]{3,2,1,0:T(8,128)(2,1)S(1)}, bf16[4,4,64,384]{3,2,1,0:T(8,128)(2,1)}, u32[]{:S(2)}, u32[]{:S(2)}) collective-permute-start(bf16[4,4,64,384]{3,2,1,0:T(8,128)(2,1)S(1)} %copy-done.14), channel_id=1, source_target_pairs={{0,16},{16,0},{1,17},{17,1},{2,18},{18,2},{3,19},{19,3},{4,20},{20... | collective-permute-start | bytes 2359304 | tf_op jit(solution)/shard_map/ppermute | solution.py:379
  185.6 28.0 %collective-permute-start.37 = (bf16[3,384,384]{2,1,0:T(8,128)(2,1)}, bf16[3,384,384]{2,1,0:T(8,128)(2,1)}, u32[]{:S(2)}, u32[]{:S(2)}) collective-permute-start(bf16[3,384,384]{2,1,0:T(8,128)(2,1)} %get-tuple-element.332), channel_id=1, source_target_pairs={{0,4},{12,8},{1,5},{13,9},{2,6},{14,10},{3,7},{15,11},{16,20},{28,... | collective-permute-start | bytes 2654216 | tf_op jit(solution)/shard_map/ppermute | solution.py:498
  190.9 20.8 %collective-permute-start.36 = (bf16[2,384,384]{2,1,0:T(8,128)(2,1)}, bf16[2,384,384]{2,1,0:T(8,128)(2,1)}, u32[]{:S(2)}, u32[]{:S(2)}) collective-permute-start(bf16[2,384,384]{2,1,0:T(8,128)(2,1)} %add_convert_fusion.4), channel_id=1, source_target_pairs={{4,8},{8,4},{5,9},{9,5},{6,10},{10,6},{7,11},{11,7},{20,24},{24,20... | collective-permute-start | bytes 1769480 | tf_op jit(solution)/shard_map/ppermute | solution.py:498
  192.4 21.2 %collective-permute-start.33 = (bf16[64,3072]{1,0:T(8,128)(2,1)}, bf16[64,3072]{1,0:T(8,128)(2,1)}, u32[]{:S(2)}, u32[]{:S(2)}) collective-permute-start(bf16[64,3072]{1,0:T(8,128)(2,1)} %get-tuple-element.309), channel_id=1, source_target_pairs={{0,2},{1,3},{2,0},{3,1},{4,6},{5,7},{6,4},{7,5},{8,10},{9,11},{10,... | collective-permute-start | bytes 1179656 | tf_op jit(solution)/shard_map/ppermute | solution.py:376
  193.3 23.2 %collective-permute-start.34 = (bf16[64,3072]{1,0:T(8,128)(2,1)}, bf16[64,3072]{1,0:T(8,128)(2,1)}, u32[]{:S(2)}, u32[]{:S(2)}) collective-permute-start(bf16[64,3072]{1,0:T(8,128)(2,1)} %get-tuple-element.310), channel_id=1, source_target_pairs={{0,12},{4,0},{8,4},{12,8},{1,13},{5,1},{9,5},{13,9},{2,14},{6,2},{... | collective-permute-start | bytes 1179656 | tf_op jit(solution)/shard_map/ppermute | solution.py:373
  216.5 24.0 %collective-permute-start.39 = (bf16[1536,384]{1,0:T(8,128)(2,1)S(1)}, bf16[1536,384]{1,0:T(8,128)(2,1)S(1)}, u32[]{:S(2)}, u32[]{:S(2)}) collective-permute-start(bf16[1536,384]{1,0:T(8,128)(2,1)S(1)} %copy-done.46), channel_id=1, source_target_pairs={{0,16},{16,0},{1,17},{17,1},{2,18},{18,2},{3,19},{19,3},{4,20},{20... | collective-permute-start | bytes 3538952 | tf_op jit(solution)/shard_map/ppermute | solution.py:379
  216.5 21.7 %collective-permute-start.42 = (bf16[3,384,384]{2,1,0:T(8,128)(2,1)}, bf16[3,384,384]{2,1,0:T(8,128)(2,1)S(1)}, u32[]{:S(2)}, u32[]{:S(2)}) collective-permute-start(bf16[3,384,384]{2,1,0:T(8,128)(2,1)} %get-tuple-element.349), channel_id=1, source_target_pairs={{0,4},{12,8},{1,5},{13,9},{2,6},{14,10},{3,7},{15,11},{16,20},{28,... | collective-permute-start | bytes 2654216 | tf_op jit(solution)/shard_map/ppermute | solution.py:498
  219.9 29.1 %collective-permute-start.41 = (bf16[2,384,384]{2,1,0:T(8,128)(2,1)}, bf16[2,384,384]{2,1,0:T(8,128)(2,1)S(1)}, u32[]{:S(2)}, u32[]{:S(2)}) collective-permute-start(bf16[2,384,384]{2,1,0:T(8,128)(2,1)} %add_convert_fusion.3), channel_id=1, source_target_pairs={{4,8},{8,4},{5,9},{9,5},{6,10},{10,6},{7,11},{11,7},{20,24},{24,20... | collective-permute-start | bytes 1769480 | tf_op jit(solution)/shard_map/ppermute | solution.py:498
  220.6 28.4 %collective-permute-start.38 = (bf16[64,3072]{1,0:T(8,128)(2,1)}, bf16[64,3072]{1,0:T(8,128)(2,1)S(1)}, u32[]{:S(2)}, u32[]{:S(2)}) collective-permute-start(bf16[64,3072]{1,0:T(8,128)(2,1)} %get-tuple-element.338), channel_id=1, source_target_pairs={{0,4},{4,8},{8,12},{12,0},{1,5},{5,9},{9,13},{13,1},{2,6},{6,10},{... | collective-permute-start | bytes 1179656 | tf_op jit(solution)/shard_map/ppermute | solution.py:373
  (86 other events, 858.6 us)

commit v5 on v4

--- a/solution.py
+++ b/solution.py
@@ -400,7 +400,7 @@
         return [shift(p, d) for p, d in zip(pieces, ds)]
 
     send_bi = cut(inputs, across)
-    near_bi = moved(send_bi, across)
+    near_bi = [paced(p[None])[0] for p in moved(send_bi, across)]
     later_in, later_up = tie(inputs, *send_bi), tie(upstream, *send_bi)
     here_hi, here_hu = to(later_in, 0)[None], to(later_up, 0)[None]
     send_ci, send_cu, send_bu = cut(later_in, others), cut(later_up, others), cut(later_up, across)
@@ -496,7 +496,7 @@
         send = to_send(c, step) if first[c] is None else first[c]
         first[c] = None
         came = lax.ppermute(send, "ctx", [(step, step + 1), (n - 1 - step, n - 2 - step)])
-        arrived[c].append(came if step else paced(came))
+        arrived[c].append(paced(came))
 
     def mine_of(step):
         return jnp.where(me == step + 1, 0, n - 2 - step)

time: 290 us -> 288 us (level)
    ppermute x21, waiting for transfers between devices: 21.6 us -> 11.5 us  [flip(): return lax.ppermute(x, 'space', [(i, i ^ bit) for i in range(n_space)])]
    ppermute x9, waiting for transfers between devices: 41.8 us -> 50.9 us  [shift(): return lax.ppermute(x, 'ctx', [(i, (i + d) % n) for i in range(n)])]
  transfers between devices with their start and end apart: 49 -> 49, of which waited for: 24 -> 25; matrix products, arithmetic and copies ran while one was open for 8% -> 8% of each run, Pallas kernels for 27% -> 28%
where the time goes in v5:
time: 288 us; the launch traced here: 287 us
  waiting for transfers between devices  106 us (37%)
  Pallas kernels  87.5 us (30%)
  starting transfers between devices  58.4 us (20%)
  other arithmetic  18.2 us (6%)
  local copies, waits for them, and re-layouts  15.7 us (5%)
    ppermute x9, waiting for transfers between devices, shift(): return lax.ppermute(x, 'ctx', [(i, (i + d) % n) for i in range(n)])  50.9 us
    pallas_call x6, Pallas kernels, outer(): pl.pallas_call(kernel, grid_spec=pltpu.PrefetchScalarGridSpec(num_scalar_...  40.5 us
    ppermute x12, waiting for transfers between devices, advance(): lax.ppermute(send, 'ctx', [(step, step + 1), (n - 1 - step, n - 2 - step)])  25 us
    ppermute x12, starting transfers between devices, advance(): lax.ppermute(send, 'ctx', [(step, step + 1), (n - 1 - step, n - 2 - step)])  19.2 us
    ppermute x7, waiting for transfers between devices, swap(): return lax.ppermute(x, 'dp', [(0, 1), (1, 0)])  18.3 us
    pallas_call x3, Pallas kernels, project(): pl.pallas_call(kernel, grid=(count,), in_specs=[pl.BlockSpec((size, model...  17.4 us
    ppermute x9, starting transfers between devices, shift(): return lax.ppermute(x, 'ctx', [(i, (i + d) % n) for i in range(n)])  16.6 us
    pallas_call x1, Pallas kernels, backproject(): pl.pallas_call(kernel, grid=(model // wide,), in_specs=[pl.BlockSpec((row...  14.2 us
  transfers between devices with their start and end apart: 49, of which 25 were waited for; matrix products, arithmetic and copies ran while one was open for 8% of the time, Pallas kernels for 28%

profile of v5, /device:TPU:0, one launch (start us, length us, event | category | flops | bytes accessed | tf_op | source)
XLA Modules:
  0.0 286.9 jit_solution(12316073772919445195)
XLA Ops:
  11.2 12.8 %collective-permute-done = bf16[64,3072]{1,0:T(8,128)(2,1)S(1)} collective-permute-done((bf16[64,3072]{1,0:T(8,128)(2,1)S(1)}, bf16[64,3072]{1,0:T(8,128)(2,1)S(1)}, u32[]{:S(2)}, u32[]{:S(2)}) %collective-permute-start) | collective-permute-done | bytes 393248 | tf_op jit(solution)/shard_map/ppermute | solution.py:373
  24.0 4.0 %collective-permute-done.1 = bf16[1,64,3072]{2,1,0:T(8,128)(2,1)S(1)} collective-permute-done((bf16[1,64,3072]{2,1,0:T(8,128)(2,1)S(1)}, bf16[1,64,3072]{2,1,0:T(8,128)(2,1)S(1)}, u32[]{:S(2)}, u32[]{:S(2)}) %collective-permute-start.1) | collective-permute-done | bytes 393248 | tf_op jit(solution)/shard_map/ppermute | solution.py:376
  39.8 4.0 %collective-permute-done.4 = bf16[64,3072]{1,0:T(8,128)(2,1)S(1)} collective-permute-done((bf16[64,3072]{1,0:T(8,128)(2,1)}, bf16[64,3072]{1,0:T(8,128)(2,1)S(1)}, u32[]{:S(2)}, u32[]{:S(2)}) %collective-permute-start.4) | collective-permute-done | bytes 393248 | tf_op jit(solution)/shard_map/ppermute | solution.py:373
  43.8 6.9 %collective-permute-done.5 = bf16[64,3072]{1,0:T(8,128)(2,1)S(1)} collective-permute-done((bf16[64,3072]{1,0:T(8,128)(2,1)S(1)}, bf16[64,3072]{1,0:T(8,128)(2,1)S(1)}, u32[]{:S(2)}, u32[]{:S(2)}) %collective-permute-start.5) | collective-permute-done | bytes 393248 | tf_op jit(solution)/shard_map/ppermute | solution.py:373
  55.6 8.4 %collective-permute-done.12 = bf16[2,1,64,1536]{3,2,0,1:T(8,128)(2,1)S(1)} collective-permute-done((bf16[2,1,64,1536]{3,2,0,1:T(8,128)(2,1)S(1)}, bf16[2,1,64,1536]{3,2,0,1:T(8,128)(2,1)S(1)}, u32[]{:S(2)}, u32[]{:S(2)}) %collective-permute-start.12) | collective-permute-done | bytes 393248 | tf_op jit(solution)/shard_map/ppermute | solution.py:379
  65.1 8.3 %collective-permute-done.9 = bf16[64,3072]{1,0:T(8,128)(2,1)S(1)} collective-permute-done((bf16[64,3072]{1,0:T(8,128)(2,1)S(1)}, bf16[64,3072]{1,0:T(8,128)(2,1)S(1)}, u32[]{:S(2)}, u32[]{:S(2)}) %collective-permute-start.9) | collective-permute-done | bytes 393248 | tf_op jit(solution)/shard_map/ppermute | solution.py:373
  77.1 10.9 %shard_map.76 = (bf16[1024,384]{1,0:T(8,128)(2,1)S(1)}, bf16[1024,384]{1,0:T(8,128)(2,1)S(1)}, bf16[1024,384]{1,0:T(8,128)(2,1)S(1)}) custom-call(bf16[128,3072]{1,0:T(8,128)(2,1)S(1)} %bitcast.141, bf16[256,3072]{1,0:T(8,128)(2,1)S(1)} %bitcast.123, bf16[128,3072]{1,0:T(8,128)(2,1)S(1)} %bitcast.147, bf16[128,3072]{1,0:T(8,128)(2,1)S(1)} %bitcast.142, ...), custom_call_target="tpu_custom_call" | custom-call | flops 1 | bytes 1 | tf_op jit(solution)/shard_map/pallas_call | solution.py:161
  88.1 8.2 %collective-permute-done.14 = bf16[64,3072]{1,0:T(8,128)(2,1)S(1)} collective-permute-done((bf16[64,3072]{1,0:T(8,128)(2,1)S(1)}, bf16[64,3072]{1,0:T(8,128)(2,1)S(1)}, u32[]{:S(2)}, u32[]{:S(2)}) %collective-permute-start.14) | collective-permute-done | bytes 393248 | tf_op jit(solution)/shard_map/ppermute | solution.py:373
  111.1 3.9 %shard_map.78 = bf16[256,384]{1,0:T(8,128)(2,1)} custom-call(bf16[64,3072]{1,0:T(8,128)(2,1)} %copy-done.36, bf16[64,3072]{1,0:T(8,128)(2,1)} %bitcast.47.refs_1_.refs_5_, bf16[64,3072]{1,0:T(8,128)(2,1)} %bitcast.234, bf16[64,3072]{1,0:T(8,128)(2,1)} %bitcast.237, bf16[1,3072,384]{2,1,0:T(8,128)(2,1)} %bitcast.179), custom_call_target="tpu_custom_call" | custom-call | flops 1 | bytes 1 | tf_op jit(solution)/shard_map/pallas_call | solution.py:161
  116.0 4.6 %shard_map.79 = (bf16[4,4,64,384]{3,2,1,0:T(8,128)(2,1)S(1)}, bf16[4,4,64,384]{3,2,1,0:T(8,128)(2,1)S(1)}, bf16[4,4,64,384]{3,2,1,0:T(8,128)(2,1)S(1)}, bf16[3,2,4,64,384]{4,3,2,1,0:T(8,128)(2,1)S(1)}) custom-call(s32[4]{0:T(128)S(1)} %gather_fusion, bf16[4,4,64,384]{3,2,1,0:T(8,128)(2,1)S(1)} %bitcast.189, bf16[4,4,64,384]{3,2,1,0:T(8,128)(2,1)S(1)} %bitcast.191, ...), custom_call_target="tpu_custom_call" | custom-call | flops 1 | bytes 1 | tf_op jit(solution)/shard_map/pallas_call | solution.py:102
  126.4 14.2 %shard_map.80 = (bf16[64,3072]{1,0:T(8,128)(2,1)}, bf16[64,3072]{1,0:T(8,128)(2,1)}, bf16[64,3072]{1,0:T(8,128)(2,1)}, bf16[64,3072]{1,0:T(8,128)(2,1)}, bf16[64...) custom-call(bf16[1024,384]{1,0:T(8,128)(2,1)} %bitcast.183, bf16[1024,384]{1,0:T(8,128)(2,1)} %bitcast.187, ...), custom_call_target="tpu_custom_call" | custom-call | flops 1 | bytes 1 | tf_op jit(solution)/shard_map/pallas_call | solution.py:268
  143.3 8.7 %shard_map.81 = (bf16[1536,384]{1,0:T(8,128)(2,1)}, bf16[3,384,384]{2,1,0:T(8,128)(2,1)}) custom-call(s32[3]{0:T(128)} %pad_add_fusion.scalars_ref, bf16[128,1536]{1,0:T(8,128)(2,1)} %bitcast.201, bf16[256,1536]{1,0:T(8,128)(2,1)} %bitcast.55.refs_1_.refs_4_, bf16[128,1536]{1,0:T(8,128)(2,1)} %bitcast.207, bf16[128,1536]{1,0:T(8,128)(2,1)} %bitcast.202, ...), custom_call_target="tpu_custom_call" | custom-call | flops 1 | bytes 1 | tf_op jit(solution)/shard_map/pallas_call | solution.py:221
  158.9 7.6 %shard_map.82 = (f32[1536,384]{1,0:T(8,128)}, f32[1536,384]{1,0:T(8,128)}) custom-call(s32[3]{0:T(128)} %stack.136.scalars_ref, bf16[128,3072]{1,0:T(8,128)(2,1)} %bitcast.145, bf16[256,3072]{1,0:T(8,128)(2,1)} %bitcast.127, bf16[128,3072]{1,0:T(8,128)(2,1)} %bitcast.151, bf16[128,3072]{1,0:T(8,128)(2,1)} %bitcast.146, bf16[256,3072]{1,0:T(8,128)(2,1)} %bitcast.128, ...), custom_call_target="tpu_custom_call" | custom-call | flops 1 | bytes 1 | tf_op jit(solution)/shard_map/pallas_call | solution.py:221
  166.5 4.9 %collective-permute-done.30 = bf16[4,4,64,384]{3,2,1,0:T(8,128)(2,1)S(1)} collective-permute-done((bf16[4,4,64,384]{3,2,1,0:T(8,128)(2,1)S(1)}, bf16[4,4,64,384]{3,2,1,0:T(8,128)(2,1)S(1)}, u32[]{:S(2)}, u32[]{:S(2)}) %collective-permute-start.30) | collective-permute-done | bytes 786464 | tf_op jit(solution)/shard_map/ppermute | solution.py:379
  172.3 6.4 %shard_map.83 = (bf16[1536,384]{1,0:T(8,128)(2,1)}, bf16[3,384,384]{2,1,0:T(8,128)(2,1)}) custom-call(s32[3]{0:T(128)} %pad_add_fusion.2.scalars_ref, bf16[128,1536]{1,0:T(8,128)(2,1)} %bitcast.203, bf16[256,1536]{1,0:T(8,128)(2,1)} %bitcast.69.refs_1_, bf16[128,1536]{1,0:T(8,128)(2,1)} %bitcast.209, bf16[128,1536]{1,0:T(8,128)(2,1)} %bitcast.204, ...), custom_call_target="tpu_custom_call" | custom-call | flops 1 | bytes 1 | tf_op jit(solution)/shard_map/pallas_call | solution.py:221
  184.7 5.1 %collective-permute-start.37 = (bf16[3,384,384]{2,1,0:T(8,128)(2,1)}, bf16[3,384,384]{2,1,0:T(8,128)(2,1)}, u32[]{:S(2)}, u32[]{:S(2)}) collective-permute-start(bf16[3,384,384]{2,1,0:T(8,128)(2,1)} %get-tuple-element.332), channel_id=1, source_target_pairs={{0,4},{12,8},{1,5},{13,9},{2,6},{14,10},{3,7},{15,11},{16,20},{28,... | collective-permute-start | bytes 2654216 | tf_op jit(solution)/shard_map/ppermute | solution.py:498
  198.8 5.5 %shard_map.85 = bf16[1536,384]{1,0:T(8,128)(2,1)} custom-call(s32[3]{0:T(128)} %stack.138.scalars_ref, bf16[128,3072]{1,0:T(8,128)(2,1)} %bitcast.155, bf16[256,3072]{1,0:T(8,128)(2,1)} %bitcast.119, bf16[64,3072]{1,0:T(8,128)(2,1)} %copy-done.36, bf16[128,3072]{1,0:T(8,128)(2,1)} %bitcast.156, bf16[256,3072]{1,0:T(8,128)(2,1)} %bitcast.120, ...), custom_call_target="tpu_custom_call" | custom-call | flops 1 | bytes 1 | tf_op jit(solution)/shard_map/pallas_call | solution.py:221
  204.3 6.4 %shard_map.86 = (bf16[1536,384]{1,0:T(8,128)(2,1)}, bf16[3,384,384]{2,1,0:T(8,128)(2,1)}) custom-call(s32[3]{0:T(128)} %pad_add_fusion.2.scalars_ref, bf16[128,1536]{1,0:T(8,128)(2,1)} %bitcast.205, bf16[256,1536]{1,0:T(8,128)(2,1)} %bitcast.69.refs_1_, bf16[128,1536]{1,0:T(8,128)(2,1)} %bitcast.211, bf16[128,1536]{1,0:T(8,128)(2,1)} %bitcast.206, ...), custom_call_target="tpu_custom_call" | custom-call | flops 1 | bytes 1 | tf_op jit(solution)/shard_map/pallas_call | solution.py:221
  226.8 5.8 %shard_map.87 = f32[1536,384]{1,0:T(8,128)} custom-call(s32[3]{0:T(128)} %stack.136.scalars_ref, bf16[128,3072]{1,0:T(8,128)(2,1)} %bitcast.157, bf16[256,3072]{1,0:T(8,128)(2,1)} %bitcast.121, bf16[64,3072]{1,0:T(8,128)(2,1)} %copy-done.36, bf16[128,3072]{1,0:T(8,128)(2,1)} %bitcast.158, bf16[256,3072]{1,0:T(8,128)(2,1)} %bitcast.122, ...), custom_call_target="tpu_custom_call" | custom-call | flops 1 | bytes 1 | tf_op jit(solution)/shard_map/pallas_call | solution.py:221
  233.3 4.4 %collective-permute-done.42.refs_9_ = bf16[3,384,384]{2,1,0:T(8,128)(2,1)S(1)} collective-permute-done((bf16[3,384,384]{2,1,0:T(8,128)(2,1)}, bf16[3,384,384]{2,1,0:T(8,128)(2,1)S(1)}, u32[]{:S(2)}, u32[]{:S(2)}) %collective-permute-start.42) | collective-permute-done | bytes 884768 | tf_op jit(solution)/shard_map/ppermute | solution.py:498
  241.4 6.7 %collective-permute-done.38.refs_3_ = bf16[64,3072]{1,0:T(8,128)(2,1)S(1)} collective-permute-done((bf16[64,3072]{1,0:T(8,128)(2,1)}, bf16[64,3072]{1,0:T(8,128)(2,1)S(1)}, u32[]{:S(2)}, u32[]{:S(2)}) %collective-permute-start.38) | collective-permute-done | bytes 393248 | tf_op jit(solution)/shard_map/ppermute | solution.py:373
  255.1 3.9 %collective-permute-done.43.refs_7_ = bf16[1,384,384]{2,1,0:T(8,128)(2,1)S(1)} collective-permute-done((bf16[1,384,384]{2,1,0:T(8,128)(2,1)S(1)}, bf16[1,384,384]{2,1,0:T(8,128)(2,1)S(1)}, u32[]{:S(2)}, u32[]{:S(2)}) %collective-permute-start.43) | collective-permute-done | bytes 294944 | tf_op jit(solution)/shard_map/ppermute | solution.py:498
  265.8 9.4 %collective-permute-done.46.refs_11_ = bf16[1,384,384]{2,1,0:T(8,128)(2,1)S(1)} collective-permute-done((bf16[1,384,384]{2,1,0:T(8,128)(2,1)S(1)}, bf16[1,384,384]{2,1,0:T(8,128)(2,1)S(1)}, u32[]{:S(2)}, u32[]{:S(2)}) %collective-permute-start.46) | collective-permute-done | bytes 294944 | tf_op jit(solution)/shard_map/ppermute | solution.py:498
  277.3 4.9 %shard_map.89 = (f32[3,384,384]{2,1,0:T(8,128)}, f32[1,384,384]{2,1,0:T(8,128)}) custom-call(s32[16]{0:T(128)} %stack.142.at_ref, bf16[4,384,384]{2,1,0:T(8,128)(2,1)} %bitcast.224, bf16[3,384,384]{2,1,0:T(8,128)(2,1)} %copy-done.39, bf16[2,384,384]{2,1,0:T(8,128)(2,1)} %collective-permute-done.36.refs_2_, ...), custom_call_target="tpu_custom_call" | custom-call | flops 1 | bytes 1 | tf_op jit(solution)/shard_map/pallas_call | solution.py:318
  (246 shorter events, 119.5 us)
Async XLA Ops:
  0.6 27.4 %collective-permute-start.3 = (bf16[3,3072,384]{2,1,0:T(8,128)(2,1)}, bf16[3,3072,384]{2,1,0:T(8,128)(2,1)}, u32[]{:S(2)}, u32[]{:S(2)}) collective-permute-start(bf16[3,3072,384]{2,1,0:T(8,128)(2,1)} %refs_4_), channel_id=1, source_target_pairs={{0,1},{1,0},{2,3},{3,2},{4,5},{5,4},{6,7},{7,6},{8,9},{9,8},{10,11... | collective-permute-start | bytes 21233672 | tf_op jit(solution)/shard_map/ppermute | solution.py:376
  2.2 21.9 %collective-permute-start = (bf16[64,3072]{1,0:T(8,128)(2,1)S(1)}, bf16[64,3072]{1,0:T(8,128)(2,1)S(1)}, u32[]{:S(2)}, u32[]{:S(2)}) collective-permute-start(bf16[64,3072]{1,0:T(8,128)(2,1)S(1)} %dynamic-slice_bitcast_fusion.5), channel_id=1, source_target_pairs={{0,8},{4,12},{8,0},{12,4},{1,9},{5,13},{9,1},{13,5},{2,10},{6,14},... | collective-permute-start | bytes 1179656 | tf_op jit(solution)/shard_map/ppermute | solution.py:373
  28.1 22.6 %collective-permute-start.8 = (bf16[2,1,64,3072]{3,2,1,0:T(8,128)(2,1)S(1)}, bf16[2,1,64,3072]{3,2,1,0:T(8,128)(2,1)S(1)}, u32[]{:S(2)}, u32[]{:S(2)}) collective-permute-start(bf16[2,1,64,3072]{3,2,1,0:T(8,128)(2,1)S(1)} %pad_maximum_fusion.2), channel_id=1, source_target_pairs={{0,1},{1,0},{2,3},{3,2},{4,5},{5,4},{6,7},{7,6},{8,9},{9,8},{10,11... | collective-permute-start | bytes 2359304 | tf_op jit(solution)/shard_map/ppermute | solution.py:376
  31.4 19.4 %collective-permute-start.5 = (bf16[64,3072]{1,0:T(8,128)(2,1)S(1)}, bf16[64,3072]{1,0:T(8,128)(2,1)S(1)}, u32[]{:S(2)}, u32[]{:S(2)}) collective-permute-start(bf16[64,3072]{1,0:T(8,128)(2,1)S(1)} %get-tuple-element.205), channel_id=1, source_target_pairs={{0,12},{4,0},{8,4},{12,8},{1,13},{5,1},{9,5},{13,9},{2,14},{6,2},{... | collective-permute-start | bytes 1179656 | tf_op jit(solution)/shard_map/ppermute | solution.py:373
  50.9 22.5 %collective-permute-start.13 = (bf16[2,1,64,3072]{3,2,0,1:T(8,128)(2,1)S(1)}, bf16[2,1,64,3072]{3,2,0,1:T(8,128)(2,1)S(1)}, u32[]{:S(2)}, u32[]{:S(2)}) collective-permute-start(bf16[2,1,64,3072]{3,2,0,1:T(8,128)(2,1)S(1)} %pad_maximum_fusion.3), channel_id=1, source_target_pairs={{0,1},{1,0},{2,3},{3,2},{4,5},{5,4},{6,7},{7,6},{8,9},{9,8},{10,11... | collective-permute-start | bytes 2359304 | tf_op jit(solution)/shard_map/ppermute | solution.py:376
  51.1 22.3 %collective-permute-start.11 = (bf16[2,64,3072]{2,1,0:T(8,128)(2,1)S(1)}, bf16[2,64,3072]{2,1,0:T(8,128)(2,1)S(1)}, u32[]{:S(2)}, u32[]{:S(2)}) collective-permute-start(bf16[2,64,3072]{2,1,0:T(8,128)(2,1)S(1)} %get-tuple-element.419), channel_id=1, source_target_pairs={{0,2},{1,3},{2,0},{3,1},{4,6},{5,7},{6,4},{7,5},{8,10},{9,11},{10,... | collective-permute-start | bytes 2359304 | tf_op jit(solution)/shard_map/ppermute | solution.py:376
  55.6 17.8 %collective-permute-start.9 = (bf16[64,3072]{1,0:T(8,128)(2,1)S(1)}, bf16[64,3072]{1,0:T(8,128)(2,1)S(1)}, u32[]{:S(2)}, u32[]{:S(2)}) collective-permute-start(bf16[64,3072]{1,0:T(8,128)(2,1)S(1)} %copy-done.54), channel_id=1, source_target_pairs={{0,4},{4,8},{8,12},{12,0},{1,5},{5,9},{9,13},{13,1},{2,6},{6,10},{... | collective-permute-start | bytes 1179656 | tf_op jit(solution)/shard_map/ppermute | solution.py:373
  73.8 22.5 %collective-permute-start.16 = (bf16[2,2,64,1536]{3,2,1,0:T(8,128)(2,1)S(1)}, bf16[2,2,64,1536]{3,2,1,0:T(8,128)(2,1)}, u32[]{:S(2)}, u32[]{:S(2)}) collective-permute-start(bf16[2,2,64,1536]{3,2,1,0:T(8,128)(2,1)S(1)} %fusion), channel_id=1, source_target_pairs={{0,16},{16,0},{1,17},{17,1},{2,18},{18,2},{3,19},{19,3},{4,20},{20... | collective-permute-start | bytes 2359304 | tf_op jit(solution)/shard_map/ppermute | solution.py:379
  75.4 20.9 %collective-permute-start.15 = (bf16[2,64,3072]{2,1,0:T(8,128)(2,1)S(1)}, bf16[2,64,3072]{2,1,0:T(8,128)(2,1)S(1)}, u32[]{:S(2)}, u32[]{:S(2)}) collective-permute-start(bf16[2,64,3072]{2,1,0:T(8,128)(2,1)S(1)} %get-tuple-element.417), channel_id=1, source_target_pairs={{0,2},{1,3},{2,0},{3,1},{4,6},{5,7},{6,4},{7,5},{8,10},{9,11},{10,... | collective-permute-start | bytes 2359304 | tf_op jit(solution)/shard_map/ppermute | solution.py:376
  76.0 20.3 %collective-permute-start.14 = (bf16[64,3072]{1,0:T(8,128)(2,1)S(1)}, bf16[64,3072]{1,0:T(8,128)(2,1)S(1)}, u32[]{:S(2)}, u32[]{:S(2)}) collective-permute-start(bf16[64,3072]{1,0:T(8,128)(2,1)S(1)} %copy-done.53), channel_id=1, source_target_pairs={{0,8},{4,12},{8,0},{12,4},{1,9},{5,13},{9,1},{13,5},{2,10},{6,14},... | collective-permute-start | bytes 1179656 | tf_op jit(solution)/shard_map/ppermute | solution.py:373
  122.5 20.7 %collective-permute-start.26 = (bf16[4,4,64,384]{3,2,1,0:T(8,128)(2,1)S(1)}, bf16[4,4,64,384]{3,2,1,0:T(8,128)(2,1)}, u32[]{:S(2)}, u32[]{:S(2)}) collective-permute-start(bf16[4,4,64,384]{3,2,1,0:T(8,128)(2,1)S(1)} %get-tuple-element.263), channel_id=1, source_target_pairs={{0,16},{16,0},{1,17},{17,1},{2,18},{18,2},{3,19},{19,3},{4,20},{20... | collective-permute-start | bytes 2359304 | tf_op jit(solution)/shard_map/ppermute | solution.py:379
  123.9 19.4 %collective-permute-start.24 = (bf16[2,2,64,1536]{3,2,1,0:T(8,128)(2,1)}, bf16[2,2,64,1536]{3,2,1,0:T(8,128)(2,1)}, u32[]{:S(2)}, u32[]{:S(2)}) collective-permute-start(bf16[2,2,64,1536]{3,2,1,0:T(8,128)(2,1)} %collective-permute-done.16), channel_id=1, source_target_pairs={{0,1},{1,0},{2,3},{3,2},{4,5},{5,4},{6,7},{7,6},{8,9},{9,8},{10,11... | collective-permute-start | bytes 2359304 | tf_op jit(solution)/shard_map/ppermute | solution.py:376
  123.9 19.3 %collective-permute-start.25 = (bf16[2,1,64,1536]{3,2,0,1:T(8,128)(2,1)S(1)}, bf16[2,1,64,1536]{3,2,0,1:T(8,128)(2,1)}, u32[]{:S(2)}, u32[]{:S(2)}) collective-permute-start(bf16[2,1,64,1536]{3,2,0,1:T(8,128)(2,1)S(1)} %copy-done.30), channel_id=1, source_target_pairs={{0,1},{1,0},{2,3},{3,2},{4,5},{5,4},{6,7},{7,6},{8,9},{9,8},{10,11... | collective-permute-start | bytes 1179656 | tf_op jit(solution)/shard_map/ppermute | solution.py:376
  152.1 19.3 %collective-permute-start.30 = (bf16[4,4,64,384]{3,2,1,0:T(8,128)(2,1)S(1)}, bf16[4,4,64,384]{3,2,1,0:T(8,128)(2,1)S(1)}, u32[]{:S(2)}, u32[]{:S(2)}) collective-permute-start(bf16[4,4,64,384]{3,2,1,0:T(8,128)(2,1)S(1)} %copy-done.16), channel_id=1, source_target_pairs={{0,16},{16,0},{1,17},{17,1},{2,18},{18,2},{3,19},{19,3},{4,20},{20... | collective-permute-start | bytes 2359304 | tf_op jit(solution)/shard_map/ppermute | solution.py:379
  153.4 25.4 %collective-permute-start.29 = (bf16[128,3072]{1,0:T(8,128)(2,1)S(1)}, bf16[128,3072]{1,0:T(8,128)(2,1)}, u32[]{:S(2)}, u32[]{:S(2)}) collective-permute-start(bf16[128,3072]{1,0:T(8,128)(2,1)S(1)} %copy-done.58), channel_id=1, source_target_pairs={{0,2},{1,3},{2,0},{3,1},{4,6},{5,7},{6,4},{7,5},{8,10},{9,11},{10,... | collective-permute-start | bytes 2359304 | tf_op jit(solution)/shard_map/ppermute | solution.py:376
  154.7 26.4 %collective-permute-start.32 = (bf16[3,384,384]{2,1,0:T(8,128)(2,1)}, bf16[3,384,384]{2,1,0:T(8,128)(2,1)S(1)}, u32[]{:S(2)}, u32[]{:S(2)}) collective-permute-start(bf16[3,384,384]{2,1,0:T(8,128)(2,1)} %get-tuple-element.306), channel_id=1, source_target_pairs={{0,4},{12,8},{1,5},{13,9},{2,6},{14,10},{3,7},{15,11},{16,20},{28,... | collective-permute-start | bytes 2654216 | tf_op jit(solution)/shard_map/ppermute | solution.py:498
  158.9 24.5 %collective-permute-start.31 = (bf16[64,3072]{1,0:T(8,128)(2,1)}, bf16[64,3072]{1,0:T(8,128)(2,1)S(1)}, u32[]{:S(2)}, u32[]{:S(2)}) collective-permute-start(bf16[64,3072]{1,0:T(8,128)(2,1)} %add_convert_fusion.6), channel_id=1, source_target_pairs={{0,8},{4,12},{8,0},{12,4},{1,9},{5,13},{9,1},{13,5},{2,10},{6,14},... | collective-permute-start | bytes 1179656 | tf_op jit(solution)/shard_map/ppermute | solution.py:373
  183.4 20.9 %collective-permute-start.35 = (bf16[4,4,64,384]{3,2,1,0:T(8,128)(2,1)S(1)}, bf16[4,4,64,384]{3,2,1,0:T(8,128)(2,1)}, u32[]{:S(2)}, u32[]{:S(2)}) collective-permute-start(bf16[4,4,64,384]{3,2,1,0:T(8,128)(2,1)S(1)} %copy-done.14), channel_id=1, source_target_pairs={{0,16},{16,0},{1,17},{17,1},{2,18},{18,2},{3,19},{19,3},{4,20},{20... | collective-permute-start | bytes 2359304 | tf_op jit(solution)/shard_map/ppermute | solution.py:379
  184.7 28.0 %collective-permute-start.37 = (bf16[3,384,384]{2,1,0:T(8,128)(2,1)}, bf16[3,384,384]{2,1,0:T(8,128)(2,1)}, u32[]{:S(2)}, u32[]{:S(2)}) collective-permute-start(bf16[3,384,384]{2,1,0:T(8,128)(2,1)} %get-tuple-element.332), channel_id=1, source_target_pairs={{0,4},{12,8},{1,5},{13,9},{2,6},{14,10},{3,7},{15,11},{16,20},{28,... | collective-permute-start | bytes 2654216 | tf_op jit(solution)/shard_map/ppermute | solution.py:498
  191.2 21.4 %collective-permute-start.33 = (bf16[64,3072]{1,0:T(8,128)(2,1)}, bf16[64,3072]{1,0:T(8,128)(2,1)}, u32[]{:S(2)}, u32[]{:S(2)}) collective-permute-start(bf16[64,3072]{1,0:T(8,128)(2,1)} %get-tuple-element.309), channel_id=1, source_target_pairs={{0,2},{1,3},{2,0},{3,1},{4,6},{5,7},{6,4},{7,5},{8,10},{9,11},{10,... | collective-permute-start | bytes 1179656 | tf_op jit(solution)/shard_map/ppermute | solution.py:376
  192.3 22.1 %collective-permute-start.34 = (bf16[64,3072]{1,0:T(8,128)(2,1)}, bf16[64,3072]{1,0:T(8,128)(2,1)}, u32[]{:S(2)}, u32[]{:S(2)}) collective-permute-start(bf16[64,3072]{1,0:T(8,128)(2,1)} %get-tuple-element.310), channel_id=1, source_target_pairs={{0,12},{4,0},{8,4},{12,8},{1,13},{5,1},{9,5},{13,9},{2,14},{6,2},{... | collective-permute-start | bytes 1179656 | tf_op jit(solution)/shard_map/ppermute | solution.py:373
  214.4 24.8 %collective-permute-start.39 = (bf16[1536,384]{1,0:T(8,128)(2,1)S(1)}, bf16[1536,384]{1,0:T(8,128)(2,1)S(1)}, u32[]{:S(2)}, u32[]{:S(2)}) collective-permute-start(bf16[1536,384]{1,0:T(8,128)(2,1)S(1)} %copy-done.46), channel_id=1, source_target_pairs={{0,16},{16,0},{1,17},{17,1},{2,18},{18,2},{3,19},{19,3},{4,20},{20... | collective-permute-start | bytes 3538952 | tf_op jit(solution)/shard_map/ppermute | solution.py:379
  216.1 21.6 %collective-permute-start.42 = (bf16[3,384,384]{2,1,0:T(8,128)(2,1)}, bf16[3,384,384]{2,1,0:T(8,128)(2,1)S(1)}, u32[]{:S(2)}, u32[]{:S(2)}) collective-permute-start(bf16[3,384,384]{2,1,0:T(8,128)(2,1)} %get-tuple-element.349), channel_id=1, source_target_pairs={{0,4},{12,8},{1,5},{13,9},{2,6},{14,10},{3,7},{15,11},{16,20},{28,... | collective-permute-start | bytes 2654216 | tf_op jit(solution)/shard_map/ppermute | solution.py:498
  220.6 27.4 %collective-permute-start.38 = (bf16[64,3072]{1,0:T(8,128)(2,1)}, bf16[64,3072]{1,0:T(8,128)(2,1)S(1)}, u32[]{:S(2)}, u32[]{:S(2)}) collective-permute-start(bf16[64,3072]{1,0:T(8,128)(2,1)} %get-tuple-element.338), channel_id=1, source_target_pairs={{0,4},{4,8},{8,12},{12,0},{1,5},{5,9},{9,13},{13,1},{2,6},{6,10},{... | collective-permute-start | bytes 1179656 | tf_op jit(solution)/shard_map/ppermute | solution.py:373
  (86 other events, 838.3 us)

commit v6 on v5

--- a/solution.py
+++ b/solution.py
@@ -412,7 +412,7 @@
 
     pair_hi, pair_hu = jnp.stack([here_hi, there_hi]), jnp.stack([here_hu, there_hu])
     here_bi = jnp.stack(near_bi)
-    near_ci = moved(send_ci, others)
+    near_ci = [paced(p[None])[0] for p in moved(send_ci, others)]
     there_bi = flip(here_bi, bits[0])
     lent_hi = lend(pair_hi)
     all_hi = spread(pair_hi)
@@ -422,7 +422,7 @@
 
     pair_bi = jnp.stack([here_bi, there_bi])
     here_ci = jnp.stack(near_ci)
-    near_cu = moved(send_cu, others)
+    near_cu = [paced(p[None])[0] for p in moved(send_cu, others)]
     there_ci = flip(here_ci, bits[0])
     lent_bi = lend(pair_bi)
     all_bi = spread(pair_bi)

time: 288 us -> 286 us (level)
  waiting for transfers between devices: 106 us -> 102 us
    ppermute x7, waiting for transfers between devices: 18.3 us -> 7.42 us  [swap(): return lax.ppermute(x, 'dp', [(0, 1), (1, 0)])]
    ppermute x9, waiting for transfers between devices: 50.9 us -> 57.4 us  [shift(): return lax.ppermute(x, 'ctx', [(i, (i + d) % n) for i in range(n)])]
  transfers between devices with their start and end apart: 49 -> 49, of which waited for: 25 -> 22; matrix products, arithmetic and copies ran while one was open for 8% -> 8% of each run, Pallas kernels for 28% -> 28%
where the time goes in v6:
time: 286 us; the launch traced here: 285 us
  waiting for transfers between devices  102 us (36%)
  Pallas kernels  87.5 us (31%)
  starting transfers between devices  59.9 us (21%)
  other arithmetic  18.2 us (6%)
  local copies, waits for them, and re-layouts  16.4 us (6%)
    ppermute x9, waiting for transfers between devices, shift(): return lax.ppermute(x, 'ctx', [(i, (i + d) % n) for i in range(n)])  57.4 us
    pallas_call x6, Pallas kernels, outer(): pl.pallas_call(kernel, grid_spec=pltpu.PrefetchScalarGridSpec(num_scalar_...  40.5 us
    ppermute x12, waiting for transfers between devices, advance(): lax.ppermute(send, 'ctx', [(step, step + 1), (n - 1 - step, n - 2 - step)])  25.3 us
    ppermute x12, starting transfers between devices, advance(): lax.ppermute(send, 'ctx', [(step, step + 1), (n - 1 - step, n - 2 - step)])  20.1 us
    ppermute x9, starting transfers between devices, shift(): return lax.ppermute(x, 'ctx', [(i, (i + d) % n) for i in range(n)])  18.6 us
    pallas_call x3, Pallas kernels, project(): pl.pallas_call(kernel, grid=(count,), in_specs=[pl.BlockSpec((size, model...  17.4 us
    pallas_call x1, Pallas kernels, backproject(): pl.pallas_call(kernel, grid=(model // wide,), in_specs=[pl.BlockSpec((row...  14.2 us
    ppermute x21, starting transfers between devices, flip(): return lax.ppermute(x, 'space', [(i, i ^ bit) for i in range(n_space)])  13.5 us
  transfers between devices with their start and end apart: 49, of which 22 were waited for; matrix products, arithmetic and copies ran while one was open for 8% of the time, Pallas kernels for 28%

profile of v6, /device:TPU:0, one launch (start us, length us, event | category | flops | bytes accessed | tf_op | source)
XLA Modules:
  0.0 285.3 jit_solution(17137083566869300469)
XLA Ops:
  11.2 12.8 %collective-permute-done = bf16[64,3072]{1,0:T(8,128)(2,1)S(1)} collective-permute-done((bf16[64,3072]{1,0:T(8,128)(2,1)S(1)}, bf16[64,3072]{1,0:T(8,128)(2,1)S(1)}, u32[]{:S(2)}, u32[]{:S(2)}) %collective-permute-start) | collective-permute-done | bytes 393248 | tf_op jit(solution)/shard_map/ppermute | solution.py:373
  24.0 4.0 %collective-permute-done.1 = bf16[1,64,3072]{2,1,0:T(8,128)(2,1)S(1)} collective-permute-done((bf16[1,64,3072]{2,1,0:T(8,128)(2,1)S(1)}, bf16[1,64,3072]{2,1,0:T(8,128)(2,1)S(1)}, u32[]{:S(2)}, u32[]{:S(2)}) %collective-permute-start.1) | collective-permute-done | bytes 393248 | tf_op jit(solution)/shard_map/ppermute | solution.py:376
  36.2 6.0 %collective-permute-done.4 = bf16[64,3072]{1,0:T(8,128)(2,1)S(1)} collective-permute-done((bf16[64,3072]{1,0:T(8,128)(2,1)}, bf16[64,3072]{1,0:T(8,128)(2,1)S(1)}, u32[]{:S(2)}, u32[]{:S(2)}) %collective-permute-start.4) | collective-permute-done | bytes 393248 | tf_op jit(solution)/shard_map/ppermute | solution.py:373
  42.2 7.3 %collective-permute-done.5 = bf16[64,3072]{1,0:T(8,128)(2,1)S(1)} collective-permute-done((bf16[64,3072]{1,0:T(8,128)(2,1)S(1)}, bf16[64,3072]{1,0:T(8,128)(2,1)S(1)}, u32[]{:S(2)}, u32[]{:S(2)}) %collective-permute-start.5) | collective-permute-done | bytes 393248 | tf_op jit(solution)/shard_map/ppermute | solution.py:373
  56.9 8.4 %collective-permute-done.9 = bf16[64,3072]{1,0:T(8,128)(2,1)S(1)} collective-permute-done((bf16[64,3072]{1,0:T(8,128)(2,1)S(1)}, bf16[64,3072]{1,0:T(8,128)(2,1)S(1)}, u32[]{:S(2)}, u32[]{:S(2)}) %collective-permute-start.9) | collective-permute-done | bytes 393248 | tf_op jit(solution)/shard_map/ppermute | solution.py:373
  65.2 5.9 %collective-permute-done.10 = bf16[64,3072]{1,0:T(8,128)(2,1)S(1)} collective-permute-done((bf16[64,3072]{1,0:T(8,128)(2,1)S(1)}, bf16[64,3072]{1,0:T(8,128)(2,1)S(1)}, u32[]{:S(2)}, u32[]{:S(2)}) %collective-permute-start.10) | collective-permute-done | bytes 393248 | tf_op jit(solution)/shard_map/ppermute | solution.py:373
  76.9 10.9 %shard_map.76 = (bf16[1024,384]{1,0:T(8,128)(2,1)S(1)}, bf16[1024,384]{1,0:T(8,128)(2,1)S(1)}, bf16[1024,384]{1,0:T(8,128)(2,1)S(1)}) custom-call(bf16[128,3072]{1,0:T(8,128)(2,1)S(1)} %bitcast.149, bf16[256,3072]{1,0:T(8,128)(2,1)S(1)} %bitcast.131, bf16[128,3072]{1,0:T(8,128)(2,1)S(1)} %bitcast.155, bf16[128,3072]{1,0:T(8,128)(2,1)S(1)} %bitcast.150, ...), custom_call_target="tpu_custom_call" | custom-call | flops 1 | bytes 1 | tf_op jit(solution)/shard_map/pallas_call | solution.py:161
  87.9 6.9 %collective-permute-done.14 = bf16[64,3072]{1,0:T(8,128)(2,1)S(1)} collective-permute-done((bf16[64,3072]{1,0:T(8,128)(2,1)S(1)}, bf16[64,3072]{1,0:T(8,128)(2,1)S(1)}, u32[]{:S(2)}, u32[]{:S(2)}) %collective-permute-start.14) | collective-permute-done | bytes 393248 | tf_op jit(solution)/shard_map/ppermute | solution.py:373
  109.6 3.9 %shard_map.78 = bf16[256,384]{1,0:T(8,128)(2,1)} custom-call(bf16[64,3072]{1,0:T(8,128)(2,1)} %copy-done.36, bf16[64,3072]{1,0:T(8,128)(2,1)} %bitcast.55.refs_1_.refs_5_, bf16[64,3072]{1,0:T(8,128)(2,1)} %bitcast.242, bf16[64,3072]{1,0:T(8,128)(2,1)} %bitcast.245, bf16[1,3072,384]{2,1,0:T(8,128)(2,1)} %bitcast.187), custom_call_target="tpu_custom_call" | custom-call | flops 1 | bytes 1 | tf_op jit(solution)/shard_map/pallas_call | solution.py:161
  114.4 4.6 %shard_map.79 = (bf16[4,4,64,384]{3,2,1,0:T(8,128)(2,1)S(1)}, bf16[4,4,64,384]{3,2,1,0:T(8,128)(2,1)S(1)}, bf16[4,4,64,384]{3,2,1,0:T(8,128)(2,1)S(1)}, bf16[3,2,4,64,384]{4,3,2,1,0:T(8,128)(2,1)S(1)}) custom-call(s32[4]{0:T(128)S(1)} %gather_fusion, bf16[4,4,64,384]{3,2,1,0:T(8,128)(2,1)S(1)} %bitcast.197, bf16[4,4,64,384]{3,2,1,0:T(8,128)(2,1)S(1)} %bitcast.199, ...), custom_call_target="tpu_custom_call" | custom-call | flops 1 | bytes 1 | tf_op jit(solution)/shard_map/pallas_call | solution.py:102
  124.9 14.2 %shard_map.80 = (bf16[64,3072]{1,0:T(8,128)(2,1)}, bf16[64,3072]{1,0:T(8,128)(2,1)}, bf16[64,3072]{1,0:T(8,128)(2,1)}, bf16[64,3072]{1,0:T(8,128)(2,1)}, bf16[64...) custom-call(bf16[1024,384]{1,0:T(8,128)(2,1)} %bitcast.191, bf16[1024,384]{1,0:T(8,128)(2,1)} %bitcast.195, ...), custom_call_target="tpu_custom_call" | custom-call | flops 1 | bytes 1 | tf_op jit(solution)/shard_map/pallas_call | solution.py:268
  141.8 8.7 %shard_map.81 = (bf16[1536,384]{1,0:T(8,128)(2,1)}, bf16[3,384,384]{2,1,0:T(8,128)(2,1)}) custom-call(s32[3]{0:T(128)} %pad_add_fusion.scalars_ref, bf16[128,1536]{1,0:T(8,128)(2,1)} %bitcast.209, bf16[256,1536]{1,0:T(8,128)(2,1)} %bitcast.63.refs_1_.refs_4_, bf16[128,1536]{1,0:T(8,128)(2,1)} %bitcast.215, bf16[128,1536]{1,0:T(8,128)(2,1)} %bitcast.210, ...), custom_call_target="tpu_custom_call" | custom-call | flops 1 | bytes 1 | tf_op jit(solution)/shard_map/pallas_call | solution.py:221
  156.8 7.6 %shard_map.82 = (f32[1536,384]{1,0:T(8,128)}, f32[1536,384]{1,0:T(8,128)}) custom-call(s32[3]{0:T(128)} %stack.136.scalars_ref, bf16[128,3072]{1,0:T(8,128)(2,1)} %bitcast.153, bf16[256,3072]{1,0:T(8,128)(2,1)} %bitcast.135, bf16[128,3072]{1,0:T(8,128)(2,1)} %bitcast.159, bf16[128,3072]{1,0:T(8,128)(2,1)} %bitcast.154, bf16[256,3072]{1,0:T(8,128)(2,1)} %bitcast.136, ...), custom_call_target="tpu_custom_call" | custom-call | flops 1 | bytes 1 | tf_op jit(solution)/shard_map/pallas_call | solution.py:221
  164.4 5.5 %collective-permute-done.30 = bf16[4,4,64,384]{3,2,1,0:T(8,128)(2,1)S(1)} collective-permute-done((bf16[4,4,64,384]{3,2,1,0:T(8,128)(2,1)S(1)}, bf16[4,4,64,384]{3,2,1,0:T(8,128)(2,1)S(1)}, u32[]{:S(2)}, u32[]{:S(2)}) %collective-permute-start.30) | collective-permute-done | bytes 786464 | tf_op jit(solution)/shard_map/ppermute | solution.py:379
  170.8 6.4 %shard_map.83 = (bf16[1536,384]{1,0:T(8,128)(2,1)}, bf16[3,384,384]{2,1,0:T(8,128)(2,1)}) custom-call(s32[3]{0:T(128)} %pad_add_fusion.2.scalars_ref, bf16[128,1536]{1,0:T(8,128)(2,1)} %bitcast.211, bf16[256,1536]{1,0:T(8,128)(2,1)} %bitcast.77.refs_1_, bf16[128,1536]{1,0:T(8,128)(2,1)} %bitcast.217, bf16[128,1536]{1,0:T(8,128)(2,1)} %bitcast.212, ...), custom_call_target="tpu_custom_call" | custom-call | flops 1 | bytes 1 | tf_op jit(solution)/shard_map/pallas_call | solution.py:221
  183.1 6.1 %collective-permute-start.37 = (bf16[3,384,384]{2,1,0:T(8,128)(2,1)}, bf16[3,384,384]{2,1,0:T(8,128)(2,1)}, u32[]{:S(2)}, u32[]{:S(2)}) collective-permute-start(bf16[3,384,384]{2,1,0:T(8,128)(2,1)} %get-tuple-element.332), channel_id=1, source_target_pairs={{0,4},{12,8},{1,5},{13,9},{2,6},{14,10},{3,7},{15,11},{16,20},{28,... | collective-permute-start | bytes 2654216 | tf_op jit(solution)/shard_map/ppermute | solution.py:498
  197.2 5.5 %shard_map.85 = bf16[1536,384]{1,0:T(8,128)(2,1)} custom-call(s32[3]{0:T(128)} %stack.138.scalars_ref, bf16[128,3072]{1,0:T(8,128)(2,1)} %bitcast.163, bf16[256,3072]{1,0:T(8,128)(2,1)} %bitcast.127, bf16[64,3072]{1,0:T(8,128)(2,1)} %copy-done.36, bf16[128,3072]{1,0:T(8,128)(2,1)} %bitcast.164, bf16[256,3072]{1,0:T(8,128)(2,1)} %bitcast.128, ...), custom_call_target="tpu_custom_call" | custom-call | flops 1 | bytes 1 | tf_op jit(solution)/shard_map/pallas_call | solution.py:221
  202.7 6.4 %shard_map.86 = (bf16[1536,384]{1,0:T(8,128)(2,1)}, bf16[3,384,384]{2,1,0:T(8,128)(2,1)}) custom-call(s32[3]{0:T(128)} %pad_add_fusion.2.scalars_ref, bf16[128,1536]{1,0:T(8,128)(2,1)} %bitcast.213, bf16[256,1536]{1,0:T(8,128)(2,1)} %bitcast.77.refs_1_, bf16[128,1536]{1,0:T(8,128)(2,1)} %bitcast.219, bf16[128,1536]{1,0:T(8,128)(2,1)} %bitcast.214, ...), custom_call_target="tpu_custom_call" | custom-call | flops 1 | bytes 1 | tf_op jit(solution)/shard_map/pallas_call | solution.py:221
  225.3 5.8 %shard_map.87 = f32[1536,384]{1,0:T(8,128)} custom-call(s32[3]{0:T(128)} %stack.136.scalars_ref, bf16[128,3072]{1,0:T(8,128)(2,1)} %bitcast.165, bf16[256,3072]{1,0:T(8,128)(2,1)} %bitcast.129, bf16[64,3072]{1,0:T(8,128)(2,1)} %copy-done.36, bf16[128,3072]{1,0:T(8,128)(2,1)} %bitcast.166, bf16[256,3072]{1,0:T(8,128)(2,1)} %bitcast.130, ...), custom_call_target="tpu_custom_call" | custom-call | flops 1 | bytes 1 | tf_op jit(solution)/shard_map/pallas_call | solution.py:221
  231.9 5.4 %collective-permute-done.42.refs_9_ = bf16[3,384,384]{2,1,0:T(8,128)(2,1)S(1)} collective-permute-done((bf16[3,384,384]{2,1,0:T(8,128)(2,1)}, bf16[3,384,384]{2,1,0:T(8,128)(2,1)S(1)}, u32[]{:S(2)}, u32[]{:S(2)}) %collective-permute-start.42) | collective-permute-done | bytes 884768 | tf_op jit(solution)/shard_map/ppermute | solution.py:498
  241.3 5.8 %collective-permute-done.38.refs_3_ = bf16[64,3072]{1,0:T(8,128)(2,1)S(1)} collective-permute-done((bf16[64,3072]{1,0:T(8,128)(2,1)}, bf16[64,3072]{1,0:T(8,128)(2,1)S(1)}, u32[]{:S(2)}, u32[]{:S(2)}) %collective-permute-start.38) | collective-permute-done | bytes 393248 | tf_op jit(solution)/shard_map/ppermute | solution.py:373
  254.1 3.9 %collective-permute-done.43.refs_7_ = bf16[1,384,384]{2,1,0:T(8,128)(2,1)S(1)} collective-permute-done((bf16[1,384,384]{2,1,0:T(8,128)(2,1)S(1)}, bf16[1,384,384]{2,1,0:T(8,128)(2,1)S(1)}, u32[]{:S(2)}, u32[]{:S(2)}) %collective-permute-start.43) | collective-permute-done | bytes 294944 | tf_op jit(solution)/shard_map/ppermute | solution.py:498
  264.5 9.4 %collective-permute-done.46.refs_11_ = bf16[1,384,384]{2,1,0:T(8,128)(2,1)S(1)} collective-permute-done((bf16[1,384,384]{2,1,0:T(8,128)(2,1)S(1)}, bf16[1,384,384]{2,1,0:T(8,128)(2,1)S(1)}, u32[]{:S(2)}, u32[]{:S(2)}) %collective-permute-start.46) | collective-permute-done | bytes 294944 | tf_op jit(solution)/shard_map/ppermute | solution.py:498
  276.0 4.9 %shard_map.89 = (f32[3,384,384]{2,1,0:T(8,128)}, f32[1,384,384]{2,1,0:T(8,128)}) custom-call(s32[16]{0:T(128)} %stack.142.at_ref, bf16[4,384,384]{2,1,0:T(8,128)(2,1)} %bitcast.232, bf16[3,384,384]{2,1,0:T(8,128)(2,1)} %copy-done.39, bf16[2,384,384]{2,1,0:T(8,128)(2,1)} %collective-permute-done.36.refs_2_, ...), custom_call_target="tpu_custom_call" | custom-call | flops 1 | bytes 1 | tf_op jit(solution)/shard_map/pallas_call | solution.py:318
  (246 shorter events, 117.5 us)
Async XLA Ops:
  0.6 27.4 %collective-permute-start.3 = (bf16[3,3072,384]{2,1,0:T(8,128)(2,1)}, bf16[3,3072,384]{2,1,0:T(8,128)(2,1)}, u32[]{:S(2)}, u32[]{:S(2)}) collective-permute-start(bf16[3,3072,384]{2,1,0:T(8,128)(2,1)} %refs_4_), channel_id=1, source_target_pairs={{0,1},{1,0},{2,3},{3,2},{4,5},{5,4},{6,7},{7,6},{8,9},{9,8},{10,11... | collective-permute-start | bytes 21233672 | tf_op jit(solution)/shard_map/ppermute | solution.py:376
  2.2 21.9 %collective-permute-start = (bf16[64,3072]{1,0:T(8,128)(2,1)S(1)}, bf16[64,3072]{1,0:T(8,128)(2,1)S(1)}, u32[]{:S(2)}, u32[]{:S(2)}) collective-permute-start(bf16[64,3072]{1,0:T(8,128)(2,1)S(1)} %dynamic-slice_bitcast_fusion.5), channel_id=1, source_target_pairs={{0,8},{4,12},{8,0},{12,4},{1,9},{5,13},{9,1},{13,5},{2,10},{6,14},... | collective-permute-start | bytes 1179656 | tf_op jit(solution)/shard_map/ppermute | solution.py:373
  28.1 21.4 %collective-permute-start.8 = (bf16[2,1,64,3072]{3,2,1,0:T(8,128)(2,1)S(1)}, bf16[2,1,64,3072]{3,2,1,0:T(8,128)(2,1)S(1)}, u32[]{:S(2)}, u32[]{:S(2)}) collective-permute-start(bf16[2,1,64,3072]{3,2,1,0:T(8,128)(2,1)S(1)} %pad_maximum_fusion.2), channel_id=1, source_target_pairs={{0,1},{1,0},{2,3},{3,2},{4,5},{5,4},{6,7},{7,6},{8,9},{9,8},{10,11... | collective-permute-start | bytes 2359304 | tf_op jit(solution)/shard_map/ppermute | solution.py:376
  29.9 19.7 %collective-permute-start.5 = (bf16[64,3072]{1,0:T(8,128)(2,1)S(1)}, bf16[64,3072]{1,0:T(8,128)(2,1)S(1)}, u32[]{:S(2)}, u32[]{:S(2)}) collective-permute-start(bf16[64,3072]{1,0:T(8,128)(2,1)S(1)} %get-tuple-element.205), channel_id=1, source_target_pairs={{0,12},{4,0},{8,4},{12,8},{1,13},{5,1},{9,5},{13,9},{2,14},{6,2},{... | collective-permute-start | bytes 1179656 | tf_op jit(solution)/shard_map/ppermute | solution.py:373
  49.7 21.5 %collective-permute-start.13 = (bf16[2,1,64,3072]{3,2,0,1:T(8,128)(2,1)S(1)}, bf16[2,1,64,3072]{3,2,0,1:T(8,128)(2,1)S(1)}, u32[]{:S(2)}, u32[]{:S(2)}) collective-permute-start(bf16[2,1,64,3072]{3,2,0,1:T(8,128)(2,1)S(1)} %pad_maximum_fusion.3), channel_id=1, source_target_pairs={{0,1},{1,0},{2,3},{3,2},{4,5},{5,4},{6,7},{7,6},{8,9},{9,8},{10,11... | collective-permute-start | bytes 2359304 | tf_op jit(solution)/shard_map/ppermute | solution.py:376
  49.9 21.3 %collective-permute-start.11 = (bf16[2,64,3072]{2,1,0:T(8,128)(2,1)S(1)}, bf16[2,64,3072]{2,1,0:T(8,128)(2,1)S(1)}, u32[]{:S(2)}, u32[]{:S(2)}) collective-permute-start(bf16[2,64,3072]{2,1,0:T(8,128)(2,1)S(1)} %get-tuple-element.419), channel_id=1, source_target_pairs={{0,2},{1,3},{2,0},{3,1},{4,6},{5,7},{6,4},{7,5},{8,10},{9,11},{10,... | collective-permute-start | bytes 2359304 | tf_op jit(solution)/shard_map/ppermute | solution.py:376
  51.8 19.4 %collective-permute-start.10 = (bf16[64,3072]{1,0:T(8,128)(2,1)S(1)}, bf16[64,3072]{1,0:T(8,128)(2,1)S(1)}, u32[]{:S(2)}, u32[]{:S(2)}) collective-permute-start(bf16[64,3072]{1,0:T(8,128)(2,1)S(1)} %copy-done.54), channel_id=1, source_target_pairs={{0,12},{4,0},{8,4},{12,8},{1,13},{5,1},{9,5},{13,9},{2,14},{6,2},{... | collective-permute-start | bytes 1179656 | tf_op jit(solution)/shard_map/ppermute | solution.py:373
  72.3 22.5 %collective-permute-start.16 = (bf16[2,2,64,1536]{3,2,1,0:T(8,128)(2,1)S(1)}, bf16[2,2,64,1536]{3,2,1,0:T(8,128)(2,1)}, u32[]{:S(2)}, u32[]{:S(2)}) collective-permute-start(bf16[2,2,64,1536]{3,2,1,0:T(8,128)(2,1)S(1)} %fusion), channel_id=1, source_target_pairs={{0,16},{16,0},{1,17},{17,1},{2,18},{18,2},{3,19},{19,3},{4,20},{20... | collective-permute-start | bytes 2359304 | tf_op jit(solution)/shard_map/ppermute | solution.py:379
  73.9 20.9 %collective-permute-start.15 = (bf16[2,64,3072]{2,1,0:T(8,128)(2,1)S(1)}, bf16[2,64,3072]{2,1,0:T(8,128)(2,1)S(1)}, u32[]{:S(2)}, u32[]{:S(2)}) collective-permute-start(bf16[2,64,3072]{2,1,0:T(8,128)(2,1)S(1)} %get-tuple-element.417), channel_id=1, source_target_pairs={{0,2},{1,3},{2,0},{3,1},{4,6},{5,7},{6,4},{7,5},{8,10},{9,11},{10,... | collective-permute-start | bytes 2359304 | tf_op jit(solution)/shard_map/ppermute | solution.py:376
  74.5 20.3 %collective-permute-start.14 = (bf16[64,3072]{1,0:T(8,128)(2,1)S(1)}, bf16[64,3072]{1,0:T(8,128)(2,1)S(1)}, u32[]{:S(2)}, u32[]{:S(2)}) collective-permute-start(bf16[64,3072]{1,0:T(8,128)(2,1)S(1)} %copy-done.53), channel_id=1, source_target_pairs={{0,8},{4,12},{8,0},{12,4},{1,9},{5,13},{9,1},{13,5},{2,10},{6,14},... | collective-permute-start | bytes 1179656 | tf_op jit(solution)/shard_map/ppermute | solution.py:373
  121.0 20.7 %collective-permute-start.26 = (bf16[4,4,64,384]{3,2,1,0:T(8,128)(2,1)S(1)}, bf16[4,4,64,384]{3,2,1,0:T(8,128)(2,1)}, u32[]{:S(2)}, u32[]{:S(2)}) collective-permute-start(bf16[4,4,64,384]{3,2,1,0:T(8,128)(2,1)S(1)} %get-tuple-element.263), channel_id=1, source_target_pairs={{0,16},{16,0},{1,17},{17,1},{2,18},{18,2},{3,19},{19,3},{4,20},{20... | collective-permute-start | bytes 2359304 | tf_op jit(solution)/shard_map/ppermute | solution.py:379
  121.9 19.9 %collective-permute-start.24 = (bf16[2,2,64,1536]{3,2,1,0:T(8,128)(2,1)}, bf16[2,2,64,1536]{3,2,1,0:T(8,128)(2,1)}, u32[]{:S(2)}, u32[]{:S(2)}) collective-permute-start(bf16[2,2,64,1536]{3,2,1,0:T(8,128)(2,1)} %collective-permute-done.16), channel_id=1, source_target_pairs={{0,1},{1,0},{2,3},{3,2},{4,5},{5,4},{6,7},{7,6},{8,9},{9,8},{10,11... | collective-permute-start | bytes 2359304 | tf_op jit(solution)/shard_map/ppermute | solution.py:376
  121.9 19.8 %collective-permute-start.25 = (bf16[2,1,64,1536]{3,2,0,1:T(8,128)(2,1)S(1)}, bf16[2,1,64,1536]{3,2,0,1:T(8,128)(2,1)}, u32[]{:S(2)}, u32[]{:S(2)}) collective-permute-start(bf16[2,1,64,1536]{3,2,0,1:T(8,128)(2,1)S(1)} %copy-done.30), channel_id=1, source_target_pairs={{0,1},{1,0},{2,3},{3,2},{4,5},{5,4},{6,7},{7,6},{8,9},{9,8},{10,11... | collective-permute-start | bytes 1179656 | tf_op jit(solution)/shard_map/ppermute | solution.py:376
  150.6 19.3 %collective-permute-start.30 = (bf16[4,4,64,384]{3,2,1,0:T(8,128)(2,1)S(1)}, bf16[4,4,64,384]{3,2,1,0:T(8,128)(2,1)S(1)}, u32[]{:S(2)}, u32[]{:S(2)}) collective-permute-start(bf16[4,4,64,384]{3,2,1,0:T(8,128)(2,1)S(1)} %copy-done.16), channel_id=1, source_target_pairs={{0,16},{16,0},{1,17},{17,1},{2,18},{18,2},{3,19},{19,3},{4,20},{20... | collective-permute-start | bytes 2359304 | tf_op jit(solution)/shard_map/ppermute | solution.py:379
  151.4 25.8 %collective-permute-start.29 = (bf16[128,3072]{1,0:T(8,128)(2,1)S(1)}, bf16[128,3072]{1,0:T(8,128)(2,1)}, u32[]{:S(2)}, u32[]{:S(2)}) collective-permute-start(bf16[128,3072]{1,0:T(8,128)(2,1)S(1)} %copy-done.58), channel_id=1, source_target_pairs={{0,2},{1,3},{2,0},{3,1},{4,6},{5,7},{6,4},{7,5},{8,10},{9,11},{10,... | collective-permute-start | bytes 2359304 | tf_op jit(solution)/shard_map/ppermute | solution.py:376
  153.2 26.4 %collective-permute-start.32 = (bf16[3,384,384]{2,1,0:T(8,128)(2,1)}, bf16[3,384,384]{2,1,0:T(8,128)(2,1)S(1)}, u32[]{:S(2)}, u32[]{:S(2)}) collective-permute-start(bf16[3,384,384]{2,1,0:T(8,128)(2,1)} %get-tuple-element.306), channel_id=1, source_target_pairs={{0,4},{12,8},{1,5},{13,9},{2,6},{14,10},{3,7},{15,11},{16,20},{28,... | collective-permute-start | bytes 2654216 | tf_op jit(solution)/shard_map/ppermute | solution.py:498
  156.6 25.0 %collective-permute-start.31 = (bf16[64,3072]{1,0:T(8,128)(2,1)}, bf16[64,3072]{1,0:T(8,128)(2,1)S(1)}, u32[]{:S(2)}, u32[]{:S(2)}) collective-permute-start(bf16[64,3072]{1,0:T(8,128)(2,1)} %add_convert_fusion.6), channel_id=1, source_target_pairs={{0,8},{4,12},{8,0},{12,4},{1,9},{5,13},{9,1},{13,5},{2,10},{6,14},... | collective-permute-start | bytes 1179656 | tf_op jit(solution)/shard_map/ppermute | solution.py:373
  181.6 21.1 %collective-permute-start.35 = (bf16[4,4,64,384]{3,2,1,0:T(8,128)(2,1)S(1)}, bf16[4,4,64,384]{3,2,1,0:T(8,128)(2,1)}, u32[]{:S(2)}, u32[]{:S(2)}) collective-permute-start(bf16[4,4,64,384]{3,2,1,0:T(8,128)(2,1)S(1)} %copy-done.14), channel_id=1, source_target_pairs={{0,16},{16,0},{1,17},{17,1},{2,18},{18,2},{3,19},{19,3},{4,20},{20... | collective-permute-start | bytes 2359304 | tf_op jit(solution)/shard_map/ppermute | solution.py:379
  183.1 28.0 %collective-permute-start.37 = (bf16[3,384,384]{2,1,0:T(8,128)(2,1)}, bf16[3,384,384]{2,1,0:T(8,128)(2,1)}, u32[]{:S(2)}, u32[]{:S(2)}) collective-permute-start(bf16[3,384,384]{2,1,0:T(8,128)(2,1)} %get-tuple-element.332), channel_id=1, source_target_pairs={{0,4},{12,8},{1,5},{13,9},{2,6},{14,10},{3,7},{15,11},{16,20},{28,... | collective-permute-start | bytes 2654216 | tf_op jit(solution)/shard_map/ppermute | solution.py:498
  190.7 20.4 %collective-permute-start.33 = (bf16[64,3072]{1,0:T(8,128)(2,1)}, bf16[64,3072]{1,0:T(8,128)(2,1)}, u32[]{:S(2)}, u32[]{:S(2)}) collective-permute-start(bf16[64,3072]{1,0:T(8,128)(2,1)} %get-tuple-element.309), channel_id=1, source_target_pairs={{0,2},{1,3},{2,0},{3,1},{4,6},{5,7},{6,4},{7,5},{8,10},{9,11},{10,... | collective-permute-start | bytes 1179656 | tf_op jit(solution)/shard_map/ppermute | solution.py:376
  191.6 23.0 %collective-permute-start.34 = (bf16[64,3072]{1,0:T(8,128)(2,1)}, bf16[64,3072]{1,0:T(8,128)(2,1)}, u32[]{:S(2)}, u32[]{:S(2)}) collective-permute-start(bf16[64,3072]{1,0:T(8,128)(2,1)} %get-tuple-element.310), channel_id=1, source_target_pairs={{0,12},{4,0},{8,4},{12,8},{1,13},{5,1},{9,5},{13,9},{2,14},{6,2},{... | collective-permute-start | bytes 1179656 | tf_op jit(solution)/shard_map/ppermute | solution.py:373
  214.6 24.5 %collective-permute-start.39 = (bf16[1536,384]{1,0:T(8,128)(2,1)S(1)}, bf16[1536,384]{1,0:T(8,128)(2,1)S(1)}, u32[]{:S(2)}, u32[]{:S(2)}) collective-permute-start(bf16[1536,384]{1,0:T(8,128)(2,1)S(1)} %copy-done.46), channel_id=1, source_target_pairs={{0,16},{16,0},{1,17},{17,1},{2,18},{18,2},{3,19},{19,3},{4,20},{20... | collective-permute-start | bytes 3538952 | tf_op jit(solution)/shard_map/ppermute | solution.py:379
  214.6 22.6 %collective-permute-start.42 = (bf16[3,384,384]{2,1,0:T(8,128)(2,1)}, bf16[3,384,384]{2,1,0:T(8,128)(2,1)S(1)}, u32[]{:S(2)}, u32[]{:S(2)}) collective-permute-start(bf16[3,384,384]{2,1,0:T(8,128)(2,1)} %get-tuple-element.349), channel_id=1, source_target_pairs={{0,4},{12,8},{1,5},{13,9},{2,6},{14,10},{3,7},{15,11},{16,20},{28,... | collective-permute-start | bytes 2654216 | tf_op jit(solution)/shard_map/ppermute | solution.py:498
  219.8 27.3 %collective-permute-start.38 = (bf16[64,3072]{1,0:T(8,128)(2,1)}, bf16[64,3072]{1,0:T(8,128)(2,1)S(1)}, u32[]{:S(2)}, u32[]{:S(2)}) collective-permute-start(bf16[64,3072]{1,0:T(8,128)(2,1)} %get-tuple-element.338), channel_id=1, source_target_pairs={{0,4},{4,8},{8,12},{12,0},{1,5},{5,9},{9,13},{13,1},{2,6},{6,10},{... | collective-permute-start | bytes 1179656 | tf_op jit(solution)/shard_map/ppermute | solution.py:373
  (86 other events, 824.9 us)

commit v7 on v6

--- a/solution.py
+++ b/solution.py
@@ -449,6 +449,7 @@
     here_bu = spread(here_bu[None])
     from_hi = spread(lent_hi)
     (o_near,) = project([all_hu, all_cu], out_weight[None])
+    there_bu = paced(tie(there_bu, o_near))
     there_bu, from_hi, here_bu, o_near, all_hu, all_cu, lent_ci, lent_bi = tie_all(
         there_bu, from_hi, here_bu, o_near, all_hu, all_cu, lent_ci, lent_bi
     )

time: 286 us -> 286 us (level)
  no operation moved by 1% of the time
where the time goes in v7:
time: 286 us; the launch traced here: 285 us
  waiting for transfers between devices  102 us (36%)
  Pallas kernels  87.5 us (31%)
  starting transfers between devices  59.9 us (21%)
  other arithmetic  18.2 us (6%)
  local copies, waits for them, and re-layouts  16.4 us (6%)
    ppermute x9, waiting for transfers between devices, shift(): return lax.ppermute(x, 'ctx', [(i, (i + d) % n) for i in range(n)])  57.4 us
    pallas_call x6, Pallas kernels, outer(): pl.pallas_call(kernel, grid_spec=pltpu.PrefetchScalarGridSpec(num_scalar_...  40.5 us
    ppermute x12, waiting for transfers between devices, advance(): lax.ppermute(send, 'ctx', [(step, step + 1), (n - 1 - step, n - 2 - step)])  25.3 us
    ppermute x12, starting transfers between devices, advance(): lax.ppermute(send, 'ctx', [(step, step + 1), (n - 1 - step, n - 2 - step)])  20.1 us
    ppermute x9, starting transfers between devices, shift(): return lax.ppermute(x, 'ctx', [(i, (i + d) % n) for i in range(n)])  18.6 us
    pallas_call x3, Pallas kernels, project(): pl.pallas_call(kernel, grid=(count,), in_specs=[pl.BlockSpec((size, model...  17.4 us
    pallas_call x1, Pallas kernels, backproject(): pl.pallas_call(kernel, grid=(model // wide,), in_specs=[pl.BlockSpec((row...  14.2 us
    ppermute x21, starting transfers between devices, flip(): return lax.ppermute(x, 'space', [(i, i ^ bit) for i in range(n_space)])  13.5 us
  transfers between devices with their start and end apart: 49, of which 22 were waited for; matrix products, arithmetic and copies ran while one was open for 8% of the time, Pallas kernels for 28%

profile of v7, /device:TPU:0, one launch (start us, length us, event | category | flops | bytes accessed | tf_op | source)
XLA Modules:
  0.0 285.3 jit_solution(1991905897373590060)
XLA Ops:
  11.2 12.8 %collective-permute-done = bf16[64,3072]{1,0:T(8,128)(2,1)S(1)} collective-permute-done((bf16[64,3072]{1,0:T(8,128)(2,1)S(1)}, bf16[64,3072]{1,0:T(8,128)(2,1)S(1)}, u32[]{:S(2)}, u32[]{:S(2)}) %collective-permute-start) | collective-permute-done | bytes 393248 | tf_op jit(solution)/shard_map/ppermute | solution.py:373
  24.0 4.0 %collective-permute-done.1 = bf16[1,64,3072]{2,1,0:T(8,128)(2,1)S(1)} collective-permute-done((bf16[1,64,3072]{2,1,0:T(8,128)(2,1)S(1)}, bf16[1,64,3072]{2,1,0:T(8,128)(2,1)S(1)}, u32[]{:S(2)}, u32[]{:S(2)}) %collective-permute-start.1) | collective-permute-done | bytes 393248 | tf_op jit(solution)/shard_map/ppermute | solution.py:376
  36.2 6.0 %collective-permute-done.4 = bf16[64,3072]{1,0:T(8,128)(2,1)S(1)} collective-permute-done((bf16[64,3072]{1,0:T(8,128)(2,1)}, bf16[64,3072]{1,0:T(8,128)(2,1)S(1)}, u32[]{:S(2)}, u32[]{:S(2)}) %collective-permute-start.4) | collective-permute-done | bytes 393248 | tf_op jit(solution)/shard_map/ppermute | solution.py:373
  42.2 7.3 %collective-permute-done.5 = bf16[64,3072]{1,0:T(8,128)(2,1)S(1)} collective-permute-done((bf16[64,3072]{1,0:T(8,128)(2,1)S(1)}, bf16[64,3072]{1,0:T(8,128)(2,1)S(1)}, u32[]{:S(2)}, u32[]{:S(2)}) %collective-permute-start.5) | collective-permute-done | bytes 393248 | tf_op jit(solution)/shard_map/ppermute | solution.py:373
  56.9 8.4 %collective-permute-done.9 = bf16[64,3072]{1,0:T(8,128)(2,1)S(1)} collective-permute-done((bf16[64,3072]{1,0:T(8,128)(2,1)S(1)}, bf16[64,3072]{1,0:T(8,128)(2,1)S(1)}, u32[]{:S(2)}, u32[]{:S(2)}) %collective-permute-start.9) | collective-permute-done | bytes 393248 | tf_op jit(solution)/shard_map/ppermute | solution.py:373
  65.2 5.9 %collective-permute-done.10 = bf16[64,3072]{1,0:T(8,128)(2,1)S(1)} collective-permute-done((bf16[64,3072]{1,0:T(8,128)(2,1)S(1)}, bf16[64,3072]{1,0:T(8,128)(2,1)S(1)}, u32[]{:S(2)}, u32[]{:S(2)}) %collective-permute-start.10) | collective-permute-done | bytes 393248 | tf_op jit(solution)/shard_map/ppermute | solution.py:373
  76.9 10.9 %shard_map.76 = (bf16[1024,384]{1,0:T(8,128)(2,1)S(1)}, bf16[1024,384]{1,0:T(8,128)(2,1)S(1)}, bf16[1024,384]{1,0:T(8,128)(2,1)S(1)}) custom-call(bf16[128,3072]{1,0:T(8,128)(2,1)S(1)} %bitcast.149, bf16[256,3072]{1,0:T(8,128)(2,1)S(1)} %bitcast.131, bf16[128,3072]{1,0:T(8,128)(2,1)S(1)} %bitcast.155, bf16[128,3072]{1,0:T(8,128)(2,1)S(1)} %bitcast.150, ...), custom_call_target="tpu_custom_call" | custom-call | flops 1 | bytes 1 | tf_op jit(solution)/shard_map/pallas_call | solution.py:161
  87.9 6.9 %collective-permute-done.14 = bf16[64,3072]{1,0:T(8,128)(2,1)S(1)} collective-permute-done((bf16[64,3072]{1,0:T(8,128)(2,1)S(1)}, bf16[64,3072]{1,0:T(8,128)(2,1)S(1)}, u32[]{:S(2)}, u32[]{:S(2)}) %collective-permute-start.14) | collective-permute-done | bytes 393248 | tf_op jit(solution)/shard_map/ppermute | solution.py:373
  109.6 3.9 %shard_map.78 = bf16[256,384]{1,0:T(8,128)(2,1)} custom-call(bf16[64,3072]{1,0:T(8,128)(2,1)} %copy-done.36, bf16[64,3072]{1,0:T(8,128)(2,1)} %bitcast.55.refs_1_.refs_5_, bf16[64,3072]{1,0:T(8,128)(2,1)} %bitcast.242, bf16[64,3072]{1,0:T(8,128)(2,1)} %bitcast.245, bf16[1,3072,384]{2,1,0:T(8,128)(2,1)} %bitcast.187), custom_call_target="tpu_custom_call" | custom-call | flops 1 | bytes 1 | tf_op jit(solution)/shard_map/pallas_call | solution.py:161
  114.4 4.6 %shard_map.79 = (bf16[4,4,64,384]{3,2,1,0:T(8,128)(2,1)S(1)}, bf16[4,4,64,384]{3,2,1,0:T(8,128)(2,1)S(1)}, bf16[4,4,64,384]{3,2,1,0:T(8,128)(2,1)S(1)}, bf16[3,2,4,64,384]{4,3,2,1,0:T(8,128)(2,1)S(1)}) custom-call(s32[4]{0:T(128)S(1)} %gather_fusion, bf16[4,4,64,384]{3,2,1,0:T(8,128)(2,1)S(1)} %bitcast.197, bf16[4,4,64,384]{3,2,1,0:T(8,128)(2,1)S(1)} %bitcast.199, ...), custom_call_target="tpu_custom_call" | custom-call | flops 1 | bytes 1 | tf_op jit(solution)/shard_map/pallas_call | solution.py:102
  124.9 14.2 %shard_map.80 = (bf16[64,3072]{1,0:T(8,128)(2,1)}, bf16[64,3072]{1,0:T(8,128)(2,1)}, bf16[64,3072]{1,0:T(8,128)(2,1)}, bf16[64,3072]{1,0:T(8,128)(2,1)}, bf16[64...) custom-call(bf16[1024,384]{1,0:T(8,128)(2,1)} %bitcast.191, bf16[1024,384]{1,0:T(8,128)(2,1)} %bitcast.195, ...), custom_call_target="tpu_custom_call" | custom-call | flops 1 | bytes 1 | tf_op jit(solution)/shard_map/pallas_call | solution.py:268
  141.8 8.7 %shard_map.81 = (bf16[1536,384]{1,0:T(8,128)(2,1)}, bf16[3,384,384]{2,1,0:T(8,128)(2,1)}) custom-call(s32[3]{0:T(128)} %pad_add_fusion.scalars_ref, bf16[128,1536]{1,0:T(8,128)(2,1)} %bitcast.209, bf16[256,1536]{1,0:T(8,128)(2,1)} %bitcast.63.refs_1_.refs_4_, bf16[128,1536]{1,0:T(8,128)(2,1)} %bitcast.215, bf16[128,1536]{1,0:T(8,128)(2,1)} %bitcast.210, ...), custom_call_target="tpu_custom_call" | custom-call | flops 1 | bytes 1 | tf_op jit(solution)/shard_map/pallas_call | solution.py:221
  156.8 7.6 %shard_map.82 = (f32[1536,384]{1,0:T(8,128)}, f32[1536,384]{1,0:T(8,128)}) custom-call(s32[3]{0:T(128)} %stack.136.scalars_ref, bf16[128,3072]{1,0:T(8,128)(2,1)} %bitcast.153, bf16[256,3072]{1,0:T(8,128)(2,1)} %bitcast.135, bf16[128,3072]{1,0:T(8,128)(2,1)} %bitcast.159, bf16[128,3072]{1,0:T(8,128)(2,1)} %bitcast.154, bf16[256,3072]{1,0:T(8,128)(2,1)} %bitcast.136, ...), custom_call_target="tpu_custom_call" | custom-call | flops 1 | bytes 1 | tf_op jit(solution)/shard_map/pallas_call | solution.py:221
  164.4 5.5 %collective-permute-done.30 = bf16[4,4,64,384]{3,2,1,0:T(8,128)(2,1)S(1)} collective-permute-done((bf16[4,4,64,384]{3,2,1,0:T(8,128)(2,1)S(1)}, bf16[4,4,64,384]{3,2,1,0:T(8,128)(2,1)S(1)}, u32[]{:S(2)}, u32[]{:S(2)}) %collective-permute-start.30) | collective-permute-done | bytes 786464 | tf_op jit(solution)/shard_map/ppermute | solution.py:379
  170.8 6.4 %shard_map.83 = (bf16[1536,384]{1,0:T(8,128)(2,1)}, bf16[3,384,384]{2,1,0:T(8,128)(2,1)}) custom-call(s32[3]{0:T(128)} %pad_add_fusion.2.scalars_ref, bf16[128,1536]{1,0:T(8,128)(2,1)} %bitcast.211, bf16[256,1536]{1,0:T(8,128)(2,1)} %bitcast.77.refs_1_, bf16[128,1536]{1,0:T(8,128)(2,1)} %bitcast.217, bf16[128,1536]{1,0:T(8,128)(2,1)} %bitcast.212, ...), custom_call_target="tpu_custom_call" | custom-call | flops 1 | bytes 1 | tf_op jit(solution)/shard_map/pallas_call | solution.py:221
  183.1 6.1 %collective-permute-start.37 = (bf16[3,384,384]{2,1,0:T(8,128)(2,1)}, bf16[3,384,384]{2,1,0:T(8,128)(2,1)}, u32[]{:S(2)}, u32[]{:S(2)}) collective-permute-start(bf16[3,384,384]{2,1,0:T(8,128)(2,1)} %get-tuple-element.334), channel_id=1, source_target_pairs={{0,4},{12,8},{1,5},{13,9},{2,6},{14,10},{3,7},{15,11},{16,20},{28,... | collective-permute-start | bytes 2654216 | tf_op jit(solution)/shard_map/ppermute | solution.py:499
  197.2 5.5 %shard_map.85 = bf16[1536,384]{1,0:T(8,128)(2,1)} custom-call(s32[3]{0:T(128)} %stack.138.scalars_ref, bf16[128,3072]{1,0:T(8,128)(2,1)} %bitcast.163, bf16[256,3072]{1,0:T(8,128)(2,1)} %bitcast.127, bf16[64,3072]{1,0:T(8,128)(2,1)} %copy-done.36, bf16[128,3072]{1,0:T(8,128)(2,1)} %bitcast.164, bf16[256,3072]{1,0:T(8,128)(2,1)} %bitcast.128, ...), custom_call_target="tpu_custom_call" | custom-call | flops 1 | bytes 1 | tf_op jit(solution)/shard_map/pallas_call | solution.py:221
  202.7 6.4 %shard_map.86 = (bf16[1536,384]{1,0:T(8,128)(2,1)}, bf16[3,384,384]{2,1,0:T(8,128)(2,1)}) custom-call(s32[3]{0:T(128)} %pad_add_fusion.2.scalars_ref, bf16[128,1536]{1,0:T(8,128)(2,1)} %bitcast.213, bf16[256,1536]{1,0:T(8,128)(2,1)} %bitcast.77.refs_1_, bf16[128,1536]{1,0:T(8,128)(2,1)} %bitcast.219, bf16[128,1536]{1,0:T(8,128)(2,1)} %bitcast.214, ...), custom_call_target="tpu_custom_call" | custom-call | flops 1 | bytes 1 | tf_op jit(solution)/shard_map/pallas_call | solution.py:221
  225.3 5.8 %shard_map.87 = f32[1536,384]{1,0:T(8,128)} custom-call(s32[3]{0:T(128)} %stack.136.scalars_ref, bf16[128,3072]{1,0:T(8,128)(2,1)} %bitcast.165, bf16[256,3072]{1,0:T(8,128)(2,1)} %bitcast.129, bf16[64,3072]{1,0:T(8,128)(2,1)} %copy-done.36, bf16[128,3072]{1,0:T(8,128)(2,1)} %bitcast.166, bf16[256,3072]{1,0:T(8,128)(2,1)} %bitcast.130, ...), custom_call_target="tpu_custom_call" | custom-call | flops 1 | bytes 1 | tf_op jit(solution)/shard_map/pallas_call | solution.py:221
  231.9 5.4 %collective-permute-done.42.refs_9_ = bf16[3,384,384]{2,1,0:T(8,128)(2,1)S(1)} collective-permute-done((bf16[3,384,384]{2,1,0:T(8,128)(2,1)}, bf16[3,384,384]{2,1,0:T(8,128)(2,1)S(1)}, u32[]{:S(2)}, u32[]{:S(2)}) %collective-permute-start.42) | collective-permute-done | bytes 884768 | tf_op jit(solution)/shard_map/ppermute | solution.py:499
  241.3 5.8 %collective-permute-done.38.refs_3_ = bf16[64,3072]{1,0:T(8,128)(2,1)S(1)} collective-permute-done((bf16[64,3072]{1,0:T(8,128)(2,1)}, bf16[64,3072]{1,0:T(8,128)(2,1)S(1)}, u32[]{:S(2)}, u32[]{:S(2)}) %collective-permute-start.38) | collective-permute-done | bytes 393248 | tf_op jit(solution)/shard_map/ppermute | solution.py:373
  254.1 3.9 %collective-permute-done.43.refs_7_ = bf16[1,384,384]{2,1,0:T(8,128)(2,1)S(1)} collective-permute-done((bf16[1,384,384]{2,1,0:T(8,128)(2,1)S(1)}, bf16[1,384,384]{2,1,0:T(8,128)(2,1)S(1)}, u32[]{:S(2)}, u32[]{:S(2)}) %collective-permute-start.43) | collective-permute-done | bytes 294944 | tf_op jit(solution)/shard_map/ppermute | solution.py:499
  264.5 9.4 %collective-permute-done.46.refs_11_ = bf16[1,384,384]{2,1,0:T(8,128)(2,1)S(1)} collective-permute-done((bf16[1,384,384]{2,1,0:T(8,128)(2,1)S(1)}, bf16[1,384,384]{2,1,0:T(8,128)(2,1)S(1)}, u32[]{:S(2)}, u32[]{:S(2)}) %collective-permute-start.46) | collective-permute-done | bytes 294944 | tf_op jit(solution)/shard_map/ppermute | solution.py:499
  276.0 4.9 %shard_map.89 = (f32[3,384,384]{2,1,0:T(8,128)}, f32[1,384,384]{2,1,0:T(8,128)}) custom-call(s32[16]{0:T(128)} %stack.142.at_ref, bf16[4,384,384]{2,1,0:T(8,128)(2,1)} %bitcast.232, bf16[3,384,384]{2,1,0:T(8,128)(2,1)} %copy-done.39, bf16[2,384,384]{2,1,0:T(8,128)(2,1)} %collective-permute-done.36.refs_2_, ...), custom_call_target="tpu_custom_call" | custom-call | flops 1 | bytes 1 | tf_op jit(solution)/shard_map/pallas_call | solution.py:318
  (246 shorter events, 117.5 us)
Async XLA Ops:
  0.6 27.4 %collective-permute-start.3 = (bf16[3,3072,384]{2,1,0:T(8,128)(2,1)}, bf16[3,3072,384]{2,1,0:T(8,128)(2,1)}, u32[]{:S(2)}, u32[]{:S(2)}) collective-permute-start(bf16[3,3072,384]{2,1,0:T(8,128)(2,1)} %refs_4_), channel_id=1, source_target_pairs={{0,1},{1,0},{2,3},{3,2},{4,5},{5,4},{6,7},{7,6},{8,9},{9,8},{10,11... | collective-permute-start | bytes 21233672 | tf_op jit(solution)/shard_map/ppermute | solution.py:376
  2.2 21.9 %collective-permute-start = (bf16[64,3072]{1,0:T(8,128)(2,1)S(1)}, bf16[64,3072]{1,0:T(8,128)(2,1)S(1)}, u32[]{:S(2)}, u32[]{:S(2)}) collective-permute-start(bf16[64,3072]{1,0:T(8,128)(2,1)S(1)} %dynamic-slice_bitcast_fusion.5), channel_id=1, source_target_pairs={{0,8},{4,12},{8,0},{12,4},{1,9},{5,13},{9,1},{13,5},{2,10},{6,14},... | collective-permute-start | bytes 1179656 | tf_op jit(solution)/shard_map/ppermute | solution.py:373
  28.1 21.4 %collective-permute-start.8 = (bf16[2,1,64,3072]{3,2,1,0:T(8,128)(2,1)S(1)}, bf16[2,1,64,3072]{3,2,1,0:T(8,128)(2,1)S(1)}, u32[]{:S(2)}, u32[]{:S(2)}) collective-permute-start(bf16[2,1,64,3072]{3,2,1,0:T(8,128)(2,1)S(1)} %pad_maximum_fusion.2), channel_id=1, source_target_pairs={{0,1},{1,0},{2,3},{3,2},{4,5},{5,4},{6,7},{7,6},{8,9},{9,8},{10,11... | collective-permute-start | bytes 2359304 | tf_op jit(solution)/shard_map/ppermute | solution.py:376
  29.9 19.7 %collective-permute-start.5 = (bf16[64,3072]{1,0:T(8,128)(2,1)S(1)}, bf16[64,3072]{1,0:T(8,128)(2,1)S(1)}, u32[]{:S(2)}, u32[]{:S(2)}) collective-permute-start(bf16[64,3072]{1,0:T(8,128)(2,1)S(1)} %get-tuple-element.206), channel_id=1, source_target_pairs={{0,12},{4,0},{8,4},{12,8},{1,13},{5,1},{9,5},{13,9},{2,14},{6,2},{... | collective-permute-start | bytes 1179656 | tf_op jit(solution)/shard_map/ppermute | solution.py:373
  49.7 21.5 %collective-permute-start.13 = (bf16[2,1,64,3072]{3,2,0,1:T(8,128)(2,1)S(1)}, bf16[2,1,64,3072]{3,2,0,1:T(8,128)(2,1)S(1)}, u32[]{:S(2)}, u32[]{:S(2)}) collective-permute-start(bf16[2,1,64,3072]{3,2,0,1:T(8,128)(2,1)S(1)} %pad_maximum_fusion.3), channel_id=1, source_target_pairs={{0,1},{1,0},{2,3},{3,2},{4,5},{5,4},{6,7},{7,6},{8,9},{9,8},{10,11... | collective-permute-start | bytes 2359304 | tf_op jit(solution)/shard_map/ppermute | solution.py:376
  49.9 21.3 %collective-permute-start.11 = (bf16[2,64,3072]{2,1,0:T(8,128)(2,1)S(1)}, bf16[2,64,3072]{2,1,0:T(8,128)(2,1)S(1)}, u32[]{:S(2)}, u32[]{:S(2)}) collective-permute-start(bf16[2,64,3072]{2,1,0:T(8,128)(2,1)S(1)} %get-tuple-element.421), channel_id=1, source_target_pairs={{0,2},{1,3},{2,0},{3,1},{4,6},{5,7},{6,4},{7,5},{8,10},{9,11},{10,... | collective-permute-start | bytes 2359304 | tf_op jit(solution)/shard_map/ppermute | solution.py:376
  51.8 19.4 %collective-permute-start.10 = (bf16[64,3072]{1,0:T(8,128)(2,1)S(1)}, bf16[64,3072]{1,0:T(8,128)(2,1)S(1)}, u32[]{:S(2)}, u32[]{:S(2)}) collective-permute-start(bf16[64,3072]{1,0:T(8,128)(2,1)S(1)} %copy-done.54), channel_id=1, source_target_pairs={{0,12},{4,0},{8,4},{12,8},{1,13},{5,1},{9,5},{13,9},{2,14},{6,2},{... | collective-permute-start | bytes 1179656 | tf_op jit(solution)/shard_map/ppermute | solution.py:373
  72.3 22.5 %collective-permute-start.16 = (bf16[2,2,64,1536]{3,2,1,0:T(8,128)(2,1)S(1)}, bf16[2,2,64,1536]{3,2,1,0:T(8,128)(2,1)}, u32[]{:S(2)}, u32[]{:S(2)}) collective-permute-start(bf16[2,2,64,1536]{3,2,1,0:T(8,128)(2,1)S(1)} %fusion), channel_id=1, source_target_pairs={{0,16},{16,0},{1,17},{17,1},{2,18},{18,2},{3,19},{19,3},{4,20},{20... | collective-permute-start | bytes 2359304 | tf_op jit(solution)/shard_map/ppermute | solution.py:379
  73.9 20.9 %collective-permute-start.15 = (bf16[2,64,3072]{2,1,0:T(8,128)(2,1)S(1)}, bf16[2,64,3072]{2,1,0:T(8,128)(2,1)S(1)}, u32[]{:S(2)}, u32[]{:S(2)}) collective-permute-start(bf16[2,64,3072]{2,1,0:T(8,128)(2,1)S(1)} %get-tuple-element.419), channel_id=1, source_target_pairs={{0,2},{1,3},{2,0},{3,1},{4,6},{5,7},{6,4},{7,5},{8,10},{9,11},{10,... | collective-permute-start | bytes 2359304 | tf_op jit(solution)/shard_map/ppermute | solution.py:376
  74.5 20.3 %collective-permute-start.14 = (bf16[64,3072]{1,0:T(8,128)(2,1)S(1)}, bf16[64,3072]{1,0:T(8,128)(2,1)S(1)}, u32[]{:S(2)}, u32[]{:S(2)}) collective-permute-start(bf16[64,3072]{1,0:T(8,128)(2,1)S(1)} %copy-done.53), channel_id=1, source_target_pairs={{0,8},{4,12},{8,0},{12,4},{1,9},{5,13},{9,1},{13,5},{2,10},{6,14},... | collective-permute-start | bytes 1179656 | tf_op jit(solution)/shard_map/ppermute | solution.py:373
  121.0 20.7 %collective-permute-start.26 = (bf16[4,4,64,384]{3,2,1,0:T(8,128)(2,1)S(1)}, bf16[4,4,64,384]{3,2,1,0:T(8,128)(2,1)}, u32[]{:S(2)}, u32[]{:S(2)}) collective-permute-start(bf16[4,4,64,384]{3,2,1,0:T(8,128)(2,1)S(1)} %get-tuple-element.265), channel_id=1, source_target_pairs={{0,16},{16,0},{1,17},{17,1},{2,18},{18,2},{3,19},{19,3},{4,20},{20... | collective-permute-start | bytes 2359304 | tf_op jit(solution)/shard_map/ppermute | solution.py:379
  121.9 19.9 %collective-permute-start.24 = (bf16[2,2,64,1536]{3,2,1,0:T(8,128)(2,1)}, bf16[2,2,64,1536]{3,2,1,0:T(8,128)(2,1)}, u32[]{:S(2)}, u32[]{:S(2)}) collective-permute-start(bf16[2,2,64,1536]{3,2,1,0:T(8,128)(2,1)} %collective-permute-done.16), channel_id=1, source_target_pairs={{0,1},{1,0},{2,3},{3,2},{4,5},{5,4},{6,7},{7,6},{8,9},{9,8},{10,11... | collective-permute-start | bytes 2359304 | tf_op jit(solution)/shard_map/ppermute | solution.py:376
  121.9 19.8 %collective-permute-start.25 = (bf16[2,1,64,1536]{3,2,0,1:T(8,128)(2,1)S(1)}, bf16[2,1,64,1536]{3,2,0,1:T(8,128)(2,1)}, u32[]{:S(2)}, u32[]{:S(2)}) collective-permute-start(bf16[2,1,64,1536]{3,2,0,1:T(8,128)(2,1)S(1)} %copy-done.30), channel_id=1, source_target_pairs={{0,1},{1,0},{2,3},{3,2},{4,5},{5,4},{6,7},{7,6},{8,9},{9,8},{10,11... | collective-permute-start | bytes 1179656 | tf_op jit(solution)/shard_map/ppermute | solution.py:376
  150.6 19.3 %collective-permute-start.30 = (bf16[4,4,64,384]{3,2,1,0:T(8,128)(2,1)S(1)}, bf16[4,4,64,384]{3,2,1,0:T(8,128)(2,1)S(1)}, u32[]{:S(2)}, u32[]{:S(2)}) collective-permute-start(bf16[4,4,64,384]{3,2,1,0:T(8,128)(2,1)S(1)} %copy-done.16), channel_id=1, source_target_pairs={{0,16},{16,0},{1,17},{17,1},{2,18},{18,2},{3,19},{19,3},{4,20},{20... | collective-permute-start | bytes 2359304 | tf_op jit(solution)/shard_map/ppermute | solution.py:379
  151.4 25.8 %collective-permute-start.29 = (bf16[128,3072]{1,0:T(8,128)(2,1)S(1)}, bf16[128,3072]{1,0:T(8,128)(2,1)}, u32[]{:S(2)}, u32[]{:S(2)}) collective-permute-start(bf16[128,3072]{1,0:T(8,128)(2,1)S(1)} %copy-done.58), channel_id=1, source_target_pairs={{0,2},{1,3},{2,0},{3,1},{4,6},{5,7},{6,4},{7,5},{8,10},{9,11},{10,... | collective-permute-start | bytes 2359304 | tf_op jit(solution)/shard_map/ppermute | solution.py:376
  153.2 26.4 %collective-permute-start.32 = (bf16[3,384,384]{2,1,0:T(8,128)(2,1)}, bf16[3,384,384]{2,1,0:T(8,128)(2,1)S(1)}, u32[]{:S(2)}, u32[]{:S(2)}) collective-permute-start(bf16[3,384,384]{2,1,0:T(8,128)(2,1)} %get-tuple-element.308), channel_id=1, source_target_pairs={{0,4},{12,8},{1,5},{13,9},{2,6},{14,10},{3,7},{15,11},{16,20},{28,... | collective-permute-start | bytes 2654216 | tf_op jit(solution)/shard_map/ppermute | solution.py:499
  156.6 25.0 %collective-permute-start.31 = (bf16[64,3072]{1,0:T(8,128)(2,1)}, bf16[64,3072]{1,0:T(8,128)(2,1)S(1)}, u32[]{:S(2)}, u32[]{:S(2)}) collective-permute-start(bf16[64,3072]{1,0:T(8,128)(2,1)} %add_convert_fusion.6), channel_id=1, source_target_pairs={{0,8},{4,12},{8,0},{12,4},{1,9},{5,13},{9,1},{13,5},{2,10},{6,14},... | collective-permute-start | bytes 1179656 | tf_op jit(solution)/shard_map/ppermute | solution.py:373
  181.6 21.1 %collective-permute-start.35 = (bf16[4,4,64,384]{3,2,1,0:T(8,128)(2,1)S(1)}, bf16[4,4,64,384]{3,2,1,0:T(8,128)(2,1)}, u32[]{:S(2)}, u32[]{:S(2)}) collective-permute-start(bf16[4,4,64,384]{3,2,1,0:T(8,128)(2,1)S(1)} %copy-done.14), channel_id=1, source_target_pairs={{0,16},{16,0},{1,17},{17,1},{2,18},{18,2},{3,19},{19,3},{4,20},{20... | collective-permute-start | bytes 2359304 | tf_op jit(solution)/shard_map/ppermute | solution.py:379
  183.1 28.0 %collective-permute-start.37 = (bf16[3,384,384]{2,1,0:T(8,128)(2,1)}, bf16[3,384,384]{2,1,0:T(8,128)(2,1)}, u32[]{:S(2)}, u32[]{:S(2)}) collective-permute-start(bf16[3,384,384]{2,1,0:T(8,128)(2,1)} %get-tuple-element.334), channel_id=1, source_target_pairs={{0,4},{12,8},{1,5},{13,9},{2,6},{14,10},{3,7},{15,11},{16,20},{28,... | collective-permute-start | bytes 2654216 | tf_op jit(solution)/shard_map/ppermute | solution.py:499
  190.7 20.4 %collective-permute-start.33 = (bf16[64,3072]{1,0:T(8,128)(2,1)}, bf16[64,3072]{1,0:T(8,128)(2,1)}, u32[]{:S(2)}, u32[]{:S(2)}) collective-permute-start(bf16[64,3072]{1,0:T(8,128)(2,1)} %get-tuple-element.311), channel_id=1, source_target_pairs={{0,2},{1,3},{2,0},{3,1},{4,6},{5,7},{6,4},{7,5},{8,10},{9,11},{10,... | collective-permute-start | bytes 1179656 | tf_op jit(solution)/shard_map/ppermute | solution.py:376
  191.6 23.0 %collective-permute-start.34 = (bf16[64,3072]{1,0:T(8,128)(2,1)}, bf16[64,3072]{1,0:T(8,128)(2,1)}, u32[]{:S(2)}, u32[]{:S(2)}) collective-permute-start(bf16[64,3072]{1,0:T(8,128)(2,1)} %get-tuple-element.312), channel_id=1, source_target_pairs={{0,12},{4,0},{8,4},{12,8},{1,13},{5,1},{9,5},{13,9},{2,14},{6,2},{... | collective-permute-start | bytes 1179656 | tf_op jit(solution)/shard_map/ppermute | solution.py:373
  214.6 24.5 %collective-permute-start.39 = (bf16[1536,384]{1,0:T(8,128)(2,1)S(1)}, bf16[1536,384]{1,0:T(8,128)(2,1)S(1)}, u32[]{:S(2)}, u32[]{:S(2)}) collective-permute-start(bf16[1536,384]{1,0:T(8,128)(2,1)S(1)} %copy-done.46), channel_id=1, source_target_pairs={{0,16},{16,0},{1,17},{17,1},{2,18},{18,2},{3,19},{19,3},{4,20},{20... | collective-permute-start | bytes 3538952 | tf_op jit(solution)/shard_map/ppermute | solution.py:379
  214.6 22.6 %collective-permute-start.42 = (bf16[3,384,384]{2,1,0:T(8,128)(2,1)}, bf16[3,384,384]{2,1,0:T(8,128)(2,1)S(1)}, u32[]{:S(2)}, u32[]{:S(2)}) collective-permute-start(bf16[3,384,384]{2,1,0:T(8,128)(2,1)} %get-tuple-element.351), channel_id=1, source_target_pairs={{0,4},{12,8},{1,5},{13,9},{2,6},{14,10},{3,7},{15,11},{16,20},{28,... | collective-permute-start | bytes 2654216 | tf_op jit(solution)/shard_map/ppermute | solution.py:499
  219.8 27.3 %collective-permute-start.38 = (bf16[64,3072]{1,0:T(8,128)(2,1)}, bf16[64,3072]{1,0:T(8,128)(2,1)S(1)}, u32[]{:S(2)}, u32[]{:S(2)}) collective-permute-start(bf16[64,3072]{1,0:T(8,128)(2,1)} %get-tuple-element.340), channel_id=1, source_target_pairs={{0,4},{4,8},{8,12},{12,0},{1,5},{5,9},{9,13},{13,1},{2,6},{6,10},{... | collective-permute-start | bytes 1179656 | tf_op jit(solution)/shard_map/ppermute | solution.py:373
  (86 other events, 824.9 us)
